TPU v7x, 256 devices: a whole 4x4x8 slice. The times are simulated.
256 devices in a mesh: dp: 2 (over core), expert: 128 (over z, y, x).
Axes of the slice: x: 4, y: 4, z: 8, core: 2. Of those that a mesh axis runs over, the one named last changes fastest.
Arguments:
- queries: bfloat16 [32768, 5120], P(('dp', 'expert')), may hold values from -6 to 6
- key_rows: bfloat16 [32768, 1024], P(('dp', 'expert')), may hold values from -6 to 6
- value_rows: bfloat16 [32768, 1024], P(('dp', 'expert')), may hold values from -6 to 6
- segments: int32 [256, 128], P(('dp', 'expert')), may hold values from 0 to 3, never falling along the last dimension, each value on 1 to 64 neighbouring positions
- swap_flags: int32 [128], P('expert'), may hold values 0 or 1
- expert_ids: int32 [32768, 1], P(('dp', 'expert')), may hold values from 0 to 15; in each aligned block of 128 rows (0 to 127, 128 to 255, ...) at most 10 rows name the same one
- norm_gain: bfloat16 [5120], replicated, may hold values from 0.25 to 1.75
- gate_weight: bfloat16 [5120, 32768], P(None, 'expert'), may hold values from -0.078125 to 0.078125
- up_weight: bfloat16 [5120, 32768], P(None, 'expert'), may hold values from -0.078125 to 0.078125
- down_weight: bfloat16 [32768, 5120], P('expert'), may hold values from -0.0625 to 0.0625
Outputs:
- layer_out: bfloat16 [32768, 5120], P(('dp', 'expert'))
Inputs may be any that keep to these rules, and one draw needn't show every extreme that they name: `expert_ids`: within each pack, no expert id is named by more than 10 tokens, and some ids are named by exactly 10 tokens in some packs. `segments`: within each pack the document number never falls.
All inputs are finite; a program needn't handle non-finite values. No bound on the sum of `swap_flags` on one device may be relied on, other than what follows from the above.
Results may differ from a plain program's by a relative error of at most 0.015.
Values may be sent and summed in bfloat16 or wider, within the bound.
No kernel may reach another device: no remote copies, remote signals or barrier semaphores. Data moves between devices by JAX's collectives and lax.ppermute only.
A program may use at most 192 MiB of HBM per device.

v0:
```python
import functools
import itertools

import jax
import jax.numpy as jnp
from jax import lax
from jax.experimental import pallas as pl
from jax.experimental.pallas import tpu as pltpu
from jax.sharding import PartitionSpec as P

HEADS = 40
KVH = 8
GROUP = HEADS // KVH
HD = 128
D = 5120
FF = 256
EXP_WIN = 4
CAP = 10
TOK = 128
ROWS = EXP_WIN * CAP
LINE = 4 * ROWS
HALF = D // 2
CUT = 1280
ALL = ("dp", "expert")
MIB = 1 << 20
HINT = 6_000_000_000


def device_pairs(target):
    pairs = []
    for dp, z, y, x in itertools.product(range(2), range(8), range(4), range(4)):
        to = target(dp, z, y, x)
        pairs.append((((dp * 8 + z) * 4 + y) * 4 + x, ((to[0] * 8 + to[1]) * 4 + to[2]) * 4 + to[3]))
    return pairs


def plane_shift(phase, step):
    def target(dp, z, y, x):
        if (dp == 0) == (phase == 1):
            return dp, z, y, (x + step) % 4
        return dp, z, (y + step) % 4, x

    return device_pairs(target)


def to_expert(kind):
    offset = {1: (2, -2), 2: (-3, 3), 3: (-1, 1)}[kind]
    return device_pairs(lambda dp, z, y, x: (dp, (z + offset[z % 2]) % 8, y, x))


def reverse(pairs):
    return [(b, a) for a, b in pairs]


def send(value, pairs):
    return lax.ppermute(value, ALL, pairs)


def attention_kernel(info, q0, q1, k0, k1, v0, v1, bias_ref, route_ref, gain_ref, attn_ref, pick_ref, b0, b1, b2, b3, acc):
    moved = info[0] > 0
    bias = bias_ref[...]
    acc[...] = jnp.zeros_like(acc)
    for h in range(KVH):
        cols = slice(h * HD, (h + 1) * HD)
        key = jnp.where(moved, k1[:, cols], k0[:, cols])
        value = jnp.where(moved, v1[:, cols], v0[:, cols])
        heads = [slice((h * GROUP + g) * HD, (h * GROUP + g + 1) * HD) for g in range(GROUP)]
        query = jnp.concatenate([jnp.where(moved, q1[:, c], q0[:, c]) for c in heads], axis=0)
        scores = lax.dot_general(query, key, (((1,), (1,)), ((), ())), preferred_element_type=jnp.float32)
        scores = scores.reshape(GROUP, TOK, TOK) * HD ** (-0.5) + bias[None]
        top = jnp.max(scores, axis=-1, keepdims=True)
        expo = jnp.exp(scores - top)
        probs = (expo * (1.0 / jnp.sum(expo, axis=-1, keepdims=True))).astype(jnp.bfloat16)
        mixed = jnp.dot(probs.reshape(GROUP * TOK, TOK), value, preferred_element_type=jnp.float32)
        mixed = mixed.astype(jnp.bfloat16)
        for g, c in enumerate(heads):
            part = mixed[g * TOK:(g + 1) * TOK]
            attn_ref[:, c] = part
            part_f = part.astype(jnp.float32)
            acc[...] += part_f * part_f
    scale = lax.rsqrt(jnp.sum(acc[...], axis=-1, keepdims=True) * (1.0 / D) + 1e-05)
    route = route_ref[...]
    kind = jnp.where(route < EXP_WIN, ((route - info[1]) * info[2]) & 3, 64)
    lanes = lax.broadcasted_iota(jnp.int32, (TOK, TOK), 1)
    earlier = (lax.broadcasted_iota(jnp.int32, (TOK, TOK), 0) < lanes).astype(jnp.bfloat16)
    chosen = (lax.broadcasted_iota(jnp.int32, (16, TOK), 0) == kind).astype(jnp.bfloat16)
    order = jnp.dot(chosen, earlier, preferred_element_type=jnp.float32)
    slot = jnp.sum(chosen.astype(jnp.float32) * order, axis=0, keepdims=True).astype(jnp.int32)
    place = kind * 16 + slot
    pick = (lax.broadcasted_iota(jnp.int32, (64, TOK), 0) == place).astype(jnp.bfloat16)
    pick_ref[...] = pick
    for n in range(8):
        c = slice(n * 640, (n + 1) * 640)
        normed = (attn_ref[:, c].astype(jnp.float32) * scale * gain_ref[:, c].astype(jnp.float32)).astype(jnp.bfloat16)
        rows = jnp.dot(pick, normed, preferred_element_type=jnp.float32).astype(jnp.bfloat16)
        for i, b in enumerate((b0, b1, b2, b3)):
            b[:, c] = rows[i * 16:i * 16 + CAP]


def attention(info, q0, q1, k0, k1, v0, v1, bias, route, gain):
    vmem = pl.BlockSpec(memory_space=pltpu.VMEM)
    rows = jax.ShapeDtypeStruct((CAP, D), jnp.bfloat16)
    return pl.pallas_call(
        attention_kernel,
        out_shape=(
            jax.ShapeDtypeStruct((TOK, D), jnp.bfloat16),
            jax.ShapeDtypeStruct((64, TOK), jnp.bfloat16),
            rows, rows, rows, rows,
        ),
        in_specs=[pl.BlockSpec(memory_space=pltpu.SMEM)] + [vmem] * 9,
        out_specs=(vmem,) * 6,
        scratch_shapes=[pltpu.VMEM((TOK, TOK), jnp.float32)],
        compiler_params=pltpu.CompilerParams(vmem_limit_bytes=32 * MIB),
        cost_estimate=pl.CostEstimate(flops=400_000_000, bytes_accessed=6_000_000, transcendentals=660_000),
        name="attention",
    )(info, q0, q1, k0, k1, v0, v1, bias, route, gain)


def silu_mul(gate, up):
    return (gate / (1.0 + jnp.exp(-gate)) * up).astype(jnp.bfloat16)


def hidden_kernel(count, parts, info, *refs):
    xs, srcs, h_ref = refs[:count], list(refs[count:-1]), refs[-1]
    near = info[3] * HALF
    far = HALF - near
    for i, part in enumerate(parts):
        if part == "own":
            g, u = (srcs.pop(0) for _ in range(2))
            pieces = [(g.at[pl.ds(k, CUT)], u.at[pl.ds(k, CUT)], k) for k in range(0, D, CUT)]
        else:
            ga1, ga2, gb1, gb2, ua, ub = (srcs.pop(0) for _ in range(6))
            head, tail = pl.ds(0, CUT), pl.ds(CUT, CUT)
            pieces = [
                (ga1, ua.at[head], near),
                (ga2, ua.at[tail], near + CUT),
                (gb1, ub.at[head], far),
                (gb2, ub.at[tail], far + CUT),
            ]
        gate = up = None
        for g, u, k in pieces:
            at = pl.ds(k if isinstance(k, int) else pl.multiple_of(k, HD), CUT)
            x = jnp.concatenate([r[:, at] for r in xs], axis=0)
            gate_term = jnp.dot(x, g[...], preferred_element_type=jnp.float32)
            up_term = jnp.dot(x, u[...], preferred_element_type=jnp.float32)
            gate, up = (gate_term, up_term) if gate is None else (gate + gate_term, up + up_term)
        h_ref[:, i * FF:(i + 1) * FF] = silu_mul(gate, up)


def hidden(info, xs, parts, weights, flops=0):
    count, n = len(xs), len(parts)
    vmem = pl.BlockSpec(memory_space=pltpu.VMEM)
    total = count * LINE
    return pl.pallas_call(
        functools.partial(hidden_kernel, count, parts),
        out_shape=jax.ShapeDtypeStruct((total, n * FF), jnp.bfloat16),
        in_specs=[pl.BlockSpec(memory_space=pltpu.SMEM)] + [vmem] * (count + len(weights)),
        out_specs=vmem,
        compiler_params=pltpu.CompilerParams(vmem_limit_bytes=24 * MIB),
        cost_estimate=pl.CostEstimate(flops=max(flops, 4 * total * D * n * FF), bytes_accessed=4 * D * n * FF + 2 * total * D, transcendentals=total * n * FF),
        name="hidden",
    )(info, *xs, *weights)


def down_kernel(info, h_line, h_near, h_other, h_last, own_w, wa, wb, *outs):
    near = pl.ds(pl.multiple_of(info[3] * (FF // 2), FF // 2), FF // 2)
    far = pl.ds(pl.multiple_of((1 - info[3]) * (FF // 2), FF // 2), FF // 2)
    own = jnp.concatenate([h_line[...], h_near[...], h_last[:, :FF]], axis=0)
    last = h_last.at[:, pl.ds(FF, FF)]
    other = [jnp.concatenate([h_other[:, part], last[:, part]], axis=0) for part in (near, far)]
    h = jnp.concatenate([own, *other], axis=1)
    tile = 512
    for n in range(D // tile):
        cols = pl.ds(n * tile, tile)
        w = jnp.concatenate([own_w[:, cols], wa[:, cols], wb[:, cols]], axis=0)
        y = jnp.dot(h, w, preferred_element_type=jnp.float32).astype(jnp.bfloat16)
        half, at = divmod(n * tile, HALF)
        for i in range(4):
            outs[4 * half + i][:, at:at + tile] = y[i * LINE:(i + 1) * LINE]


def down(info, hs, own_w, wa, wb):
    vmem = pl.BlockSpec(memory_space=pltpu.VMEM)
    total = 4 * LINE
    outs = pl.pallas_call(
        down_kernel,
        out_shape=tuple(jax.ShapeDtypeStruct((LINE, HALF), jnp.bfloat16) for _ in range(8)),
        in_specs=[pl.BlockSpec(memory_space=pltpu.SMEM)] + [vmem] * (len(hs) + 3),
        out_specs=(vmem,) * 8,
        compiler_params=pltpu.CompilerParams(vmem_limit_bytes=24 * MIB),
        cost_estimate=pl.CostEstimate(flops=2 * total * 2 * FF * D, bytes_accessed=4 * FF * D + 2 * total * D, transcendentals=0),
        name="down",
    )(info, *hs, own_w, wa, wb)
    return outs[:4], outs[4:]


def hold(value, flops):
    hbm = pl.BlockSpec(memory_space=pl.ANY)
    return pl.pallas_call(
        lambda value_ref, out_ref: None,
        out_shape=jax.ShapeDtypeStruct(value.shape, value.dtype),
        in_specs=[hbm],
        out_specs=hbm,
        input_output_aliases={0: 0},
        cost_estimate=pl.CostEstimate(flops=flops, bytes_accessed=0, transcendentals=0),
        name="hold",
    )(value)


def line_sums_kernel(*refs):
    parts, outs = refs[:6], refs[6:]
    tile = 512
    for n in range(D // tile):
        half, at = divmod(n * tile, HALF)
        a, b, c = (r[:, at:at + tile].astype(jnp.float32) for r in parts[3 * half:3 * half + 3])
        total = a + b + c
        for i, o in enumerate(outs):
            o[:, n * tile:(n + 1) * tile] = total[i * ROWS:(i + 1) * ROWS].astype(jnp.bfloat16)


def line_sums(halves):
    vmem = pl.BlockSpec(memory_space=pltpu.VMEM)
    return pl.pallas_call(
        line_sums_kernel,
        out_shape=tuple(jax.ShapeDtypeStruct((ROWS, D), jnp.bfloat16) for _ in range(4)),
        in_specs=[vmem] * 6,
        out_specs=(vmem,) * 4,
        compiler_params=pltpu.CompilerParams(vmem_limit_bytes=24 * MIB),
        cost_estimate=pl.CostEstimate(flops=2 * LINE * D, bytes_accessed=8 * LINE * D, transcendentals=0),
        name="line_sums",
    )(*halves[0], *halves[1])


def stack_kernel(*refs):
    at = 0
    for r in refs[:-1]:
        refs[-1][at:at + r.shape[0], :] = r[...]
        at += r.shape[0]


def stack(parts):
    vmem = pl.BlockSpec(memory_space=pltpu.VMEM)
    rows = sum(p.shape[0] for p in parts)
    return pl.pallas_call(
        stack_kernel,
        out_shape=jax.ShapeDtypeStruct((rows, D), jnp.bfloat16),
        in_specs=[vmem] * len(parts),
        out_specs=vmem,
        compiler_params=pltpu.CompilerParams(vmem_limit_bytes=16 * MIB),
        cost_estimate=pl.CostEstimate(flops=0, bytes_accessed=4 * rows * D, transcendentals=0),
        name="stack",
    )(*parts)


def combine_kernel(pick_ref, attn_ref, r0, r1, r2, r3, out_ref):
    for n in range(8):
        c = slice(n * 640, (n + 1) * 640)
        total = attn_ref[:, c].astype(jnp.float32)
        for i, r in enumerate((r0, r1, r2, r3)):
            total += lax.dot_general(
                pick_ref[i * 16:i * 16 + CAP], r[:, c], (((0,), (0,)), ((), ())), preferred_element_type=jnp.float32
            )
        out_ref[:, c] = total.astype(jnp.bfloat16)


def combine(pick, attn, rows):
    vmem = pl.BlockSpec(memory_space=pltpu.VMEM)
    return pl.pallas_call(
        combine_kernel,
        out_shape=jax.ShapeDtypeStruct((TOK, D), jnp.bfloat16),
        in_specs=[vmem] * 6,
        out_specs=vmem,
        compiler_params=pltpu.CompilerParams(vmem_limit_bytes=32 * MIB),
        cost_estimate=pl.CostEstimate(flops=60_000_000, bytes_accessed=3_000_000, transcendentals=0),
        name="combine",
    )(pick, attn, *rows)


def add_up(parts):
    total = parts[0].astype(jnp.float32)
    for p in parts[1:]:
        total = total + p.astype(jnp.float32)
    return total.astype(jnp.bfloat16)


def after(value, *others):
    return lax.optimization_barrier((value, others))[0]


def per_device(queries, key_rows, value_rows, segments, swap_flags, expert_ids, norm_gain, gate_weight, up_weight, down_weight):
    dp = lax.axis_index("dp")
    z = lax.axis_index("expert") // 16
    info = jnp.stack([swap_flags[0], z // 2, 1 - 2 * (z % 2), dp]).astype(jnp.int32)

    across = device_pairs(lambda d, zz, y, x: (d, zz ^ 1, y, x))
    beside = device_pairs(lambda d, zz, y, x: (1 - d, zz, y, x))
    g_first = send(lax.dynamic_slice_in_dim(gate_weight, dp * HALF, CUT, 0), across)

    seg_local = segments.astype(jnp.bfloat16)
    q1, k1, v1, s1 = (send(a, beside) for a in (queries, key_rows, value_rows, seg_local))
    seg = jnp.where(swap_flags[0] > 0, s1, seg_local)[0].astype(jnp.float32)
    position = jnp.arange(TOK)
    allowed = (seg[:, None] == seg[None, :]) & (position[:, None] >= position[None, :])
    bias = jnp.where(allowed, jnp.float32(0), jnp.float32(-1e30))
    attn, pick, *rows = attention(
        info, queries, q1, key_rows, k1, value_rows, v1, bias, expert_ids.reshape(1, TOK), norm_gain.reshape(1, D)
    )

    moved = [send(rows[k], to_expert(k)) for k in (1, 2, 3)]
    mine = jnp.concatenate([rows[0]] + after(moved, g_first), axis=0)
    g_rest = lax.dynamic_slice_in_dim(gate_weight, dp * HALF + CUT, HALF - CUT, 0)
    g_rest = send(after(g_rest, moved), across)
    line = stack([mine] + [send(mine, plane_shift(1, s)) for s in (1, 3, 2)])
    line_out = after(line, g_rest)
    c1, c3, c2 = (send(line_out, plane_shift(2, s)) for s in (1, 3, 2))
    u_half = lax.dynamic_slice_in_dim(up_weight, dp * HALF, HALF, 0)
    u_half = send(after(u_half, line_out), across)

    own_gu = (gate_weight, up_weight)
    h_line = hidden(info, [line], ("own",), own_gu)
    g_first, g_rest, u_half = after((g_first, g_rest, u_half), h_line)
    other_gu = (g_first, g_rest, send(g_first, beside), send(g_rest, beside), u_half, send(u_half, beside))
    h_near = hidden(info, [c1, c3], ("own",), own_gu, HINT)
    wa = send(after(lax.dynamic_slice_in_dim(down_weight, dp * (FF // 2), FF // 2, 0), line_out), across)
    h_other = hidden(info, [after(line, h_near), c1, c3], ("other",), other_gu)
    h_last = hidden(info, [after(c2, h_other)], ("own", "other"), own_gu + other_gu)
    hs = (h_line, h_near, h_other, h_last)

    wa = after(wa, h_last)
    outs0, outs1 = down(info, hs, down_weight, wa, send(wa, beside))

    relay0 = send(outs0[3], plane_shift(2, 1))
    relay1 = send(outs1[3], plane_shift(2, 3))
    plain0 = send(outs0[1], plane_shift(2, 3))
    plain1 = send(outs1[2], plane_shift(2, 1))
    both0 = send(add_up([outs0[2], relay0]), plane_shift(2, 1))
    both1 = send(add_up([outs1[1], relay1]), plane_shift(2, 3))
    halves = ((outs0[0], plain0, both0), (outs1[0], plain1, both1))
    back = line_sums(halves)
    mine_sum = add_up([back[0]] + [send(b, plane_shift(1, s)) for b, s in zip(back[1:], (3, 1, 2))])
    pieces = [mine_sum[k * CAP:(k + 1) * CAP] for k in range(4)]
    returned = [pieces[0]] + [send(pieces[k], reverse(to_expert(k))) for k in (1, 2, 3)]
    return combine(pick, attn, returned)


def solution(mesh):
    in_specs = (
        P(("dp", "expert"), None),
        P(("dp", "expert"), None),
        P(("dp", "expert"), None),
        P(("dp", "expert"), None),
        P("expert"),
        P(("dp", "expert"), None),
        P(),
        P(None, "expert"),
        P(None, "expert"),
        P("expert", None),
    )
    out_specs = P(("dp", "expert"), None)
    return jax.shard_map(
        per_device, mesh=mesh, in_specs=in_specs, out_specs=out_specs, check_vma=False
    )
```

profile of v0, /device:TPU:6, one launch (start us, length us, event | category | flops | bytes accessed | tf_op | source)
XLA Modules:
  0.0 186.7 jit_solution(6916430480849441273)
XLA Ops:
  9.3 3.8 %attention.1 = (bf16[128,5120]{1,0:T(8,128)(2,1)S(1)}, bf16[64,128]{1,0:T(8,128)(2,1)S(1)}, bf16[10,5120]{1,0:T(8,128)(2,1)S(1)}, bf16[10,5120]{1,0:T(8,128)(2,1...) custom-call(s32[4]{0:T(128)S(1)} %pad_add_fusion.info, bf16[128,5120]{1,0:T(8,128)(2,1)S(1)} %copy-done.4, ...), custom_call_target="tpu_custom_call" | custom-call | flops 400000000 | bytes 6000000 | tf_op jit(solution)/shard_map/attention/pallas_call | solution.py:103
  13.2 3.3 %collective-permute-start.4 = (bf16[10,5120]{1,0:T(8,128)(2,1)S(1)}, bf16[10,5120]{1,0:T(8,128)(2,1)S(1)}, u32[]{:S(2)}, u32[]{:S(2)}) collective-permute-start(bf16[10,5120]{1,0:T(8,128)(2,1)S(1)} %get-tuple-element.39), channel_id=1, source_target_pairs={{0,32},{1,33},{2,34},{3,35},{4,36},{5,37},{6,38},{7,39},{8,40},{9,... | collective-permute-start | bytes 307208 | tf_op jit(solution)/shard_map/ppermute | solution.py:56
  16.5 3.3 %collective-permute-start.5 = (bf16[10,5120]{1,0:T(8,128)(2,1)S(1)}, bf16[10,5120]{1,0:T(8,128)(2,1)S(1)}, u32[]{:S(2)}, u32[]{:S(2)}) collective-permute-start(bf16[10,5120]{1,0:T(8,128)(2,1)S(1)} %get-tuple-element.40), channel_id=1, source_target_pairs={{0,80},{1,81},{2,82},{3,83},{4,84},{5,85},{6,86},{7,87},{8,88},{9,... | collective-permute-start | bytes 307208 | tf_op jit(solution)/shard_map/ppermute | solution.py:56
  19.8 3.6 %collective-permute-start.6 = (bf16[10,5120]{1,0:T(8,128)(2,1)S(1)}, bf16[10,5120]{1,0:T(8,128)(2,1)S(1)}, u32[]{:S(2)}, u32[]{:S(2)}) collective-permute-start(bf16[10,5120]{1,0:T(8,128)(2,1)S(1)} %get-tuple-element.41), channel_id=1, source_target_pairs={{0,112},{1,113},{2,114},{3,115},{4,116},{5,117},{6,118},{7,119},{8... | collective-permute-start | bytes 307208 | tf_op jit(solution)/shard_map/ppermute | solution.py:56
  23.4 10.8 %collective-permute-done.4 = bf16[10,5120]{1,0:T(8,128)(2,1)S(1)} collective-permute-done((bf16[10,5120]{1,0:T(8,128)(2,1)S(1)}, bf16[10,5120]{1,0:T(8,128)(2,1)S(1)}, u32[]{:S(2)}, u32[]{:S(2)}) %collective-permute-start.4) | collective-permute-done | bytes 102432 | tf_op jit(solution)/shard_map/ppermute | solution.py:56
  41.6 4.0 %collective-permute-done.8.refs_1_ = bf16[40,5120]{1,0:T(8,128)(2,1)S(1)} collective-permute-done((bf16[40,5120]{1,0:T(8,128)(2,1)S(1)}, bf16[40,5120]{1,0:T(8,128)(2,1)S(1)}, u32[]{:S(2)}, u32[]{:S(2)}) %collective-permute-start.8) | collective-permute-done | bytes 409632 | tf_op jit(solution)/shard_map/ppermute | solution.py:56
  45.6 6.1 %collective-permute-done.9.refs_2_ = bf16[40,5120]{1,0:T(8,128)(2,1)S(1)} collective-permute-done((bf16[40,5120]{1,0:T(8,128)(2,1)S(1)}, bf16[40,5120]{1,0:T(8,128)(2,1)S(1)}, u32[]{:S(2)}, u32[]{:S(2)}) %collective-permute-start.9) | collective-permute-done | bytes 409632 | tf_op jit(solution)/shard_map/ppermute | solution.py:56
  58.8 2.6 %hidden.4.h_line = bf16[160,256]{1,0:T(8,128)(2,1)S(1)} custom-call(s32[4]{0:T(128)S(1)} %copy-done.11, bf16[160,5120]{1,0:T(8,128)(2,1)} %stack.17.refs_0_, bf16[5120,256]{1,0:T(8,128)(2,1)S(1)} %copy-done, bf16[5120,256]{1,0:T(8,128)(2,1)S(1)} %copy-done.2), custom_call_target="tpu_custom_call" | custom-call | flops 838860800 | bytes 6881280 | tf_op jit(solution)/shard_map/hidden/pallas_call | solution.py:154
  63.5 18.9 %collective-permute-done.14.refs_7_ = bf16[2560,256]{1,0:T(8,128)(2,1)} collective-permute-done((bf16[2560,256]{1,0:T(8,128)(2,1)}, bf16[2560,256]{1,0:T(8,128)(2,1)}, u32[]{:S(2)}, u32[]{:S(2)}) %collective-permute-start.14) | collective-permute-done | bytes 1310752 | tf_op jit(solution)/shard_map/ppermute | solution.py:56
  83.9 3.9 %hidden.5.h_near = bf16[320,256]{1,0:T(8,128)(2,1)S(1)} custom-call(s32[4]{0:T(128)S(1)} %copy-done.11, bf16[160,5120]{1,0:T(8,128)(2,1)} %collective-permute-done.12.refs_0_.refs_1_, bf16[160,5120]{1,0:T(8,128)(2,1)} %collective-permute-done.13.refs_1_.refs_2_, bf16[5120,256]{1,0:T(8,128)(2,1)S(1)} %copy-done, bf16[5120,256]{1,0:T(8,128)(2,1)S(1)} %copy-done.2), custom_call_target="tpu_custom_call" | custom-call | flops 6000000000 | bytes 8519680 | tf_op jit(solution)/shard_map/hidden/pallas_call | solution.py:154
  87.8 5.9 %hidden.6.h_other = bf16[480,256]{1,0:T(8,128)(2,1)S(1)} custom-call(s32[4]{0:T(128)S(1)} %copy-done.11, bf16[160,5120]{1,0:T(8,128)(2,1)} %stack.17.refs_0_, bf16[160,5120]{1,0:T(8,128)(2,1)} %collective-permute-done.12.refs_0_.refs_1_, bf16[160,5120]{1,0:T(8,128)(2,1)} %collective-permute-done.13.refs_1_.refs_2_, ...), custom_call_target="tpu_custom_call" | custom-call | flops 2516582400 | bytes 10158080 | tf_op jit(solution)/shard_map/hidden/pallas_call | solution.py:154
  95.2 3.5 %hidden.7.h_last = bf16[160,512]{1,0:T(8,128)(2,1)S(1)} custom-call(s32[4]{0:T(128)S(1)} %copy-done.11, bf16[160,5120]{1,0:T(8,128)(2,1)S(1)} %collective-permute-done.18.refs_0_, bf16[5120,256]{1,0:T(8,128)(2,1)S(1)} %copy-done, bf16[5120,256]{1,0:T(8,128)(2,1)S(1)} %copy-done.3, bf16[1280,256]{1,0:T(8,128)(2,1)S(1)} %collective-permute-done.7.refs_3_, ...), custom_call_target="tpu_custom_call" | custom-call | flops 1677721600 | bytes 12124160 | tf_op jit(solution)/shard_map/hidden/pallas_call | solution.py:154
  98.6 15.2 %collective-permute-done.19.wa = bf16[128,5120]{1,0:T(8,128)(2,1)S(1)} collective-permute-done((bf16[128,5120]{1,0:T(8,128)(2,1)S(1)}, bf16[128,5120]{1,0:T(8,128)(2,1)S(1)}, u32[]{:S(2)}, u32[]{:S(2)}) %collective-permute-start.19) | collective-permute-done | bytes 1310752 | tf_op jit(solution)/shard_map/ppermute | solution.py:56
  113.8 3.0 %collective-permute-done.20.wb = bf16[128,5120]{1,0:T(8,128)(2,1)S(1)} collective-permute-done((bf16[128,5120]{1,0:T(8,128)(2,1)S(1)}, bf16[128,5120]{1,0:T(8,128)(2,1)S(1)}, u32[]{:S(2)}, u32[]{:S(2)}) %collective-permute-start.20) | collective-permute-done | bytes 1310752 | tf_op jit(solution)/shard_map/ppermute | solution.py:56
  116.8 4.1 %down.1 = (bf16[160,2560]{1,0:T(8,128)(2,1)S(1)}, bf16[160,2560]{1,0:T(8,128)(2,1)S(1)}, bf16[160,2560]{1,0:T(8,128)(2,1)S(1)}, bf16[160,2560]{1,0:T(8,128)(2,1)...) custom-call(s32[4]{0:T(128)S(1)} %copy-done.11, ...), custom_call_target="tpu_custom_call" | custom-call | flops 3355443200 | bytes 11796480 | tf_op jit(solution)/shard_map/down/pallas_call | solution.py:185
  126.5 8.3 %collective-permute-done.22 = bf16[160,2560]{1,0:T(8,128)(2,1)S(1)} collective-permute-done((bf16[160,2560]{1,0:T(8,128)(2,1)S(1)}, bf16[160,2560]{1,0:T(8,128)(2,1)S(1)}, u32[]{:S(2)}, u32[]{:S(2)}) %collective-permute-start.22) | collective-permute-done | bytes 819232 | tf_op jit(solution)/shard_map/ppermute | solution.py:56
  135.3 3.3 %collective-permute-start.26 = (bf16[160,2560]{1,0:T(8,128)(2,1)S(1)}, bf16[160,2560]{1,0:T(8,128)(2,1)S(1)}, u32[]{:S(2)}, u32[]{:S(2)}) collective-permute-start(bf16[160,2560]{1,0:T(8,128)(2,1)S(1)} %add_convert_fusion), channel_id=1, source_target_pairs={{0,12},{1,13},{2,14},{3,15},{4,0},{5,1},{6,2},{7,3},{8,4},{9,5},{1... | collective-permute-start | bytes 2457608 | tf_op jit(solution)/shard_map/ppermute | solution.py:56
  138.6 4.9 %collective-permute-done.21.refs_1_ = bf16[160,2560]{1,0:T(8,128)(2,1)S(1)} collective-permute-done((bf16[160,2560]{1,0:T(8,128)(2,1)S(1)}, bf16[160,2560]{1,0:T(8,128)(2,1)S(1)}, u32[]{:S(2)}, u32[]{:S(2)}) %collective-permute-start.21) | collective-permute-done | bytes 819232 | tf_op jit(solution)/shard_map/ppermute | solution.py:56
  143.6 8.8 %collective-permute-done.23.refs_2_ = bf16[160,2560]{1,0:T(8,128)(2,1)S(1)} collective-permute-done((bf16[160,2560]{1,0:T(8,128)(2,1)S(1)}, bf16[160,2560]{1,0:T(8,128)(2,1)S(1)}, u32[]{:S(2)}, u32[]{:S(2)}) %collective-permute-start.23) | collective-permute-done | bytes 819232 | tf_op jit(solution)/shard_map/ppermute | solution.py:56
  157.2 5.4 %collective-permute-done.29 = bf16[40,5120]{1,0:T(8,128)(2,1)S(1)} collective-permute-done((bf16[40,5120]{1,0:T(8,128)(2,1)S(1)}, bf16[40,5120]{1,0:T(8,128)(2,1)S(1)}, u32[]{:S(2)}, u32[]{:S(2)}) %collective-permute-start.29) | collective-permute-done | bytes 409632 | tf_op jit(solution)/shard_map/ppermute | solution.py:56
  169.8 3.1 %collective-permute-start.32 = (bf16[10,5120]{1,0:T(8,128)(2,1)S(1)}, bf16[10,5120]{1,0:T(8,128)(2,1)S(1)}, u32[]{:S(2)}, u32[]{:S(2)}) collective-permute-start(bf16[10,5120]{1,0:T(8,128)(2,1)S(1)} %get-tuple-element.69), channel_id=1, source_target_pairs={{112,0},{113,1},{114,2},{115,3},{116,4},{117,5},{118,6},{119,7},{1... | collective-permute-start | bytes 307208 | tf_op jit(solution)/shard_map/ppermute | solution.py:56
  172.9 2.9 %collective-permute-done.30.r1 = bf16[10,5120]{1,0:T(8,128)(2,1)S(1)} collective-permute-done((bf16[10,5120]{1,0:T(8,128)(2,1)S(1)}, bf16[10,5120]{1,0:T(8,128)(2,1)S(1)}, u32[]{:S(2)}, u32[]{:S(2)}) %collective-permute-start.30) | collective-permute-done | bytes 102432 | tf_op jit(solution)/shard_map/ppermute | solution.py:56
  175.8 4.1 %collective-permute-done.31.r2 = bf16[10,5120]{1,0:T(8,128)(2,1)S(1)} collective-permute-done((bf16[10,5120]{1,0:T(8,128)(2,1)S(1)}, bf16[10,5120]{1,0:T(8,128)(2,1)S(1)}, u32[]{:S(2)}, u32[]{:S(2)}) %collective-permute-start.31) | collective-permute-done | bytes 102432 | tf_op jit(solution)/shard_map/ppermute | solution.py:56
  179.8 4.3 %collective-permute-done.32.r3 = bf16[10,5120]{1,0:T(8,128)(2,1)S(1)} collective-permute-done((bf16[10,5120]{1,0:T(8,128)(2,1)S(1)}, bf16[10,5120]{1,0:T(8,128)(2,1)S(1)}, u32[]{:S(2)}, u32[]{:S(2)}) %collective-permute-start.32) | collective-permute-done | bytes 102432 | tf_op jit(solution)/shard_map/ppermute | solution.py:56
  (96 shorter events, 48.8 us)
Async XLA Ops:
  4.8 18.6 %collective-permute-start.7 = (bf16[1280,256]{1,0:T(8,128)(2,1)}, bf16[1280,256]{1,0:T(8,128)(2,1)S(1)}, u32[]{:S(2)}, u32[]{:S(2)}) collective-permute-start(bf16[1280,256]{1,0:T(8,128)(2,1)} %get-tuple-element.68), channel_id=1, source_target_pairs={{0,16},{1,17},{2,18},{3,19},{4,20},{5,21},{6,22},{7,23},{8,24},{9,... | collective-permute-start | bytes 1966088 | tf_op jit(solution)/shard_map/ppermute | solution.py:56
  13.2 21.0 %collective-permute-start.4 = (bf16[10,5120]{1,0:T(8,128)(2,1)S(1)}, bf16[10,5120]{1,0:T(8,128)(2,1)S(1)}, u32[]{:S(2)}, u32[]{:S(2)}) collective-permute-start(bf16[10,5120]{1,0:T(8,128)(2,1)S(1)} %get-tuple-element.39), channel_id=1, source_target_pairs={{0,32},{1,33},{2,34},{3,35},{4,36},{5,37},{6,38},{7,39},{8,40},{9,... | collective-permute-start | bytes 307208 | tf_op jit(solution)/shard_map/ppermute | solution.py:56
  16.5 17.7 %collective-permute-start.5 = (bf16[10,5120]{1,0:T(8,128)(2,1)S(1)}, bf16[10,5120]{1,0:T(8,128)(2,1)S(1)}, u32[]{:S(2)}, u32[]{:S(2)}) collective-permute-start(bf16[10,5120]{1,0:T(8,128)(2,1)S(1)} %get-tuple-element.40), channel_id=1, source_target_pairs={{0,80},{1,81},{2,82},{3,83},{4,84},{5,85},{6,86},{7,87},{8,88},{9,... | collective-permute-start | bytes 307208 | tf_op jit(solution)/shard_map/ppermute | solution.py:56
  19.8 16.0 %collective-permute-start.6 = (bf16[10,5120]{1,0:T(8,128)(2,1)S(1)}, bf16[10,5120]{1,0:T(8,128)(2,1)S(1)}, u32[]{:S(2)}, u32[]{:S(2)}) collective-permute-start(bf16[10,5120]{1,0:T(8,128)(2,1)S(1)} %get-tuple-element.41), channel_id=1, source_target_pairs={{0,112},{1,113},{2,114},{3,115},{4,116},{5,117},{6,118},{7,119},{8... | collective-permute-start | bytes 307208 | tf_op jit(solution)/shard_map/ppermute | solution.py:56
  35.8 17.2 %collective-permute-start.11 = (bf16[1280,256]{1,0:T(8,128)(2,1)S(1)}, bf16[1280,256]{1,0:T(8,128)(2,1)}, u32[]{:S(2)}, u32[]{:S(2)}) collective-permute-start(bf16[1280,256]{1,0:T(8,128)(2,1)S(1)} %copy-done.13), channel_id=1, source_target_pairs={{0,16},{1,17},{2,18},{3,19},{4,20},{5,21},{6,22},{7,23},{8,24},{9,... | collective-permute-start | bytes 1966088 | tf_op jit(solution)/shard_map/ppermute | solution.py:56
  38.2 13.6 %collective-permute-start.9 = (bf16[40,5120]{1,0:T(8,128)(2,1)S(1)}, bf16[40,5120]{1,0:T(8,128)(2,1)S(1)}, u32[]{:S(2)}, u32[]{:S(2)}) collective-permute-start(bf16[40,5120]{1,0:T(8,128)(2,1)S(1)} %pad_maximum_fusion.refs_0_), channel_id=1, source_target_pairs={{0,3},{1,0},{2,1},{3,2},{4,7},{5,4},{6,5},{7,6},{8,11},{9,8},{10,9... | collective-permute-start | bytes 1228808 | tf_op jit(solution)/shard_map/ppermute | solution.py:56
  39.7 12.0 %collective-permute-start.10 = (bf16[40,5120]{1,0:T(8,128)(2,1)S(1)}, bf16[40,5120]{1,0:T(8,128)(2,1)S(1)}, u32[]{:S(2)}, u32[]{:S(2)}) collective-permute-start(bf16[40,5120]{1,0:T(8,128)(2,1)S(1)} %pad_maximum_fusion.refs_0_), channel_id=1, source_target_pairs={{0,2},{1,3},{2,0},{3,1},{4,6},{5,7},{6,4},{7,5},{8,10},{9,11},{10,... | collective-permute-start | bytes 1228808 | tf_op jit(solution)/shard_map/ppermute | solution.py:56
  53.0 29.4 %collective-permute-start.14 = (bf16[2560,256]{1,0:T(8,128)(2,1)}, bf16[2560,256]{1,0:T(8,128)(2,1)}, u32[]{:S(2)}, u32[]{:S(2)}) collective-permute-start(bf16[2560,256]{1,0:T(8,128)(2,1)} %constant_dynamic-slice_fusion.1), channel_id=1, source_target_pairs={{0,16},{1,17},{2,18},{3,19},{4,20},{5,21},{6,22},{7,23},{8,24},{9,... | collective-permute-start | bytes 3932168 | tf_op jit(solution)/shard_map/ppermute | solution.py:56
  53.8 29.6 %collective-permute-start.12 = (bf16[160,5120]{1,0:T(8,128)(2,1)}, bf16[160,5120]{1,0:T(8,128)(2,1)}, u32[]{:S(2)}, u32[]{:S(2)}) collective-permute-start(bf16[160,5120]{1,0:T(8,128)(2,1)} %stack.17.refs_0_), channel_id=1, source_target_pairs={{0,4},{1,5},{2,6},{3,7},{4,8},{5,9},{6,10},{7,11},{8,12},{9,13},{1... | collective-permute-start | bytes 4915208 | tf_op jit(solution)/shard_map/ppermute | solution.py:56
  55.7 28.0 %collective-permute-start.13 = (bf16[160,5120]{1,0:T(8,128)(2,1)}, bf16[160,5120]{1,0:T(8,128)(2,1)}, u32[]{:S(2)}, u32[]{:S(2)}) collective-permute-start(bf16[160,5120]{1,0:T(8,128)(2,1)} %stack.17.refs_0_), channel_id=1, source_target_pairs={{0,12},{1,13},{2,14},{3,15},{4,0},{5,1},{6,2},{7,3},{8,4},{9,5},{1... | collective-permute-start | bytes 4915208 | tf_op jit(solution)/shard_map/ppermute | solution.py:56
  61.5 33.7 %collective-permute-start.18 = (bf16[160,5120]{1,0:T(8,128)(2,1)}, bf16[160,5120]{1,0:T(8,128)(2,1)S(1)}, u32[]{:S(2)}, u32[]{:S(2)}) collective-permute-start(bf16[160,5120]{1,0:T(8,128)(2,1)} %stack.17.refs_0_), channel_id=1, source_target_pairs={{0,8},{1,9},{2,10},{3,11},{4,12},{5,13},{6,14},{7,15},{8,0},{9,1},... | collective-permute-start | bytes 4915208 | tf_op jit(solution)/shard_map/ppermute | solution.py:56
  82.5 31.3 %collective-permute-start.19 = (bf16[128,5120]{1,0:T(8,128)(2,1)S(1)}, bf16[128,5120]{1,0:T(8,128)(2,1)S(1)}, u32[]{:S(2)}, u32[]{:S(2)}) collective-permute-start(bf16[128,5120]{1,0:T(8,128)(2,1)S(1)} %constant_dynamic-slice_fusion), channel_id=1, source_target_pairs={{0,16},{1,17},{2,18},{3,19},{4,20},{5,21},{6,22},{7,23},{8,24},{9,... | collective-permute-start | bytes 3932168 | tf_op jit(solution)/shard_map/ppermute | solution.py:56
  120.9 13.8 %collective-permute-start.22 = (bf16[160,2560]{1,0:T(8,128)(2,1)S(1)}, bf16[160,2560]{1,0:T(8,128)(2,1)S(1)}, u32[]{:S(2)}, u32[]{:S(2)}) collective-permute-start(bf16[160,2560]{1,0:T(8,128)(2,1)S(1)} %get-tuple-element.58), channel_id=1, source_target_pairs={{0,4},{1,5},{2,6},{3,7},{4,8},{5,9},{6,10},{7,11},{8,12},{9,13},{1... | collective-permute-start | bytes 2457608 | tf_op jit(solution)/shard_map/ppermute | solution.py:56
  122.4 12.7 %collective-permute-start.25 = (bf16[160,2560]{1,0:T(8,128)(2,1)S(1)}, bf16[160,2560]{1,0:T(8,128)(2,1)S(1)}, u32[]{:S(2)}, u32[]{:S(2)}) collective-permute-start(bf16[160,2560]{1,0:T(8,128)(2,1)S(1)} %get-tuple-element.62), channel_id=1, source_target_pairs={{0,12},{1,13},{2,14},{3,15},{4,0},{5,1},{6,2},{7,3},{8,4},{9,5},{1... | collective-permute-start | bytes 2457608 | tf_op jit(solution)/shard_map/ppermute | solution.py:56
  124.5 19.0 %collective-permute-start.21 = (bf16[160,2560]{1,0:T(8,128)(2,1)S(1)}, bf16[160,2560]{1,0:T(8,128)(2,1)S(1)}, u32[]{:S(2)}, u32[]{:S(2)}) collective-permute-start(bf16[160,2560]{1,0:T(8,128)(2,1)S(1)} %get-tuple-element.56), channel_id=1, source_target_pairs={{0,12},{1,13},{2,14},{3,15},{4,0},{5,1},{6,2},{7,3},{8,4},{9,5},{1... | collective-permute-start | bytes 2457608 | tf_op jit(solution)/shard_map/ppermute | solution.py:56
  125.1 18.4 %collective-permute-start.24 = (bf16[160,2560]{1,0:T(8,128)(2,1)S(1)}, bf16[160,2560]{1,0:T(8,128)(2,1)S(1)}, u32[]{:S(2)}, u32[]{:S(2)}) collective-permute-start(bf16[160,2560]{1,0:T(8,128)(2,1)S(1)} %get-tuple-element.60), channel_id=1, source_target_pairs={{0,4},{1,5},{2,6},{3,7},{4,8},{5,9},{6,10},{7,11},{8,12},{9,13},{1... | collective-permute-start | bytes 2457608 | tf_op jit(solution)/shard_map/ppermute | solution.py:56
  135.0 17.4 %collective-permute-start.23 = (bf16[160,2560]{1,0:T(8,128)(2,1)S(1)}, bf16[160,2560]{1,0:T(8,128)(2,1)S(1)}, u32[]{:S(2)}, u32[]{:S(2)}) collective-permute-start(bf16[160,2560]{1,0:T(8,128)(2,1)S(1)} %add_convert_fusion.1), channel_id=1, source_target_pairs={{0,4},{1,5},{2,6},{3,7},{4,8},{5,9},{6,10},{7,11},{8,12},{9,13},{1... | collective-permute-start | bytes 2457608 | tf_op jit(solution)/shard_map/ppermute | solution.py:56
  135.3 17.1 %collective-permute-start.26 = (bf16[160,2560]{1,0:T(8,128)(2,1)S(1)}, bf16[160,2560]{1,0:T(8,128)(2,1)S(1)}, u32[]{:S(2)}, u32[]{:S(2)}) collective-permute-start(bf16[160,2560]{1,0:T(8,128)(2,1)S(1)} %add_convert_fusion), channel_id=1, source_target_pairs={{0,12},{1,13},{2,14},{3,15},{4,0},{5,1},{6,2},{7,3},{8,4},{9,5},{1... | collective-permute-start | bytes 2457608 | tf_op jit(solution)/shard_map/ppermute | solution.py:56
  152.9 9.6 %collective-permute-start.29 = (bf16[40,5120]{1,0:T(8,128)(2,1)S(1)}, bf16[40,5120]{1,0:T(8,128)(2,1)S(1)}, u32[]{:S(2)}, u32[]{:S(2)}) collective-permute-start(bf16[40,5120]{1,0:T(8,128)(2,1)S(1)} %get-tuple-element.66), channel_id=1, source_target_pairs={{0,2},{1,3},{2,0},{3,1},{4,6},{5,7},{6,4},{7,5},{8,10},{9,11},{10,... | collective-permute-start | bytes 1228808 | tf_op jit(solution)/shard_map/ppermute | solution.py:56
  155.2 9.5 %collective-permute-start.28 = (bf16[40,5120]{1,0:T(8,128)(2,1)S(1)}, bf16[40,5120]{1,0:T(8,128)(2,1)S(1)}, u32[]{:S(2)}, u32[]{:S(2)}) collective-permute-start(bf16[40,5120]{1,0:T(8,128)(2,1)S(1)} %get-tuple-element.65), channel_id=1, source_target_pairs={{0,1},{1,2},{2,3},{3,0},{4,5},{5,6},{6,7},{7,4},{8,9},{9,10},{10,1... | collective-permute-start | bytes 1228808 | tf_op jit(solution)/shard_map/ppermute | solution.py:56
  156.8 10.1 %collective-permute-start.27 = (bf16[40,5120]{1,0:T(8,128)(2,1)S(1)}, bf16[40,5120]{1,0:T(8,128)(2,1)S(1)}, u32[]{:S(2)}, u32[]{:S(2)}) collective-permute-start(bf16[40,5120]{1,0:T(8,128)(2,1)S(1)} %get-tuple-element.64), channel_id=1, source_target_pairs={{0,3},{1,0},{2,1},{3,2},{4,7},{5,4},{6,5},{7,6},{8,11},{9,8},{10,9... | collective-permute-start | bytes 1228808 | tf_op jit(solution)/shard_map/ppermute | solution.py:56
  167.2 8.6 %collective-permute-start.30 = (bf16[10,5120]{1,0:T(8,128)(2,1)S(1)}, bf16[10,5120]{1,0:T(8,128)(2,1)S(1)}, u32[]{:S(2)}, u32[]{:S(2)}) collective-permute-start(bf16[10,5120]{1,0:T(8,128)(2,1)S(1)} %get-tuple-element.71), channel_id=1, source_target_pairs={{32,0},{33,1},{34,2},{35,3},{36,4},{37,5},{38,6},{39,7},{40,8},{41... | collective-permute-start | bytes 307208 | tf_op jit(solution)/shard_map/ppermute | solution.py:56
  168.6 11.2 %collective-permute-start.31 = (bf16[10,5120]{1,0:T(8,128)(2,1)S(1)}, bf16[10,5120]{1,0:T(8,128)(2,1)S(1)}, u32[]{:S(2)}, u32[]{:S(2)}) collective-permute-start(bf16[10,5120]{1,0:T(8,128)(2,1)S(1)} %get-tuple-element.70), channel_id=1, source_target_pairs={{80,0},{81,1},{82,2},{83,3},{84,4},{85,5},{86,6},{87,7},{88,8},{89... | collective-permute-start | bytes 307208 | tf_op jit(solution)/shard_map/ppermute | solution.py:56
  169.8 14.3 %collective-permute-start.32 = (bf16[10,5120]{1,0:T(8,128)(2,1)S(1)}, bf16[10,5120]{1,0:T(8,128)(2,1)S(1)}, u32[]{:S(2)}, u32[]{:S(2)}) collective-permute-start(bf16[10,5120]{1,0:T(8,128)(2,1)S(1)} %get-tuple-element.69), channel_id=1, source_target_pairs={{112,0},{113,1},{114,2},{115,3},{116,4},{117,5},{118,6},{119,7},{1... | collective-permute-start | bytes 307208 | tf_op jit(solution)/shard_map/ppermute | solution.py:56
  (25 other events, 257.3 us)
where the time goes:
time: 188 us; the launch traced here: 187 us
  waiting for transfers between devices  104 us (55%)
  starting transfers between devices  44.1 us (23%)
  Pallas kernels  28.3 us (15%)
  local copies, waits for them, and re-layouts  7.22 us (4%)
  other arithmetic  2.18 us (1%)
    ppermute x33, waiting for transfers between devices, send(): return lax.ppermute(value, ALL, pairs)  104 us
    ppermute x33, starting transfers between devices, send(): return lax.ppermute(value, ALL, pairs)  44.1 us
    pallas_call x4, Pallas kernels, hidden(): pl.pallas_call(functools.partial(hidden_kernel, count, parts), out_shape=...  15.9 us
    pallas_call x1, Pallas kernels, down(): pl.pallas_call(down_kernel, out_shape=tuple((jax.ShapeDtypeStruct((LINE,...  4.1 us
    pallas_call x1, Pallas kernels, attention(): pl.pallas_call(attention_kernel, out_shape=(jax.ShapeDtypeStruct((TOK, D)...  3.83 us
  transfers between devices with their start and end apart: 33, of which 18 were waited for; matrix products, arithmetic and copies ran while one was open for 3% of the time, Pallas kernels for 11%

commit v1 on v0

--- a/solution.py
+++ b/solution.py
@@ -110,7 +110,7 @@
         in_specs=[pl.BlockSpec(memory_space=pltpu.SMEM)] + [vmem] * 9,
         out_specs=(vmem,) * 6,
         scratch_shapes=[pltpu.VMEM((TOK, TOK), jnp.float32)],
-        compiler_params=pltpu.CompilerParams(vmem_limit_bytes=32 * MIB),
+        compiler_params=pltpu.CompilerParams(vmem_limit_bytes=14 * MIB),
         cost_estimate=pl.CostEstimate(flops=400_000_000, bytes_accessed=6_000_000, transcendentals=660_000),
         name="attention",
     )(info, q0, q1, k0, k1, v0, v1, bias, route, gain)
@@ -156,7 +156,7 @@
         out_shape=jax.ShapeDtypeStruct((total, n * FF), jnp.bfloat16),
         in_specs=[pl.BlockSpec(memory_space=pltpu.SMEM)] + [vmem] * (count + len(weights)),
         out_specs=vmem,
-        compiler_params=pltpu.CompilerParams(vmem_limit_bytes=24 * MIB),
+        compiler_params=pltpu.CompilerParams(vmem_limit_bytes=18 * MIB),
         cost_estimate=pl.CostEstimate(flops=max(flops, 4 * total * D * n * FF), bytes_accessed=4 * D * n * FF + 2 * total * D, transcendentals=total * n * FF),
         name="hidden",
     )(info, *xs, *weights)
@@ -187,7 +187,7 @@
         out_shape=tuple(jax.ShapeDtypeStruct((LINE, HALF), jnp.bfloat16) for _ in range(8)),
         in_specs=[pl.BlockSpec(memory_space=pltpu.SMEM)] + [vmem] * (len(hs) + 3),
         out_specs=(vmem,) * 8,
-        compiler_params=pltpu.CompilerParams(vmem_limit_bytes=24 * MIB),
+        compiler_params=pltpu.CompilerParams(vmem_limit_bytes=20 * MIB),
         cost_estimate=pl.CostEstimate(flops=2 * total * 2 * FF * D, bytes_accessed=4 * FF * D + 2 * total * D, transcendentals=0),
         name="down",
     )(info, *hs, own_w, wa, wb)
@@ -202,6 +202,7 @@
         in_specs=[hbm],
         out_specs=hbm,
         input_output_aliases={0: 0},
+        compiler_params=pltpu.CompilerParams(vmem_limit_bytes=MIB),
         cost_estimate=pl.CostEstimate(flops=flops, bytes_accessed=0, transcendentals=0),
         name="hold",
     )(value)
@@ -225,7 +226,7 @@
         out_shape=tuple(jax.ShapeDtypeStruct((ROWS, D), jnp.bfloat16) for _ in range(4)),
         in_specs=[vmem] * 6,
         out_specs=(vmem,) * 4,
-        compiler_params=pltpu.CompilerParams(vmem_limit_bytes=24 * MIB),
+        compiler_params=pltpu.CompilerParams(vmem_limit_bytes=12 * MIB),
         cost_estimate=pl.CostEstimate(flops=2 * LINE * D, bytes_accessed=8 * LINE * D, transcendentals=0),
         name="line_sums",
     )(*halves[0], *halves[1])
@@ -246,7 +247,7 @@
         out_shape=jax.ShapeDtypeStruct((rows, D), jnp.bfloat16),
         in_specs=[vmem] * len(parts),
         out_specs=vmem,
-        compiler_params=pltpu.CompilerParams(vmem_limit_bytes=16 * MIB),
+        compiler_params=pltpu.CompilerParams(vmem_limit_bytes=8 * MIB),
         cost_estimate=pl.CostEstimate(flops=0, bytes_accessed=4 * rows * D, transcendentals=0),
         name="stack",
     )(*parts)
@@ -270,7 +271,7 @@
         out_shape=jax.ShapeDtypeStruct((TOK, D), jnp.bfloat16),
         in_specs=[vmem] * 6,
         out_specs=vmem,
-        compiler_params=pltpu.CompilerParams(vmem_limit_bytes=32 * MIB),
+        compiler_params=pltpu.CompilerParams(vmem_limit_bytes=10 * MIB),
         cost_estimate=pl.CostEstimate(flops=60_000_000, bytes_accessed=3_000_000, transcendentals=0),
         name="combine",
     )(pick, attn, *rows)
@@ -309,24 +310,24 @@
     moved = [send(rows[k], to_expert(k)) for k in (1, 2, 3)]
     mine = jnp.concatenate([rows[0]] + after(moved, g_first), axis=0)
     g_rest = lax.dynamic_slice_in_dim(gate_weight, dp * HALF + CUT, HALF - CUT, 0)
-    g_rest = send(after(g_rest, moved), across)
+    g_rest = send(after(g_rest, pick), across)
     line = stack([mine] + [send(mine, plane_shift(1, s)) for s in (1, 3, 2)])
-    line_out = after(line, g_rest)
-    c1, c3, c2 = (send(line_out, plane_shift(2, s)) for s in (1, 3, 2))
+    c1, c3, c2 = (send(line, plane_shift(2, s)) for s in (1, 3, 2))
     u_half = lax.dynamic_slice_in_dim(up_weight, dp * HALF, HALF, 0)
-    u_half = send(after(u_half, line_out), across)
+    u_half = send(after(u_half, moved), across)
 
     own_gu = (gate_weight, up_weight)
-    h_line = hidden(info, [line], ("own",), own_gu)
+    g_rest = hold(g_rest, 3*HINT)
+    h_line = hidden(info, [after(line, g_rest)], ("own",), own_gu)
     g_first, g_rest, u_half = after((g_first, g_rest, u_half), h_line)
     other_gu = (g_first, g_rest, send(g_first, beside), send(g_rest, beside), u_half, send(u_half, beside))
     h_near = hidden(info, [c1, c3], ("own",), own_gu, HINT)
-    wa = send(after(lax.dynamic_slice_in_dim(down_weight, dp * (FF // 2), FF // 2, 0), line_out), across)
+    wa = send(after(lax.dynamic_slice_in_dim(down_weight, dp * (FF // 2), FF // 2, 0), line), across)
     h_other = hidden(info, [after(line, h_near), c1, c3], ("other",), other_gu)
-    h_last = hidden(info, [after(c2, h_other)], ("own", "other"), own_gu + other_gu)
+    wa = hold(after(wa, (h_other, c2)), 3*HINT//2)
+    h_last = hidden(info, [after(c2, wa)], ("own", "other"), own_gu + other_gu)
     hs = (h_line, h_near, h_other, h_last)
 
-    wa = after(wa, h_last)
     outs0, outs1 = down(info, hs, down_weight, wa, send(wa, beside))
 
     relay0 = send(outs0[3], plane_shift(2, 1))

time: 188 us -> 182 us (0.968)
  waiting for transfers between devices: 104 us -> 84 us
  starting transfers between devices: 44.1 us -> 56.8 us
  local copies, waits for them, and re-layouts: 7.22 us -> 14.2 us
  Pallas kernels: 28.3 us -> 23 us
    ppermute x33, waiting for transfers between devices: 104 us -> 84 us  [send(): return lax.ppermute(value, ALL, pairs)]
    ppermute x33, starting transfers between devices: 44.1 us -> 56.8 us  [send(): return lax.ppermute(value, ALL, pairs)]
    unnamed x32 -> x38, local copies, waits for them, and re-layouts: 3.39 us -> 11.4 us
    pallas_call x4, Pallas kernels: 15.9 us -> 11 us  [hidden(): pl.pallas_call(functools.partial(hidden_kernel, count, parts), out_shape=...]
  transfers between devices with their start and end apart: 33 -> 33, of which waited for: 18 -> 19; matrix products, arithmetic and copies ran while one was open for 3% -> 3% of each run, Pallas kernels for 11% -> 9%
where the time goes in v1:
time: 182 us; the launch traced here: 181 us
  waiting for transfers between devices  84 us (46%)
  starting transfers between devices  56.8 us (31%)
  Pallas kernels  23 us (13%)
  local copies, waits for them, and re-layouts  14.2 us (8%)
  other arithmetic  2.39 us (1%)
    ppermute x33, waiting for transfers between devices, send(): return lax.ppermute(value, ALL, pairs)  84 us
    ppermute x33, starting transfers between devices, send(): return lax.ppermute(value, ALL, pairs)  56.8 us
    unnamed x38, local copies, waits for them, and re-layouts  11.4 us
    pallas_call x4, Pallas kernels, hidden(): pl.pallas_call(functools.partial(hidden_kernel, count, parts), out_shape=...  11 us
    pallas_call x1, Pallas kernels, down(): pl.pallas_call(down_kernel, out_shape=tuple((jax.ShapeDtypeStruct((LINE,...  4.11 us
  transfers between devices with their start and end apart: 33, of which 19 were waited for; matrix products, arithmetic and copies ran while one was open for 3% of the time, Pallas kernels for 9%

profile of v1, /device:TPU:6, one launch (start us, length us, event | category | flops | bytes accessed | tf_op | source)
XLA Modules:
  0.0 181.4 jit_solution(16441729680445692871)
XLA Ops:
  15.7 3.2 %attention.1 = (bf16[128,5120]{1,0:T(8,128)(2,1)S(1)}, bf16[64,128]{1,0:T(8,128)(2,1)S(1)}, bf16[10,5120]{1,0:T(8,128)(2,1)S(1)}, bf16[10,5120]{1,0:T(8,128)(2,1...) custom-call(s32[4]{0:T(128)S(1)} %pad_add_fusion.info, bf16[128,5120]{1,0:T(8,128)(2,1)S(1)} %copy-done.2, ...), custom_call_target="tpu_custom_call" | custom-call | flops 400000000 | bytes 6000000 | tf_op jit(solution)/shard_map/attention/pallas_call | solution.py:103
  20.0 3.3 %collective-permute-start.4 = (bf16[10,5120]{1,0:T(8,128)(2,1)S(1)}, bf16[10,5120]{1,0:T(8,128)(2,1)S(1)}, u32[]{:S(2)}, u32[]{:S(2)}) collective-permute-start(bf16[10,5120]{1,0:T(8,128)(2,1)S(1)} %get-tuple-element.39), channel_id=1, source_target_pairs={{0,32},{1,33},{2,34},{3,35},{4,36},{5,37},{6,38},{7,39},{8,40},{9,... | collective-permute-start | bytes 307208 | tf_op jit(solution)/shard_map/ppermute | solution.py:56
  23.3 2.6 %collective-permute-start.5 = (bf16[10,5120]{1,0:T(8,128)(2,1)S(1)}, bf16[10,5120]{1,0:T(8,128)(2,1)S(1)}, u32[]{:S(2)}, u32[]{:S(2)}) collective-permute-start(bf16[10,5120]{1,0:T(8,128)(2,1)S(1)} %get-tuple-element.40), channel_id=1, source_target_pairs={{0,80},{1,81},{2,82},{3,83},{4,84},{5,85},{6,86},{7,87},{8,88},{9,... | collective-permute-start | bytes 307208 | tf_op jit(solution)/shard_map/ppermute | solution.py:56
  25.8 3.7 %collective-permute-start.6 = (bf16[10,5120]{1,0:T(8,128)(2,1)S(1)}, bf16[10,5120]{1,0:T(8,128)(2,1)S(1)}, u32[]{:S(2)}, u32[]{:S(2)}) collective-permute-start(bf16[10,5120]{1,0:T(8,128)(2,1)S(1)} %get-tuple-element.41), channel_id=1, source_target_pairs={{0,112},{1,113},{2,114},{3,115},{4,116},{5,117},{6,118},{7,119},{8... | collective-permute-start | bytes 307208 | tf_op jit(solution)/shard_map/ppermute | solution.py:56
  30.2 6.3 %collective-permute-done.5 = bf16[10,5120]{1,0:T(8,128)(2,1)S(1)} collective-permute-done((bf16[10,5120]{1,0:T(8,128)(2,1)S(1)}, bf16[10,5120]{1,0:T(8,128)(2,1)S(1)}, u32[]{:S(2)}, u32[]{:S(2)}) %collective-permute-start.5) | collective-permute-done | bytes 102432 | tf_op jit(solution)/shard_map/ppermute | solution.py:56
  36.5 4.1 %collective-permute-done.6 = bf16[10,5120]{1,0:T(8,128)(2,1)S(1)} collective-permute-done((bf16[10,5120]{1,0:T(8,128)(2,1)S(1)}, bf16[10,5120]{1,0:T(8,128)(2,1)S(1)}, u32[]{:S(2)}, u32[]{:S(2)}) %collective-permute-start.6) | collective-permute-done | bytes 102432 | tf_op jit(solution)/shard_map/ppermute | solution.py:56
  45.1 4.6 %collective-permute-done.8.refs_1_ = bf16[40,5120]{1,0:T(8,128)(2,1)} collective-permute-done((bf16[40,5120]{1,0:T(8,128)(2,1)}, bf16[40,5120]{1,0:T(8,128)(2,1)}, u32[]{:S(2)}, u32[]{:S(2)}) %collective-permute-start.8) | collective-permute-done | bytes 409632 | tf_op jit(solution)/shard_map/ppermute | solution.py:56
  49.8 6.1 %collective-permute-done.9.refs_2_ = bf16[40,5120]{1,0:T(8,128)(2,1)} collective-permute-done((bf16[40,5120]{1,0:T(8,128)(2,1)}, bf16[40,5120]{1,0:T(8,128)(2,1)}, u32[]{:S(2)}, u32[]{:S(2)}) %collective-permute-start.9) | collective-permute-done | bytes 409632 | tf_op jit(solution)/shard_map/ppermute | solution.py:56
  66.0 10.1 %collective-permute-done.14.refs_7_ = bf16[2560,256]{1,0:T(8,128)(2,1)S(1)} collective-permute-done((bf16[2560,256]{1,0:T(8,128)(2,1)S(1)}, bf16[2560,256]{1,0:T(8,128)(2,1)S(1)}, u32[]{:S(2)}, u32[]{:S(2)}) %collective-permute-start.14) | collective-permute-done | bytes 1310752 | tf_op jit(solution)/shard_map/ppermute | solution.py:56
  80.1 15.8 %collective-permute-start.16 = (bf16[1280,256]{1,0:T(8,128)(2,1)}, bf16[1280,256]{1,0:T(8,128)(2,1)S(1)}, u32[]{:S(2)}, u32[]{:S(2)}) collective-permute-start(bf16[1280,256]{1,0:T(8,128)(2,1)} %hold.2.refs_4_), channel_id=1, source_target_pairs={{0,128},{1,129},{2,130},{3,131},{4,132},{5,133},{6,134},{7,135},{8... | collective-permute-start | bytes 1966088 | tf_op jit(solution)/shard_map/ppermute | solution.py:56
  98.5 3.9 %hidden.6.h_other = bf16[480,256]{1,0:T(8,128)(2,1)S(1)} custom-call(s32[4]{0:T(128)S(1)} %copy-done.15, bf16[160,5120]{1,0:T(8,128)(2,1)S(1)} %stack.17.refs_0_, bf16[160,5120]{1,0:T(8,128)(2,1)S(1)} %collective-permute-done.12.refs_0_.refs_1_, bf16[160,5120]{1,0:T(8,128)(2,1)S(1)} %collective-permute-done.13.refs_1_.refs_2_, ...), custom_call_target="tpu_custom_call" | custom-call | flops 2516582400 | bytes 10158080 | tf_op jit(solution)/shard_map/hidden/pallas_call | solution.py:154
  102.3 5.1 %collective-permute-done.19.value_ref = bf16[128,5120]{1,0:T(8,128)(2,1)S(1)} collective-permute-done((bf16[128,5120]{1,0:T(8,128)(2,1)S(1)}, bf16[128,5120]{1,0:T(8,128)(2,1)S(1)}, u32[]{:S(2)}, u32[]{:S(2)}) %collective-permute-start.19) | collective-permute-done | bytes 1310752 | tf_op jit(solution)/shard_map/ppermute | solution.py:56
  107.4 3.1 %hidden.7.h_last = bf16[160,512]{1,0:T(8,128)(2,1)S(1)} custom-call(s32[4]{0:T(128)S(1)} %copy-done.15, bf16[160,5120]{1,0:T(8,128)(2,1)S(1)} %collective-permute-done.18.refs_0_, bf16[5120,256]{1,0:T(8,128)(2,1)S(1)} %copy-done, bf16[5120,256]{1,0:T(8,128)(2,1)S(1)} %copy-done.1, bf16[1280,256]{1,0:T(8,128)(2,1)S(1)} %collective-permute-done.7.refs_3_, ...), custom_call_target="tpu_custom_call" | custom-call | flops 1677721600 | bytes 12124160 | tf_op jit(solution)/shard_map/hidden/pallas_call | solution.py:154
  110.5 4.1 %down.1 = (bf16[160,2560]{1,0:T(8,128)(2,1)S(1)}, bf16[160,2560]{1,0:T(8,128)(2,1)S(1)}, bf16[160,2560]{1,0:T(8,128)(2,1)S(1)}, bf16[160,2560]{1,0:T(8,128)(2,1)...) custom-call(s32[4]{0:T(128)S(1)} %copy-done.15, ...), custom_call_target="tpu_custom_call" | custom-call | flops 3355443200 | bytes 11796480 | tf_op jit(solution)/shard_map/down/pallas_call | solution.py:185
  120.2 8.3 %collective-permute-done.22 = bf16[160,2560]{1,0:T(8,128)(2,1)S(1)} collective-permute-done((bf16[160,2560]{1,0:T(8,128)(2,1)S(1)}, bf16[160,2560]{1,0:T(8,128)(2,1)S(1)}, u32[]{:S(2)}, u32[]{:S(2)}) %collective-permute-start.22) | collective-permute-done | bytes 819232 | tf_op jit(solution)/shard_map/ppermute | solution.py:56
  129.3 3.0 %collective-permute-start.26 = (bf16[160,2560]{1,0:T(8,128)(2,1)S(1)}, bf16[160,2560]{1,0:T(8,128)(2,1)S(1)}, u32[]{:S(2)}, u32[]{:S(2)}) collective-permute-start(bf16[160,2560]{1,0:T(8,128)(2,1)S(1)} %add_convert_fusion), channel_id=1, source_target_pairs={{0,12},{1,13},{2,14},{3,15},{4,0},{5,1},{6,2},{7,3},{8,4},{9,5},{1... | collective-permute-start | bytes 2457608 | tf_op jit(solution)/shard_map/ppermute | solution.py:56
  132.3 5.3 %collective-permute-done.21.refs_1_ = bf16[160,2560]{1,0:T(8,128)(2,1)S(1)} collective-permute-done((bf16[160,2560]{1,0:T(8,128)(2,1)S(1)}, bf16[160,2560]{1,0:T(8,128)(2,1)S(1)}, u32[]{:S(2)}, u32[]{:S(2)}) %collective-permute-start.21) | collective-permute-done | bytes 819232 | tf_op jit(solution)/shard_map/ppermute | solution.py:56
  137.6 8.5 %collective-permute-done.23.refs_2_ = bf16[160,2560]{1,0:T(8,128)(2,1)S(1)} collective-permute-done((bf16[160,2560]{1,0:T(8,128)(2,1)S(1)}, bf16[160,2560]{1,0:T(8,128)(2,1)S(1)}, u32[]{:S(2)}, u32[]{:S(2)}) %collective-permute-start.23) | collective-permute-done | bytes 819232 | tf_op jit(solution)/shard_map/ppermute | solution.py:56
  150.5 6.1 %collective-permute-done.29 = bf16[40,5120]{1,0:T(8,128)(2,1)S(1)} collective-permute-done((bf16[40,5120]{1,0:T(8,128)(2,1)S(1)}, bf16[40,5120]{1,0:T(8,128)(2,1)S(1)}, u32[]{:S(2)}, u32[]{:S(2)}) %collective-permute-start.29) | collective-permute-done | bytes 409632 | tf_op jit(solution)/shard_map/ppermute | solution.py:56
  161.2 3.2 %collective-permute-start.30 = (bf16[10,5120]{1,0:T(8,128)(2,1)S(1)}, bf16[10,5120]{1,0:T(8,128)(2,1)S(1)}, u32[]{:S(2)}, u32[]{:S(2)}) collective-permute-start(bf16[10,5120]{1,0:T(8,128)(2,1)S(1)} %get-tuple-element.71), channel_id=1, source_target_pairs={{32,0},{33,1},{34,2},{35,3},{36,4},{37,5},{38,6},{39,7},{40,8},{41... | collective-permute-start | bytes 307208 | tf_op jit(solution)/shard_map/ppermute | solution.py:56
  164.4 2.7 %collective-permute-start.31 = (bf16[10,5120]{1,0:T(8,128)(2,1)S(1)}, bf16[10,5120]{1,0:T(8,128)(2,1)S(1)}, u32[]{:S(2)}, u32[]{:S(2)}) collective-permute-start(bf16[10,5120]{1,0:T(8,128)(2,1)S(1)} %get-tuple-element.70), channel_id=1, source_target_pairs={{80,0},{81,1},{82,2},{83,3},{84,4},{85,5},{86,6},{87,7},{88,8},{89... | collective-permute-start | bytes 307208 | tf_op jit(solution)/shard_map/ppermute | solution.py:56
  167.0 4.1 %collective-permute-done.30.r1 = bf16[10,5120]{1,0:T(8,128)(2,1)S(1)} collective-permute-done((bf16[10,5120]{1,0:T(8,128)(2,1)S(1)}, bf16[10,5120]{1,0:T(8,128)(2,1)S(1)}, u32[]{:S(2)}, u32[]{:S(2)}) %collective-permute-start.30) | collective-permute-done | bytes 102432 | tf_op jit(solution)/shard_map/ppermute | solution.py:56
  171.2 6.8 %collective-permute-done.31.r2 = bf16[10,5120]{1,0:T(8,128)(2,1)S(1)} collective-permute-done((bf16[10,5120]{1,0:T(8,128)(2,1)S(1)}, bf16[10,5120]{1,0:T(8,128)(2,1)S(1)}, u32[]{:S(2)}, u32[]{:S(2)}) %collective-permute-start.31) | collective-permute-done | bytes 102432 | tf_op jit(solution)/shard_map/ppermute | solution.py:56
  178.7 2.6 %combine.1 = bf16[128,5120]{1,0:T(8,128)(2,1)} custom-call(bf16[64,128]{1,0:T(8,128)(2,1)S(1)} %get-tuple-element.36.pick_ref, bf16[128,5120]{1,0:T(8,128)(2,1)S(1)} %copy-done.4, bf16[10,5120]{1,0:T(8,128)(2,1)S(1)} %get-tuple-element.72.r0, bf16[10,5120]{1,0:T(8,128)(2,1)S(1)} %collective-permute-done.30.r1, ...), custom_call_target="tpu_custom_call" | custom-call | flops 60000000 | bytes 3000000 | tf_op jit(solution)/shard_map/combine/pallas_call | solution.py:269
  (104 shorter events, 54.0 us)
Async XLA Ops:
  4.3 25.3 %collective-permute-start.7 = (bf16[1280,256]{1,0:T(8,128)(2,1)}, bf16[1280,256]{1,0:T(8,128)(2,1)S(1)}, u32[]{:S(2)}, u32[]{:S(2)}) collective-permute-start(bf16[1280,256]{1,0:T(8,128)(2,1)} %get-tuple-element.68), channel_id=1, source_target_pairs={{0,16},{1,17},{2,18},{3,19},{4,20},{5,21},{6,22},{7,23},{8,24},{9,... | collective-permute-start | bytes 1966088 | tf_op jit(solution)/shard_map/ppermute | solution.py:56
  23.3 13.2 %collective-permute-start.5 = (bf16[10,5120]{1,0:T(8,128)(2,1)S(1)}, bf16[10,5120]{1,0:T(8,128)(2,1)S(1)}, u32[]{:S(2)}, u32[]{:S(2)}) collective-permute-start(bf16[10,5120]{1,0:T(8,128)(2,1)S(1)} %get-tuple-element.40), channel_id=1, source_target_pairs={{0,80},{1,81},{2,82},{3,83},{4,84},{5,85},{6,86},{7,87},{8,88},{9,... | collective-permute-start | bytes 307208 | tf_op jit(solution)/shard_map/ppermute | solution.py:56
  25.8 14.7 %collective-permute-start.6 = (bf16[10,5120]{1,0:T(8,128)(2,1)S(1)}, bf16[10,5120]{1,0:T(8,128)(2,1)S(1)}, u32[]{:S(2)}, u32[]{:S(2)}) collective-permute-start(bf16[10,5120]{1,0:T(8,128)(2,1)S(1)} %get-tuple-element.41), channel_id=1, source_target_pairs={{0,112},{1,113},{2,114},{3,115},{4,116},{5,117},{6,118},{7,119},{8... | collective-permute-start | bytes 307208 | tf_op jit(solution)/shard_map/ppermute | solution.py:56
  29.5 33.1 %collective-permute-start.11 = (bf16[1280,256]{1,0:T(8,128)(2,1)}, bf16[1280,256]{1,0:T(8,128)(2,1)}, u32[]{:S(2)}, u32[]{:S(2)}) collective-permute-start(bf16[1280,256]{1,0:T(8,128)(2,1)} %get-tuple-element.45), channel_id=1, source_target_pairs={{0,16},{1,17},{2,18},{3,19},{4,20},{5,21},{6,22},{7,23},{8,24},{9,... | collective-permute-start | bytes 1966088 | tf_op jit(solution)/shard_map/ppermute | solution.py:56
  42.0 13.9 %collective-permute-start.9 = (bf16[40,5120]{1,0:T(8,128)(2,1)}, bf16[40,5120]{1,0:T(8,128)(2,1)}, u32[]{:S(2)}, u32[]{:S(2)}) collective-permute-start(bf16[40,5120]{1,0:T(8,128)(2,1)} %pad_maximum_fusion.refs_0_), channel_id=1, source_target_pairs={{0,3},{1,0},{2,1},{3,2},{4,7},{5,4},{6,5},{7,6},{8,11},{9,8},{10,9... | collective-permute-start | bytes 1228808 | tf_op jit(solution)/shard_map/ppermute | solution.py:56
  43.5 12.3 %collective-permute-start.10 = (bf16[40,5120]{1,0:T(8,128)(2,1)}, bf16[40,5120]{1,0:T(8,128)(2,1)}, u32[]{:S(2)}, u32[]{:S(2)}) collective-permute-start(bf16[40,5120]{1,0:T(8,128)(2,1)} %pad_maximum_fusion.refs_0_), channel_id=1, source_target_pairs={{0,2},{1,3},{2,0},{3,1},{4,6},{5,7},{6,4},{7,5},{8,10},{9,11},{10,... | collective-permute-start | bytes 1228808 | tf_op jit(solution)/shard_map/ppermute | solution.py:56
  45.0 31.1 %collective-permute-start.14 = (bf16[2560,256]{1,0:T(8,128)(2,1)S(1)}, bf16[2560,256]{1,0:T(8,128)(2,1)S(1)}, u32[]{:S(2)}, u32[]{:S(2)}) collective-permute-start(bf16[2560,256]{1,0:T(8,128)(2,1)S(1)} %constant_dynamic-slice_fusion.1), channel_id=1, source_target_pairs={{0,16},{1,17},{2,18},{3,19},{4,20},{5,21},{6,22},{7,23},{8,24},{9,... | collective-permute-start | bytes 3932168 | tf_op jit(solution)/shard_map/ppermute | solution.py:56
  57.3 22.4 %collective-permute-start.12 = (bf16[160,5120]{1,0:T(8,128)(2,1)S(1)}, bf16[160,5120]{1,0:T(8,128)(2,1)S(1)}, u32[]{:S(2)}, u32[]{:S(2)}) collective-permute-start(bf16[160,5120]{1,0:T(8,128)(2,1)S(1)} %stack.17.refs_0_), channel_id=1, source_target_pairs={{0,4},{1,5},{2,6},{3,7},{4,8},{5,9},{6,10},{7,11},{8,12},{9,13},{1... | collective-permute-start | bytes 4915208 | tf_op jit(solution)/shard_map/ppermute | solution.py:56
  59.0 21.1 %collective-permute-start.13 = (bf16[160,5120]{1,0:T(8,128)(2,1)S(1)}, bf16[160,5120]{1,0:T(8,128)(2,1)S(1)}, u32[]{:S(2)}, u32[]{:S(2)}) collective-permute-start(bf16[160,5120]{1,0:T(8,128)(2,1)S(1)} %stack.17.refs_0_), channel_id=1, source_target_pairs={{0,12},{1,13},{2,14},{3,15},{4,0},{5,1},{6,2},{7,3},{8,4},{9,5},{1... | collective-permute-start | bytes 4915208 | tf_op jit(solution)/shard_map/ppermute | solution.py:56
  60.7 46.7 %collective-permute-start.18 = (bf16[160,5120]{1,0:T(8,128)(2,1)S(1)}, bf16[160,5120]{1,0:T(8,128)(2,1)S(1)}, u32[]{:S(2)}, u32[]{:S(2)}) collective-permute-start(bf16[160,5120]{1,0:T(8,128)(2,1)S(1)} %stack.17.refs_0_), channel_id=1, source_target_pairs={{0,8},{1,9},{2,10},{3,11},{4,12},{5,13},{6,14},{7,15},{8,0},{9,1},... | collective-permute-start | bytes 4915208 | tf_op jit(solution)/shard_map/ppermute | solution.py:56
  76.1 22.4 %collective-permute-start.17 = (bf16[2560,256]{1,0:T(8,128)(2,1)S(1)}, bf16[2560,256]{1,0:T(8,128)(2,1)S(1)}, u32[]{:S(2)}, u32[]{:S(2)}) collective-permute-start(bf16[2560,256]{1,0:T(8,128)(2,1)S(1)} %collective-permute-done.14.refs_7_), channel_id=1, source_target_pairs={{0,128},{1,129},{2,130},{3,131},{4,132},{5,133},{6,134},{7,135},{8... | collective-permute-start | bytes 3932168 | tf_op jit(solution)/shard_map/ppermute | solution.py:56
  76.2 31.3 %collective-permute-start.19 = (bf16[128,5120]{1,0:T(8,128)(2,1)S(1)}, bf16[128,5120]{1,0:T(8,128)(2,1)S(1)}, u32[]{:S(2)}, u32[]{:S(2)}) collective-permute-start(bf16[128,5120]{1,0:T(8,128)(2,1)S(1)} %constant_dynamic-slice_fusion), channel_id=1, source_target_pairs={{0,16},{1,17},{2,18},{3,19},{4,20},{5,21},{6,22},{7,23},{8,24},{9,... | collective-permute-start | bytes 3932168 | tf_op jit(solution)/shard_map/ppermute | solution.py:56
  79.7 18.7 %collective-permute-start.15 = (bf16[1280,256]{1,0:T(8,128)(2,1)S(1)}, bf16[1280,256]{1,0:T(8,128)(2,1)S(1)}, u32[]{:S(2)}, u32[]{:S(2)}) collective-permute-start(bf16[1280,256]{1,0:T(8,128)(2,1)S(1)} %collective-permute-done.7.refs_3_), channel_id=1, source_target_pairs={{0,128},{1,129},{2,130},{3,131},{4,132},{5,133},{6,134},{7,135},{8... | collective-permute-start | bytes 1966088 | tf_op jit(solution)/shard_map/ppermute | solution.py:56
  80.1 18.3 %collective-permute-start.16 = (bf16[1280,256]{1,0:T(8,128)(2,1)}, bf16[1280,256]{1,0:T(8,128)(2,1)S(1)}, u32[]{:S(2)}, u32[]{:S(2)}) collective-permute-start(bf16[1280,256]{1,0:T(8,128)(2,1)} %hold.2.refs_4_), channel_id=1, source_target_pairs={{0,128},{1,129},{2,130},{3,131},{4,132},{5,133},{6,134},{7,135},{8... | collective-permute-start | bytes 1966088 | tf_op jit(solution)/shard_map/ppermute | solution.py:56
  114.6 13.8 %collective-permute-start.22 = (bf16[160,2560]{1,0:T(8,128)(2,1)S(1)}, bf16[160,2560]{1,0:T(8,128)(2,1)S(1)}, u32[]{:S(2)}, u32[]{:S(2)}) collective-permute-start(bf16[160,2560]{1,0:T(8,128)(2,1)S(1)} %get-tuple-element.58), channel_id=1, source_target_pairs={{0,4},{1,5},{2,6},{3,7},{4,8},{5,9},{6,10},{7,11},{8,12},{9,13},{1... | collective-permute-start | bytes 2457608 | tf_op jit(solution)/shard_map/ppermute | solution.py:56
  116.5 12.7 %collective-permute-start.25 = (bf16[160,2560]{1,0:T(8,128)(2,1)S(1)}, bf16[160,2560]{1,0:T(8,128)(2,1)S(1)}, u32[]{:S(2)}, u32[]{:S(2)}) collective-permute-start(bf16[160,2560]{1,0:T(8,128)(2,1)S(1)} %get-tuple-element.62), channel_id=1, source_target_pairs={{0,12},{1,13},{2,14},{3,15},{4,0},{5,1},{6,2},{7,3},{8,4},{9,5},{1... | collective-permute-start | bytes 2457608 | tf_op jit(solution)/shard_map/ppermute | solution.py:56
  118.2 19.4 %collective-permute-start.21 = (bf16[160,2560]{1,0:T(8,128)(2,1)S(1)}, bf16[160,2560]{1,0:T(8,128)(2,1)S(1)}, u32[]{:S(2)}, u32[]{:S(2)}) collective-permute-start(bf16[160,2560]{1,0:T(8,128)(2,1)S(1)} %get-tuple-element.56), channel_id=1, source_target_pairs={{0,12},{1,13},{2,14},{3,15},{4,0},{5,1},{6,2},{7,3},{8,4},{9,5},{1... | collective-permute-start | bytes 2457608 | tf_op jit(solution)/shard_map/ppermute | solution.py:56
  119.9 17.7 %collective-permute-start.24 = (bf16[160,2560]{1,0:T(8,128)(2,1)S(1)}, bf16[160,2560]{1,0:T(8,128)(2,1)S(1)}, u32[]{:S(2)}, u32[]{:S(2)}) collective-permute-start(bf16[160,2560]{1,0:T(8,128)(2,1)S(1)} %get-tuple-element.60), channel_id=1, source_target_pairs={{0,4},{1,5},{2,6},{3,7},{4,8},{5,9},{6,10},{7,11},{8,12},{9,13},{1... | collective-permute-start | bytes 2457608 | tf_op jit(solution)/shard_map/ppermute | solution.py:56
  128.7 17.3 %collective-permute-start.23 = (bf16[160,2560]{1,0:T(8,128)(2,1)S(1)}, bf16[160,2560]{1,0:T(8,128)(2,1)S(1)}, u32[]{:S(2)}, u32[]{:S(2)}) collective-permute-start(bf16[160,2560]{1,0:T(8,128)(2,1)S(1)} %add_convert_fusion.1), channel_id=1, source_target_pairs={{0,4},{1,5},{2,6},{3,7},{4,8},{5,9},{6,10},{7,11},{8,12},{9,13},{1... | collective-permute-start | bytes 2457608 | tf_op jit(solution)/shard_map/ppermute | solution.py:56
  129.3 17.0 %collective-permute-start.26 = (bf16[160,2560]{1,0:T(8,128)(2,1)S(1)}, bf16[160,2560]{1,0:T(8,128)(2,1)S(1)}, u32[]{:S(2)}, u32[]{:S(2)}) collective-permute-start(bf16[160,2560]{1,0:T(8,128)(2,1)S(1)} %add_convert_fusion), channel_id=1, source_target_pairs={{0,12},{1,13},{2,14},{3,15},{4,0},{5,1},{6,2},{7,3},{8,4},{9,5},{1... | collective-permute-start | bytes 2457608 | tf_op jit(solution)/shard_map/ppermute | solution.py:56
  148.4 10.3 %collective-permute-start.28 = (bf16[40,5120]{1,0:T(8,128)(2,1)S(1)}, bf16[40,5120]{1,0:T(8,128)(2,1)S(1)}, u32[]{:S(2)}, u32[]{:S(2)}) collective-permute-start(bf16[40,5120]{1,0:T(8,128)(2,1)S(1)} %get-tuple-element.65), channel_id=1, source_target_pairs={{0,1},{1,2},{2,3},{3,0},{4,5},{5,6},{6,7},{7,4},{8,9},{9,10},{10,1... | collective-permute-start | bytes 1228808 | tf_op jit(solution)/shard_map/ppermute | solution.py:56
  150.5 10.3 %collective-permute-start.27 = (bf16[40,5120]{1,0:T(8,128)(2,1)S(1)}, bf16[40,5120]{1,0:T(8,128)(2,1)S(1)}, u32[]{:S(2)}, u32[]{:S(2)}) collective-permute-start(bf16[40,5120]{1,0:T(8,128)(2,1)S(1)} %get-tuple-element.64), channel_id=1, source_target_pairs={{0,3},{1,0},{2,1},{3,2},{4,7},{5,4},{6,5},{7,6},{8,11},{9,8},{10,9... | collective-permute-start | bytes 1228808 | tf_op jit(solution)/shard_map/ppermute | solution.py:56
  164.4 13.6 %collective-permute-start.31 = (bf16[10,5120]{1,0:T(8,128)(2,1)S(1)}, bf16[10,5120]{1,0:T(8,128)(2,1)S(1)}, u32[]{:S(2)}, u32[]{:S(2)}) collective-permute-start(bf16[10,5120]{1,0:T(8,128)(2,1)S(1)} %get-tuple-element.70), channel_id=1, source_target_pairs={{80,0},{81,1},{82,2},{83,3},{84,4},{85,5},{86,6},{87,7},{88,8},{89... | collective-permute-start | bytes 307208 | tf_op jit(solution)/shard_map/ppermute | solution.py:56
  167.0 11.7 %collective-permute-start.32 = (bf16[10,5120]{1,0:T(8,128)(2,1)S(1)}, bf16[10,5120]{1,0:T(8,128)(2,1)S(1)}, u32[]{:S(2)}, u32[]{:S(2)}) collective-permute-start(bf16[10,5120]{1,0:T(8,128)(2,1)S(1)} %get-tuple-element.69), channel_id=1, source_target_pairs={{112,0},{113,1},{114,2},{115,3},{116,4},{117,5},{118,6},{119,7},{1... | collective-permute-start | bytes 307208 | tf_op jit(solution)/shard_map/ppermute | solution.py:56
  (28 other events, 180.2 us)

commit v2 on v1

--- a/solution.py
+++ b/solution.py
@@ -20,6 +20,7 @@
 ROWS = EXP_WIN * CAP
 LINE = 4 * ROWS
 HALF = D // 2
+QUARTER = D // 4
 CUT = 1280
 ALL = ("dp", "expert")
 MIB = 1 << 20
@@ -56,16 +57,30 @@
     return lax.ppermute(value, ALL, pairs)
 
 
-def attention_kernel(info, q0, q1, k0, k1, v0, v1, bias_ref, route_ref, gain_ref, attn_ref, pick_ref, b0, b1, b2, b3, acc):
-    moved = info[0] > 0
+def attention_kernel(info, q0, q1, k0, k1, v0, v1, bias_ref, route_ref, gain_ref, attn_ref, code_ref, b0, b1, b2, b3, acc, q, k, v, sem):
+    kept = [pltpu.make_async_copy(a, b, sem.at[i]) for i, (a, b) in enumerate(((k0, k), (q0, q), (v0, v)))]
+    swapped = [pltpu.make_async_copy(a, b, sem.at[i]) for i, (a, b) in enumerate(((k1, k), (q1, q), (v1, v)))]
+
+    @pl.when(info[0] > 0)
+    def _():
+        for c in swapped:
+            c.start()
+
+    @pl.when(info[0] <= 0)
+    def _():
+        for c in kept:
+            c.start()
+
     bias = bias_ref[...]
     acc[...] = jnp.zeros_like(acc)
+    for c in kept:
+        c.wait()
     for h in range(KVH):
         cols = slice(h * HD, (h + 1) * HD)
-        key = jnp.where(moved, k1[:, cols], k0[:, cols])
-        value = jnp.where(moved, v1[:, cols], v0[:, cols])
+        key = k[:, cols]
+        value = v[:, cols]
         heads = [slice((h * GROUP + g) * HD, (h * GROUP + g + 1) * HD) for g in range(GROUP)]
-        query = jnp.concatenate([jnp.where(moved, q1[:, c], q0[:, c]) for c in heads], axis=0)
+        query = jnp.concatenate([q[:, c] for c in heads], axis=0)
         scores = lax.dot_general(query, key, (((1,), (1,)), ((), ())), preferred_element_type=jnp.float32)
         scores = scores.reshape(GROUP, TOK, TOK) * HD ** (-0.5) + bias[None]
         top = jnp.max(scores, axis=-1, keepdims=True)
@@ -86,31 +101,42 @@
     chosen = (lax.broadcasted_iota(jnp.int32, (16, TOK), 0) == kind).astype(jnp.bfloat16)
     order = jnp.dot(chosen, earlier, preferred_element_type=jnp.float32)
     slot = jnp.sum(chosen.astype(jnp.float32) * order, axis=0, keepdims=True).astype(jnp.int32)
-    place = kind * 16 + slot
-    pick = (lax.broadcasted_iota(jnp.int32, (64, TOK), 0) == place).astype(jnp.bfloat16)
-    pick_ref[...] = pick
-    for n in range(8):
-        c = slice(n * 640, (n + 1) * 640)
-        normed = (attn_ref[:, c].astype(jnp.float32) * scale * gain_ref[:, c].astype(jnp.float32)).astype(jnp.bfloat16)
-        rows = jnp.dot(pick, normed, preferred_element_type=jnp.float32).astype(jnp.bfloat16)
+    code = jnp.where(kind < EXP_WIN, kind * ROWS + slot, -1000)
+    code_ref[...] = code
+    rows_at = lax.broadcasted_iota(jnp.int32, (4 * ROWS, TOK), 0)
+    picks = [(rows_at == code + q * CAP).astype(jnp.bfloat16) for q in range(4)]
+    half = QUARTER // 2
+    for n in range(2):
+        rows = None
+        for q in range(4):
+            c = slice(q * QUARTER + n * half, q * QUARTER + (n + 1) * half)
+            normed = (attn_ref[:, c].astype(jnp.float32) * scale * gain_ref[:, c].astype(jnp.float32)).astype(jnp.bfloat16)
+            term = jnp.dot(picks[q], normed, preferred_element_type=jnp.float32)
+            rows = term if rows is None else rows + term
         for i, b in enumerate((b0, b1, b2, b3)):
-            b[:, c] = rows[i * 16:i * 16 + CAP]
+            b[:, n * half:(n + 1) * half] = rows[i * ROWS:(i + 1) * ROWS].astype(jnp.bfloat16)
 
 
 def attention(info, q0, q1, k0, k1, v0, v1, bias, route, gain):
     vmem = pl.BlockSpec(memory_space=pltpu.VMEM)
-    rows = jax.ShapeDtypeStruct((CAP, D), jnp.bfloat16)
+    rows = jax.ShapeDtypeStruct((ROWS, QUARTER), jnp.bfloat16)
     return pl.pallas_call(
         attention_kernel,
         out_shape=(
             jax.ShapeDtypeStruct((TOK, D), jnp.bfloat16),
-            jax.ShapeDtypeStruct((64, TOK), jnp.bfloat16),
+            jax.ShapeDtypeStruct((1, TOK), jnp.int32),
             rows, rows, rows, rows,
         ),
-        in_specs=[pl.BlockSpec(memory_space=pltpu.SMEM)] + [vmem] * 9,
+        in_specs=[pl.BlockSpec(memory_space=pltpu.SMEM)] + [pl.BlockSpec(memory_space=pl.ANY)] * 6 + [vmem] * 3,
         out_specs=(vmem,) * 6,
-        scratch_shapes=[pltpu.VMEM((TOK, TOK), jnp.float32)],
-        compiler_params=pltpu.CompilerParams(vmem_limit_bytes=14 * MIB),
+        scratch_shapes=[
+            pltpu.VMEM((TOK, TOK), jnp.float32),
+            pltpu.VMEM((TOK, D), jnp.bfloat16),
+            pltpu.VMEM((TOK, KVH * HD), jnp.bfloat16),
+            pltpu.VMEM((TOK, KVH * HD), jnp.bfloat16),
+            pltpu.SemaphoreType.DMA((3,)),
+        ],
+        compiler_params=pltpu.CompilerParams(vmem_limit_bytes=56 * MIB),
         cost_estimate=pl.CostEstimate(flops=400_000_000, bytes_accessed=6_000_000, transcendentals=660_000),
         name="attention",
     )(info, q0, q1, k0, k1, v0, v1, bias, route, gain)
@@ -253,28 +279,82 @@
     )(*parts)
 
 
-def combine_kernel(pick_ref, attn_ref, r0, r1, r2, r3, out_ref):
-    for n in range(8):
-        c = slice(n * 640, (n + 1) * 640)
+def combine_kernel(code_ref, attn_ref, r0, r1, r2, r3, out_ref):
+    rows_at = lax.broadcasted_iota(jnp.int32, (ROWS, TOK), 0)
+    code = code_ref[...]
+    for q in range(4):
+        c = slice(q * QUARTER, (q + 1) * QUARTER)
         total = attn_ref[:, c].astype(jnp.float32)
         for i, r in enumerate((r0, r1, r2, r3)):
-            total += lax.dot_general(
-                pick_ref[i * 16:i * 16 + CAP], r[:, c], (((0,), (0,)), ((), ())), preferred_element_type=jnp.float32
-            )
+            pick = (rows_at == code - i * ROWS + q * CAP).astype(jnp.bfloat16)
+            total += lax.dot_general(pick, r[...], (((0,), (0,)), ((), ())), preferred_element_type=jnp.float32)
         out_ref[:, c] = total.astype(jnp.bfloat16)
 
 
-def combine(pick, attn, rows):
+def combine(code, attn, rows):
     vmem = pl.BlockSpec(memory_space=pltpu.VMEM)
     return pl.pallas_call(
         combine_kernel,
         out_shape=jax.ShapeDtypeStruct((TOK, D), jnp.bfloat16),
         in_specs=[vmem] * 6,
         out_specs=vmem,
-        compiler_params=pltpu.CompilerParams(vmem_limit_bytes=10 * MIB),
+        compiler_params=pltpu.CompilerParams(vmem_limit_bytes=14 * MIB),
         cost_estimate=pl.CostEstimate(flops=60_000_000, bytes_accessed=3_000_000, transcendentals=0),
         name="combine",
-    )(pick, attn, *rows)
+    )(code, attn, *rows)
+
+
+def same_row(i, q):
+    whole = lax.broadcasted_iota(jnp.int32, (ROWS, ROWS), 0) - i * CAP
+    quarter = lax.broadcasted_iota(jnp.int32, (ROWS, ROWS), 1) - q * CAP
+    return ((whole == quarter) & (whole >= 0) & (whole < CAP)).astype(jnp.bfloat16)
+
+
+def unpack_kernel(p0, p1, p2, p3, out_ref):
+    for q in range(4):
+        total = None
+        for i, p in enumerate((p0, p1, p2, p3)):
+            term = jnp.dot(same_row(i, q), p[...], preferred_element_type=jnp.float32)
+            total = term if total is None else total + term
+        out_ref[:, q * QUARTER:(q + 1) * QUARTER] = total.astype(jnp.bfloat16)
+
+
+def unpack(pieces):
+    vmem = pl.BlockSpec(memory_space=pltpu.VMEM)
+    return pl.pallas_call(
+        unpack_kernel,
+        out_shape=jax.ShapeDtypeStruct((ROWS, D), jnp.bfloat16),
+        in_specs=[vmem] * 4,
+        out_specs=vmem,
+        compiler_params=pltpu.CompilerParams(vmem_limit_bytes=8 * MIB),
+        cost_estimate=pl.CostEstimate(flops=2 * 4 * ROWS * ROWS * D, bytes_accessed=4 * ROWS * D, transcendentals=0),
+        name="unpack",
+    )(*pieces)
+
+
+def add_and_pack_kernel(a, b, c, d, *outs):
+    totals = [None] * 4
+    for q in range(4):
+        at = slice(q * QUARTER, (q + 1) * QUARTER)
+        rows = sum(r[:, at].astype(jnp.float32) for r in (a, b, c, d)).astype(jnp.bfloat16)
+        for i in range(4):
+            term = lax.dot_general(same_row(i, q), rows, (((0,), (0,)), ((), ())), preferred_element_type=jnp.float32)
+            totals[i] = term if totals[i] is None else totals[i] + term
+    for o, total in zip(outs, totals):
+        o[...] = total.astype(jnp.bfloat16)
+
+
+def add_and_pack(parts):
+    vmem = pl.BlockSpec(memory_space=pltpu.VMEM)
+    return pl.pallas_call(
+        add_and_pack_kernel,
+        out_shape=tuple(jax.ShapeDtypeStruct((ROWS, QUARTER), jnp.bfloat16) for _ in range(4)),
+        in_specs=[vmem] * 4,
+        out_specs=(vmem,) * 4,
+        compiler_params=pltpu.CompilerParams(vmem_limit_bytes=8 * MIB),
+        cost_estimate=pl.CostEstimate(flops=2 * 4 * ROWS * ROWS * D, bytes_accessed=10 * ROWS * D, transcendentals=0),
+        name="add_and_pack",
+    )(*parts)
 
 
 def add_up(parts):
@@ -303,21 +383,21 @@
     position = jnp.arange(TOK)
     allowed = (seg[:, None] == seg[None, :]) & (position[:, None] >= position[None, :])
     bias = jnp.where(allowed, jnp.float32(0), jnp.float32(-1e30))
-    attn, pick, *rows = attention(
+    attn, code, *rows = attention(
         info, queries, q1, key_rows, k1, value_rows, v1, bias, expert_ids.reshape(1, TOK), norm_gain.reshape(1, D)
     )
 
     moved = [send(rows[k], to_expert(k)) for k in (1, 2, 3)]
-    mine = jnp.concatenate([rows[0]] + after(moved, g_first), axis=0)
+    mine = unpack([rows[0]] + after(moved, g_first))
     g_rest = lax.dynamic_slice_in_dim(gate_weight, dp * HALF + CUT, HALF - CUT, 0)
-    g_rest = send(after(g_rest, pick), across)
+    g_rest = send(after(g_rest, code), across)
     line = stack([mine] + [send(mine, plane_shift(1, s)) for s in (1, 3, 2)])
     c1, c3, c2 = (send(line, plane_shift(2, s)) for s in (1, 3, 2))
     u_half = lax.dynamic_slice_in_dim(up_weight, dp * HALF, HALF, 0)
     u_half = send(after(u_half, moved), across)
 
     own_gu = (gate_weight, up_weight)
-    g_rest = hold(g_rest, 3*HINT)
+    g_rest = hold(g_rest, 3 * HINT // 2)
     h_line = hidden(info, [after(line, g_rest)], ("own",), own_gu)
     g_first, g_rest, u_half = after((g_first, g_rest, u_half), h_line)
     other_gu = (g_first, g_rest, send(g_first, beside), send(g_rest, beside), u_half, send(u_half, beside))
@@ -338,10 +418,9 @@
     both1 = send(add_up([outs1[1], relay1]), plane_shift(2, 3))
     halves = ((outs0[0], plain0, both0), (outs1[0], plain1, both1))
     back = line_sums(halves)
-    mine_sum = add_up([back[0]] + [send(b, plane_shift(1, s)) for b, s in zip(back[1:], (3, 1, 2))])
-    pieces = [mine_sum[k * CAP:(k + 1) * CAP] for k in range(4)]
+    pieces = add_and_pack([back[0]] + [send(b, plane_shift(1, s)) for b, s in zip(back[1:], (3, 1, 2))])
     returned = [pieces[0]] + [send(pieces[k], reverse(to_expert(k))) for k in (1, 2, 3)]
-    return combine(pick, attn, returned)
+    return combine(code, attn, returned)
 
 
 def solution(mesh):

time: 182 us -> 174 us (0.956)
  waiting for transfers between devices: 84 us -> 77.3 us
  Pallas kernels: 23 us -> 28.6 us
  local copies, waits for them, and re-layouts: 14.2 us -> 8.73 us
    unnamed x38 -> x24, local copies, waits for them, and re-layouts: 11.4 us -> 4.45 us
    ppermute x33, waiting for transfers between devices: 84 us -> 77.3 us  [send(): return lax.ppermute(value, ALL, pairs)]
    pallas_call x1, Pallas kernels: 3.24 us -> 5.87 us  [attention(): pl.pallas_call(attention_kernel, out_shape=(jax.ShapeDtypeStruct((TOK, D)...]
    pallas_call x0 -> x2, Pallas kernels: none -> 2.13 us  [the longest x1 1.41 us: unpack(): pl.pallas_call(unpack_kernel, out_shape=jax.ShapeDtypeStruct((ROWS, D), j...]
  transfers between devices with their start and end apart: 33 -> 33, of which waited for: 19 -> 16; matrix products, arithmetic and copies ran while one was open for 3% -> 4% of each run, Pallas kernels for 9% -> 12%
where the time goes in v2:
time: 174 us
  waiting for transfers between devices  77.3 us (44%)
  starting transfers between devices  55.6 us (32%)
  Pallas kernels  28.6 us (16%)
  local copies, waits for them, and re-layouts  8.73 us (5%)
  other arithmetic  2.49 us (1%)
    ppermute x33, waiting for transfers between devices, send(): return lax.ppermute(value, ALL, pairs)  77.3 us
    ppermute x33, starting transfers between devices, send(): return lax.ppermute(value, ALL, pairs)  55.6 us
    pallas_call x4, Pallas kernels, hidden(): pl.pallas_call(functools.partial(hidden_kernel, count, parts), out_shape=...  11.9 us
    pallas_call x1, Pallas kernels, attention(): pl.pallas_call(attention_kernel, out_shape=(jax.ShapeDtypeStruct((TOK, D)...  5.87 us
    unnamed x24, local copies, waits for them, and re-layouts  4.45 us
    pallas_call x1, Pallas kernels, down(): pl.pallas_call(down_kernel, out_shape=tuple((jax.ShapeDtypeStruct((LINE,...  4.11 us
  transfers between devices with their start and end apart: 33, of which 16 were waited for; matrix products, arithmetic and copies ran while one was open for 4% of the time, Pallas kernels for 12%

profile of v2, /device:TPU:6, one launch (start us, length us, event | category | flops | bytes accessed | tf_op | source)
XLA Modules:
  0.0 173.6 jit_solution(14540175414607966796)
XLA Ops:
  1.7 2.4 %constant_dynamic-slice_fusion.2 = (bf16[1280,256]{1,0:T(8,128)(2,1)}, bf16[1280,256]{1,0:T(8,128)(2,1)}) fusion(bf16[5120,256]{1,0:T(8,128)(2,1)} %refs_1_.3, s32[]{:T(128)S(6)} %select_n.43, s32[]{:T(128)S(6)} %select_n.42), kind=kLoop, calls=%fused_computation.7 | loop fusion | bytes 2621448 | tf_op jit(solution)/shard_map/dynamic_slice | solution.py:392
  10.5 5.9 %attention.1 = (bf16[128,5120]{1,0:T(8,128)(2,1)}, s32[1,128]{1,0:T(1,128)}, bf16[40,1280]{1,0:T(8,128)(2,1)}, bf16[40,1280]{1,0:T(8,128)(2,1)}, bf16[40,1280]{1,0:T(8,128)(2,1)}, /*index=5*/bf16[40,1280]{1,0:T(8,128)(2,1)}) custom-call(s32[4]{0:T(128)} %pad_add_fusion.info, bf16[128,5120]{1,0:T(8,128)(2,1)} %q0.1, bf16[128,5120]{1,0:T(8,128)(2,1)} %copy-done.7, ...), custom_call_target="tpu_custom_call" | custom-call | flops 400000000 | bytes 6000000 | tf_op jit(solution)/shard_map/attention/pallas_call | solution.py:123
  16.4 3.4 %collective-permute-start.4 = (bf16[40,1280]{1,0:T(8,128)(2,1)}, bf16[40,1280]{1,0:T(8,128)(2,1)S(1)}, u32[]{:S(2)}, u32[]{:S(2)}) collective-permute-start(bf16[40,1280]{1,0:T(8,128)(2,1)} %get-tuple-element.43), channel_id=1, source_target_pairs={{0,32},{1,33},{2,34},{3,35},{4,36},{5,37},{6,38},{7,39},{8,40},{9,... | collective-permute-start | bytes 307208 | tf_op jit(solution)/shard_map/ppermute | solution.py:57
  19.7 2.7 %collective-permute-start.5 = (bf16[40,1280]{1,0:T(8,128)(2,1)}, bf16[40,1280]{1,0:T(8,128)(2,1)S(1)}, u32[]{:S(2)}, u32[]{:S(2)}) collective-permute-start(bf16[40,1280]{1,0:T(8,128)(2,1)} %get-tuple-element.44), channel_id=1, source_target_pairs={{0,80},{1,81},{2,82},{3,83},{4,84},{5,85},{6,86},{7,87},{8,88},{9,... | collective-permute-start | bytes 307208 | tf_op jit(solution)/shard_map/ppermute | solution.py:57
  22.4 3.6 %collective-permute-start.6 = (bf16[40,1280]{1,0:T(8,128)(2,1)}, bf16[40,1280]{1,0:T(8,128)(2,1)S(1)}, u32[]{:S(2)}, u32[]{:S(2)}) collective-permute-start(bf16[40,1280]{1,0:T(8,128)(2,1)} %get-tuple-element.45), channel_id=1, source_target_pairs={{0,112},{1,113},{2,114},{3,115},{4,116},{5,117},{6,118},{7,119},{8... | collective-permute-start | bytes 307208 | tf_op jit(solution)/shard_map/ppermute | solution.py:57
  26.0 5.6 %collective-permute-done.4.p1 = bf16[40,1280]{1,0:T(8,128)(2,1)S(1)} collective-permute-done((bf16[40,1280]{1,0:T(8,128)(2,1)}, bf16[40,1280]{1,0:T(8,128)(2,1)S(1)}, u32[]{:S(2)}, u32[]{:S(2)}) %collective-permute-start.4) | collective-permute-done | bytes 102432 | tf_op jit(solution)/shard_map/ppermute | solution.py:57
  40.9 3.7 %collective-permute-done.8.refs_1_ = bf16[40,5120]{1,0:T(8,128)(2,1)} collective-permute-done((bf16[40,5120]{1,0:T(8,128)(2,1)}, bf16[40,5120]{1,0:T(8,128)(2,1)}, u32[]{:S(2)}, u32[]{:S(2)}) %collective-permute-start.8) | collective-permute-done | bytes 409632 | tf_op jit(solution)/shard_map/ppermute | solution.py:57
  44.6 6.1 %collective-permute-done.9.refs_2_ = bf16[40,5120]{1,0:T(8,128)(2,1)} collective-permute-done((bf16[40,5120]{1,0:T(8,128)(2,1)}, bf16[40,5120]{1,0:T(8,128)(2,1)}, u32[]{:S(2)}, u32[]{:S(2)}) %collective-permute-start.9) | collective-permute-done | bytes 409632 | tf_op jit(solution)/shard_map/ppermute | solution.py:57
  60.8 11.3 %collective-permute-done.14.refs_7_ = bf16[2560,256]{1,0:T(8,128)(2,1)} collective-permute-done((bf16[2560,256]{1,0:T(8,128)(2,1)}, bf16[2560,256]{1,0:T(8,128)(2,1)}, u32[]{:S(2)}, u32[]{:S(2)}) %collective-permute-start.14) | collective-permute-done | bytes 1310752 | tf_op jit(solution)/shard_map/ppermute | solution.py:57
  74.9 15.8 %collective-permute-start.16 = (bf16[1280,256]{1,0:T(8,128)(2,1)}, bf16[1280,256]{1,0:T(8,128)(2,1)S(1)}, u32[]{:S(2)}, u32[]{:S(2)}) collective-permute-start(bf16[1280,256]{1,0:T(8,128)(2,1)} %hold.2.refs_4_), channel_id=1, source_target_pairs={{0,128},{1,129},{2,130},{3,131},{4,132},{5,133},{6,134},{7,135},{8... | collective-permute-start | bytes 1966088 | tf_op jit(solution)/shard_map/ppermute | solution.py:57
  90.7 2.5 %hidden.5.h_near = bf16[320,256]{1,0:T(8,128)(2,1)S(1)} custom-call(s32[4]{0:T(128)S(1)} %copy-done.5, bf16[160,5120]{1,0:T(8,128)(2,1)S(1)} %collective-permute-done.12.refs_0_.refs_1_, bf16[160,5120]{1,0:T(8,128)(2,1)S(1)} %collective-permute-done.13.refs_1_.refs_2_, bf16[5120,256]{1,0:T(8,128)(2,1)S(1)} %copy-done, bf16[5120,256]{1,0:T(8,128)(2,1)S(1)} %copy-done.1), custom_call_target="tpu_custom_call" | custom-call | flops 6000000000 | bytes 8519680 | tf_op jit(solution)/shard_map/hidden/pallas_call | solution.py:180
  93.2 4.3 %hidden.6.h_other = bf16[480,256]{1,0:T(8,128)(2,1)S(1)} custom-call(s32[4]{0:T(128)S(1)} %copy-done.5, bf16[160,5120]{1,0:T(8,128)(2,1)S(1)} %stack.17.refs_0_, bf16[160,5120]{1,0:T(8,128)(2,1)S(1)} %collective-permute-done.12.refs_0_.refs_1_, bf16[160,5120]{1,0:T(8,128)(2,1)S(1)} %collective-permute-done.13.refs_1_.refs_2_, ...), custom_call_target="tpu_custom_call" | custom-call | flops 2516582400 | bytes 10158080 | tf_op jit(solution)/shard_map/hidden/pallas_call | solution.py:180
  97.5 6.0 %collective-permute-done.19.value_ref = bf16[128,5120]{1,0:T(8,128)(2,1)S(1)} collective-permute-done((bf16[128,5120]{1,0:T(8,128)(2,1)S(1)}, bf16[128,5120]{1,0:T(8,128)(2,1)S(1)}, u32[]{:S(2)}, u32[]{:S(2)}) %collective-permute-start.19) | collective-permute-done | bytes 1310752 | tf_op jit(solution)/shard_map/ppermute | solution.py:57
  103.5 3.5 %hidden.7.h_last = bf16[160,512]{1,0:T(8,128)(2,1)S(1)} custom-call(s32[4]{0:T(128)S(1)} %copy-done.5, bf16[160,5120]{1,0:T(8,128)(2,1)S(1)} %collective-permute-done.18.refs_0_, bf16[5120,256]{1,0:T(8,128)(2,1)S(1)} %copy-done, bf16[5120,256]{1,0:T(8,128)(2,1)S(1)} %copy-done.1, bf16[1280,256]{1,0:T(8,128)(2,1)S(1)} %collective-permute-done.7.refs_3_, ...), custom_call_target="tpu_custom_call" | custom-call | flops 1677721600 | bytes 12124160 | tf_op jit(solution)/shard_map/hidden/pallas_call | solution.py:180
  107.0 4.1 %down.1 = (bf16[160,2560]{1,0:T(8,128)(2,1)S(1)}, bf16[160,2560]{1,0:T(8,128)(2,1)S(1)}, bf16[160,2560]{1,0:T(8,128)(2,1)S(1)}, bf16[160,2560]{1,0:T(8,128)(2,1)...) custom-call(s32[4]{0:T(128)S(1)} %copy-done.5, ...), custom_call_target="tpu_custom_call" | custom-call | flops 3355443200 | bytes 11796480 | tf_op jit(solution)/shard_map/down/pallas_call | solution.py:211
  112.1 2.6 %collective-permute-start.25 = (bf16[160,2560]{1,0:T(8,128)(2,1)S(1)}, bf16[160,2560]{1,0:T(8,128)(2,1)S(1)}, u32[]{:S(2)}, u32[]{:S(2)}) collective-permute-start(bf16[160,2560]{1,0:T(8,128)(2,1)S(1)} %get-tuple-element.66), channel_id=1, source_target_pairs={{0,12},{1,13},{2,14},{3,15},{4,0},{5,1},{6,2},{7,3},{8,4},{9,5},{1... | collective-permute-start | bytes 2457608 | tf_op jit(solution)/shard_map/ppermute | solution.py:57
  116.7 8.3 %collective-permute-done.22 = bf16[160,2560]{1,0:T(8,128)(2,1)S(1)} collective-permute-done((bf16[160,2560]{1,0:T(8,128)(2,1)S(1)}, bf16[160,2560]{1,0:T(8,128)(2,1)S(1)}, u32[]{:S(2)}, u32[]{:S(2)}) %collective-permute-start.22) | collective-permute-done | bytes 819232 | tf_op jit(solution)/shard_map/ppermute | solution.py:57
  125.5 3.3 %collective-permute-start.26 = (bf16[160,2560]{1,0:T(8,128)(2,1)S(1)}, bf16[160,2560]{1,0:T(8,128)(2,1)S(1)}, u32[]{:S(2)}, u32[]{:S(2)}) collective-permute-start(bf16[160,2560]{1,0:T(8,128)(2,1)S(1)} %add_convert_fusion), channel_id=1, source_target_pairs={{0,12},{1,13},{2,14},{3,15},{4,0},{5,1},{6,2},{7,3},{8,4},{9,5},{1... | collective-permute-start | bytes 2457608 | tf_op jit(solution)/shard_map/ppermute | solution.py:57
  128.8 4.5 %collective-permute-done.21.refs_1_ = bf16[160,2560]{1,0:T(8,128)(2,1)S(1)} collective-permute-done((bf16[160,2560]{1,0:T(8,128)(2,1)S(1)}, bf16[160,2560]{1,0:T(8,128)(2,1)S(1)}, u32[]{:S(2)}, u32[]{:S(2)}) %collective-permute-start.21) | collective-permute-done | bytes 819232 | tf_op jit(solution)/shard_map/ppermute | solution.py:57
  133.7 8.8 %collective-permute-done.23.refs_2_ = bf16[160,2560]{1,0:T(8,128)(2,1)S(1)} collective-permute-done((bf16[160,2560]{1,0:T(8,128)(2,1)S(1)}, bf16[160,2560]{1,0:T(8,128)(2,1)S(1)}, u32[]{:S(2)}, u32[]{:S(2)}) %collective-permute-start.23) | collective-permute-done | bytes 819232 | tf_op jit(solution)/shard_map/ppermute | solution.py:57
  144.0 2.4 %collective-permute-start.28 = (bf16[40,5120]{1,0:T(8,128)(2,1)S(1)}, bf16[40,5120]{1,0:T(8,128)(2,1)S(1)}, u32[]{:S(2)}, u32[]{:S(2)}) collective-permute-start(bf16[40,5120]{1,0:T(8,128)(2,1)S(1)} %get-tuple-element.69), channel_id=1, source_target_pairs={{0,1},{1,2},{2,3},{3,0},{4,5},{5,6},{6,7},{7,4},{8,9},{9,10},{10,1... | collective-permute-start | bytes 1228808 | tf_op jit(solution)/shard_map/ppermute | solution.py:57
  146.6 10.1 %collective-permute-done.27.b = bf16[40,5120]{1,0:T(8,128)(2,1)S(1)} collective-permute-done((bf16[40,5120]{1,0:T(8,128)(2,1)S(1)}, bf16[40,5120]{1,0:T(8,128)(2,1)S(1)}, u32[]{:S(2)}, u32[]{:S(2)}) %collective-permute-start.27) | collective-permute-done | bytes 409632 | tf_op jit(solution)/shard_map/ppermute | solution.py:57
  163.4 5.6 %collective-permute-done.31.r2 = bf16[40,1280]{1,0:T(8,128)(2,1)S(1)} collective-permute-done((bf16[40,1280]{1,0:T(8,128)(2,1)S(1)}, bf16[40,1280]{1,0:T(8,128)(2,1)S(1)}, u32[]{:S(2)}, u32[]{:S(2)}) %collective-permute-start.31) | collective-permute-done | bytes 102432 | tf_op jit(solution)/shard_map/ppermute | solution.py:57
  171.0 2.6 %combine.1 = bf16[128,5120]{1,0:T(8,128)(2,1)} custom-call(s32[1,128]{1,0:T(1,128)S(1)} %copy-done.6, bf16[128,5120]{1,0:T(8,128)(2,1)S(1)} %copy-done.2, bf16[40,1280]{1,0:T(8,128)(2,1)S(1)} %get-tuple-element.71.r0, bf16[40,1280]{1,0:T(8,128)(2,1)S(1)} %collective-permute-done.30.r1, bf16[40,1280]{1,0:T(8,128)(2,1)S(1)} %collective-permute-done.31.r2, ...), custom_call_target="tpu_custom_call" | custom-call | flops 60000000 | bytes 3000000 | tf_op jit(solution)/shard_map/combine/pallas_call | solution.py:296
  (89 shorter events, 43.9 us)
Async XLA Ops:
  4.1 21.9 %collective-permute-start.7 = (bf16[1280,256]{1,0:T(8,128)(2,1)}, bf16[1280,256]{1,0:T(8,128)(2,1)S(1)}, u32[]{:S(2)}, u32[]{:S(2)}) collective-permute-start(bf16[1280,256]{1,0:T(8,128)(2,1)} %get-tuple-element.76), channel_id=1, source_target_pairs={{0,16},{1,17},{2,18},{3,19},{4,20},{5,21},{6,22},{7,23},{8,24},{9,... | collective-permute-start | bytes 1966088 | tf_op jit(solution)/shard_map/ppermute | solution.py:57
  16.4 15.2 %collective-permute-start.4 = (bf16[40,1280]{1,0:T(8,128)(2,1)}, bf16[40,1280]{1,0:T(8,128)(2,1)S(1)}, u32[]{:S(2)}, u32[]{:S(2)}) collective-permute-start(bf16[40,1280]{1,0:T(8,128)(2,1)} %get-tuple-element.43), channel_id=1, source_target_pairs={{0,32},{1,33},{2,34},{3,35},{4,36},{5,37},{6,38},{7,39},{8,40},{9,... | collective-permute-start | bytes 307208 | tf_op jit(solution)/shard_map/ppermute | solution.py:57
  19.7 11.9 %collective-permute-start.5 = (bf16[40,1280]{1,0:T(8,128)(2,1)}, bf16[40,1280]{1,0:T(8,128)(2,1)S(1)}, u32[]{:S(2)}, u32[]{:S(2)}) collective-permute-start(bf16[40,1280]{1,0:T(8,128)(2,1)} %get-tuple-element.44), channel_id=1, source_target_pairs={{0,80},{1,81},{2,82},{3,83},{4,84},{5,85},{6,86},{7,87},{8,88},{9,... | collective-permute-start | bytes 307208 | tf_op jit(solution)/shard_map/ppermute | solution.py:57
  22.4 11.6 %collective-permute-start.6 = (bf16[40,1280]{1,0:T(8,128)(2,1)}, bf16[40,1280]{1,0:T(8,128)(2,1)S(1)}, u32[]{:S(2)}, u32[]{:S(2)}) collective-permute-start(bf16[40,1280]{1,0:T(8,128)(2,1)} %get-tuple-element.45), channel_id=1, source_target_pairs={{0,112},{1,113},{2,114},{3,115},{4,116},{5,117},{6,118},{7,119},{8... | collective-permute-start | bytes 307208 | tf_op jit(solution)/shard_map/ppermute | solution.py:57
  26.0 31.4 %collective-permute-start.11 = (bf16[1280,256]{1,0:T(8,128)(2,1)}, bf16[1280,256]{1,0:T(8,128)(2,1)}, u32[]{:S(2)}, u32[]{:S(2)}) collective-permute-start(bf16[1280,256]{1,0:T(8,128)(2,1)} %get-tuple-element.49), channel_id=1, source_target_pairs={{0,16},{1,17},{2,18},{3,19},{4,20},{5,21},{6,22},{7,23},{8,24},{9,... | collective-permute-start | bytes 1966088 | tf_op jit(solution)/shard_map/ppermute | solution.py:57
  36.8 13.9 %collective-permute-start.9 = (bf16[40,5120]{1,0:T(8,128)(2,1)}, bf16[40,5120]{1,0:T(8,128)(2,1)}, u32[]{:S(2)}, u32[]{:S(2)}) collective-permute-start(bf16[40,5120]{1,0:T(8,128)(2,1)} %unpack.1.refs_0_), channel_id=1, source_target_pairs={{0,3},{1,0},{2,1},{3,2},{4,7},{5,4},{6,5},{7,6},{8,11},{9,8},{10,9... | collective-permute-start | bytes 1228808 | tf_op jit(solution)/shard_map/ppermute | solution.py:57
  38.3 12.3 %collective-permute-start.10 = (bf16[40,5120]{1,0:T(8,128)(2,1)}, bf16[40,5120]{1,0:T(8,128)(2,1)}, u32[]{:S(2)}, u32[]{:S(2)}) collective-permute-start(bf16[40,5120]{1,0:T(8,128)(2,1)} %unpack.1.refs_0_), channel_id=1, source_target_pairs={{0,2},{1,3},{2,0},{3,1},{4,6},{5,7},{6,4},{7,5},{8,10},{9,11},{10,... | collective-permute-start | bytes 1228808 | tf_op jit(solution)/shard_map/ppermute | solution.py:57
  40.9 31.2 %collective-permute-start.14 = (bf16[2560,256]{1,0:T(8,128)(2,1)}, bf16[2560,256]{1,0:T(8,128)(2,1)}, u32[]{:S(2)}, u32[]{:S(2)}) collective-permute-start(bf16[2560,256]{1,0:T(8,128)(2,1)} %constant_dynamic-slice_fusion.1), channel_id=1, source_target_pairs={{0,16},{1,17},{2,18},{3,19},{4,20},{5,21},{6,22},{7,23},{8,24},{9,... | collective-permute-start | bytes 3932168 | tf_op jit(solution)/shard_map/ppermute | solution.py:57
  52.1 22.4 %collective-permute-start.12 = (bf16[160,5120]{1,0:T(8,128)(2,1)S(1)}, bf16[160,5120]{1,0:T(8,128)(2,1)S(1)}, u32[]{:S(2)}, u32[]{:S(2)}) collective-permute-start(bf16[160,5120]{1,0:T(8,128)(2,1)S(1)} %stack.17.refs_0_), channel_id=1, source_target_pairs={{0,4},{1,5},{2,6},{3,7},{4,8},{5,9},{6,10},{7,11},{8,12},{9,13},{1... | collective-permute-start | bytes 4915208 | tf_op jit(solution)/shard_map/ppermute | solution.py:57
  53.8 21.1 %collective-permute-start.13 = (bf16[160,5120]{1,0:T(8,128)(2,1)S(1)}, bf16[160,5120]{1,0:T(8,128)(2,1)S(1)}, u32[]{:S(2)}, u32[]{:S(2)}) collective-permute-start(bf16[160,5120]{1,0:T(8,128)(2,1)S(1)} %stack.17.refs_0_), channel_id=1, source_target_pairs={{0,12},{1,13},{2,14},{3,15},{4,0},{5,1},{6,2},{7,3},{8,4},{9,5},{1... | collective-permute-start | bytes 4915208 | tf_op jit(solution)/shard_map/ppermute | solution.py:57
  55.5 48.0 %collective-permute-start.18 = (bf16[160,5120]{1,0:T(8,128)(2,1)S(1)}, bf16[160,5120]{1,0:T(8,128)(2,1)S(1)}, u32[]{:S(2)}, u32[]{:S(2)}) collective-permute-start(bf16[160,5120]{1,0:T(8,128)(2,1)S(1)} %stack.17.refs_0_), channel_id=1, source_target_pairs={{0,8},{1,9},{2,10},{3,11},{4,12},{5,13},{6,14},{7,15},{8,0},{9,1},... | collective-permute-start | bytes 4915208 | tf_op jit(solution)/shard_map/ppermute | solution.py:57
  72.1 21.1 %collective-permute-start.17 = (bf16[2560,256]{1,0:T(8,128)(2,1)}, bf16[2560,256]{1,0:T(8,128)(2,1)S(1)}, u32[]{:S(2)}, u32[]{:S(2)}) collective-permute-start(bf16[2560,256]{1,0:T(8,128)(2,1)} %collective-permute-done.14.refs_7_), channel_id=1, source_target_pairs={{0,128},{1,129},{2,130},{3,131},{4,132},{5,133},{6,134},{7,135},{8... | collective-permute-start | bytes 3932168 | tf_op jit(solution)/shard_map/ppermute | solution.py:57
  72.2 31.3 %collective-permute-start.19 = (bf16[128,5120]{1,0:T(8,128)(2,1)S(1)}, bf16[128,5120]{1,0:T(8,128)(2,1)S(1)}, u32[]{:S(2)}, u32[]{:S(2)}) collective-permute-start(bf16[128,5120]{1,0:T(8,128)(2,1)S(1)} %constant_dynamic-slice_fusion), channel_id=1, source_target_pairs={{0,16},{1,17},{2,18},{3,19},{4,20},{5,21},{6,22},{7,23},{8,24},{9,... | collective-permute-start | bytes 3932168 | tf_op jit(solution)/shard_map/ppermute | solution.py:57
  74.5 18.6 %collective-permute-start.15 = (bf16[1280,256]{1,0:T(8,128)(2,1)S(1)}, bf16[1280,256]{1,0:T(8,128)(2,1)S(1)}, u32[]{:S(2)}, u32[]{:S(2)}) collective-permute-start(bf16[1280,256]{1,0:T(8,128)(2,1)S(1)} %collective-permute-done.7.refs_3_), channel_id=1, source_target_pairs={{0,128},{1,129},{2,130},{3,131},{4,132},{5,133},{6,134},{7,135},{8... | collective-permute-start | bytes 1966088 | tf_op jit(solution)/shard_map/ppermute | solution.py:57
  74.9 18.3 %collective-permute-start.16 = (bf16[1280,256]{1,0:T(8,128)(2,1)}, bf16[1280,256]{1,0:T(8,128)(2,1)S(1)}, u32[]{:S(2)}, u32[]{:S(2)}) collective-permute-start(bf16[1280,256]{1,0:T(8,128)(2,1)} %hold.2.refs_4_), channel_id=1, source_target_pairs={{0,128},{1,129},{2,130},{3,131},{4,132},{5,133},{6,134},{7,135},{8... | collective-permute-start | bytes 1966088 | tf_op jit(solution)/shard_map/ppermute | solution.py:57
  111.1 13.8 %collective-permute-start.22 = (bf16[160,2560]{1,0:T(8,128)(2,1)S(1)}, bf16[160,2560]{1,0:T(8,128)(2,1)S(1)}, u32[]{:S(2)}, u32[]{:S(2)}) collective-permute-start(bf16[160,2560]{1,0:T(8,128)(2,1)S(1)} %get-tuple-element.62), channel_id=1, source_target_pairs={{0,4},{1,5},{2,6},{3,7},{4,8},{5,9},{6,10},{7,11},{8,12},{9,13},{1... | collective-permute-start | bytes 2457608 | tf_op jit(solution)/shard_map/ppermute | solution.py:57
  112.1 13.2 %collective-permute-start.25 = (bf16[160,2560]{1,0:T(8,128)(2,1)S(1)}, bf16[160,2560]{1,0:T(8,128)(2,1)S(1)}, u32[]{:S(2)}, u32[]{:S(2)}) collective-permute-start(bf16[160,2560]{1,0:T(8,128)(2,1)S(1)} %get-tuple-element.66), channel_id=1, source_target_pairs={{0,12},{1,13},{2,14},{3,15},{4,0},{5,1},{6,2},{7,3},{8,4},{9,5},{1... | collective-permute-start | bytes 2457608 | tf_op jit(solution)/shard_map/ppermute | solution.py:57
  114.7 18.6 %collective-permute-start.21 = (bf16[160,2560]{1,0:T(8,128)(2,1)S(1)}, bf16[160,2560]{1,0:T(8,128)(2,1)S(1)}, u32[]{:S(2)}, u32[]{:S(2)}) collective-permute-start(bf16[160,2560]{1,0:T(8,128)(2,1)S(1)} %get-tuple-element.60), channel_id=1, source_target_pairs={{0,12},{1,13},{2,14},{3,15},{4,0},{5,1},{6,2},{7,3},{8,4},{9,5},{1... | collective-permute-start | bytes 2457608 | tf_op jit(solution)/shard_map/ppermute | solution.py:57
  115.1 18.6 %collective-permute-start.24 = (bf16[160,2560]{1,0:T(8,128)(2,1)S(1)}, bf16[160,2560]{1,0:T(8,128)(2,1)S(1)}, u32[]{:S(2)}, u32[]{:S(2)}) collective-permute-start(bf16[160,2560]{1,0:T(8,128)(2,1)S(1)} %get-tuple-element.64), channel_id=1, source_target_pairs={{0,4},{1,5},{2,6},{3,7},{4,8},{5,9},{6,10},{7,11},{8,12},{9,13},{1... | collective-permute-start | bytes 2457608 | tf_op jit(solution)/shard_map/ppermute | solution.py:57
  125.2 17.3 %collective-permute-start.23 = (bf16[160,2560]{1,0:T(8,128)(2,1)S(1)}, bf16[160,2560]{1,0:T(8,128)(2,1)S(1)}, u32[]{:S(2)}, u32[]{:S(2)}) collective-permute-start(bf16[160,2560]{1,0:T(8,128)(2,1)S(1)} %add_convert_fusion.1), channel_id=1, source_target_pairs={{0,4},{1,5},{2,6},{3,7},{4,8},{5,9},{6,10},{7,11},{8,12},{9,13},{1... | collective-permute-start | bytes 2457608 | tf_op jit(solution)/shard_map/ppermute | solution.py:57
  125.5 17.0 %collective-permute-start.26 = (bf16[160,2560]{1,0:T(8,128)(2,1)S(1)}, bf16[160,2560]{1,0:T(8,128)(2,1)S(1)}, u32[]{:S(2)}, u32[]{:S(2)}) collective-permute-start(bf16[160,2560]{1,0:T(8,128)(2,1)S(1)} %add_convert_fusion), channel_id=1, source_target_pairs={{0,12},{1,13},{2,14},{3,15},{4,0},{5,1},{6,2},{7,3},{8,4},{9,5},{1... | collective-permute-start | bytes 2457608 | tf_op jit(solution)/shard_map/ppermute | solution.py:57
  143.1 13.6 %collective-permute-start.27 = (bf16[40,5120]{1,0:T(8,128)(2,1)S(1)}, bf16[40,5120]{1,0:T(8,128)(2,1)S(1)}, u32[]{:S(2)}, u32[]{:S(2)}) collective-permute-start(bf16[40,5120]{1,0:T(8,128)(2,1)S(1)} %get-tuple-element.68), channel_id=1, source_target_pairs={{0,3},{1,0},{2,1},{3,2},{4,7},{5,4},{6,5},{7,6},{8,11},{9,8},{10,9... | collective-permute-start | bytes 1228808 | tf_op jit(solution)/shard_map/ppermute | solution.py:57
  144.0 12.7 %collective-permute-start.28 = (bf16[40,5120]{1,0:T(8,128)(2,1)S(1)}, bf16[40,5120]{1,0:T(8,128)(2,1)S(1)}, u32[]{:S(2)}, u32[]{:S(2)}) collective-permute-start(bf16[40,5120]{1,0:T(8,128)(2,1)S(1)} %get-tuple-element.69), channel_id=1, source_target_pairs={{0,1},{1,2},{2,3},{3,0},{4,5},{5,6},{6,7},{7,4},{8,9},{9,10},{10,1... | collective-permute-start | bytes 1228808 | tf_op jit(solution)/shard_map/ppermute | solution.py:57
  146.4 10.3 %collective-permute-start.29 = (bf16[40,5120]{1,0:T(8,128)(2,1)S(1)}, bf16[40,5120]{1,0:T(8,128)(2,1)S(1)}, u32[]{:S(2)}, u32[]{:S(2)}) collective-permute-start(bf16[40,5120]{1,0:T(8,128)(2,1)S(1)} %get-tuple-element.70), channel_id=1, source_target_pairs={{0,2},{1,3},{2,0},{3,1},{4,6},{5,7},{6,4},{7,5},{8,10},{9,11},{10,... | collective-permute-start | bytes 1228808 | tf_op jit(solution)/shard_map/ppermute | solution.py:57
  (21 other events, 193.1 us)

commit v3 on v2

--- a/solution.py
+++ b/solution.py
@@ -147,7 +147,7 @@
 
 
 def hidden_kernel(count, parts, info, *refs):
-    xs, srcs, h_ref = refs[:count], list(refs[count:-1]), refs[-1]
+    xs, srcs, h_refs = refs[:count], list(refs[count:-len(parts)]), refs[-len(parts):]
     near = info[3] * HALF
     far = HALF - near
     for i, part in enumerate(parts):
@@ -170,7 +170,7 @@
             gate_term = jnp.dot(x, g[...], preferred_element_type=jnp.float32)
             up_term = jnp.dot(x, u[...], preferred_element_type=jnp.float32)
             gate, up = (gate_term, up_term) if gate is None else (gate + gate_term, up + up_term)
-        h_ref[:, i * FF:(i + 1) * FF] = silu_mul(gate, up)
+        h_refs[i][...] = silu_mul(gate, up)
 
 
 def hidden(info, xs, parts, weights, flops=0):
@@ -179,45 +179,46 @@
     total = count * LINE
     return pl.pallas_call(
         functools.partial(hidden_kernel, count, parts),
-        out_shape=jax.ShapeDtypeStruct((total, n * FF), jnp.bfloat16),
+        out_shape=tuple(jax.ShapeDtypeStruct((total, FF), jnp.bfloat16) for _ in parts),
         in_specs=[pl.BlockSpec(memory_space=pltpu.SMEM)] + [vmem] * (count + len(weights)),
-        out_specs=vmem,
+        out_specs=(vmem,) * n,
         compiler_params=pltpu.CompilerParams(vmem_limit_bytes=18 * MIB),
         cost_estimate=pl.CostEstimate(flops=max(flops, 4 * total * D * n * FF), bytes_accessed=4 * D * n * FF + 2 * total * D, transcendentals=total * n * FF),
         name="hidden",
     )(info, *xs, *weights)
 
 
-def down_kernel(info, h_line, h_near, h_other, h_last, own_w, wa, wb, *outs):
+def down_kernel(n_own, info, *refs):
+    chunks = (len(refs) - 4 - n_own) // 2
+    own_refs, other_ref, (own_w, wa, wb), outs = refs[:n_own], refs[n_own], refs[n_own + 1:n_own + 4], refs[n_own + 4:]
     near = pl.ds(pl.multiple_of(info[3] * (FF // 2), FF // 2), FF // 2)
     far = pl.ds(pl.multiple_of((1 - info[3]) * (FF // 2), FF // 2), FF // 2)
-    own = jnp.concatenate([h_line[...], h_near[...], h_last[:, :FF]], axis=0)
-    last = h_last.at[:, pl.ds(FF, FF)]
-    other = [jnp.concatenate([h_other[:, part], last[:, part]], axis=0) for part in (near, far)]
-    h = jnp.concatenate([own, *other], axis=1)
+    own = jnp.concatenate([r[...] for r in own_refs], axis=0)
+    h = jnp.concatenate([own, other_ref[:, near], other_ref[:, far]], axis=1)
     tile = 512
     for n in range(D // tile):
         cols = pl.ds(n * tile, tile)
         w = jnp.concatenate([own_w[:, cols], wa[:, cols], wb[:, cols]], axis=0)
         y = jnp.dot(h, w, preferred_element_type=jnp.float32).astype(jnp.bfloat16)
         half, at = divmod(n * tile, HALF)
-        for i in range(4):
-            outs[4 * half + i][:, at:at + tile] = y[i * LINE:(i + 1) * LINE]
-
-
-def down(info, hs, own_w, wa, wb):
-    vmem = pl.BlockSpec(memory_space=pltpu.VMEM)
-    total = 4 * LINE
+        for i in range(chunks):
+            outs[chunks * half + i][:, at:at + tile] = y[i * LINE:(i + 1) * LINE]
+
+
+def down(info, own, other, own_w, wa, wb):
+    vmem = pl.BlockSpec(memory_space=pltpu.VMEM)
+    total = other.shape[0]
+    chunks = total // LINE
     outs = pl.pallas_call(
-        down_kernel,
-        out_shape=tuple(jax.ShapeDtypeStruct((LINE, HALF), jnp.bfloat16) for _ in range(8)),
-        in_specs=[pl.BlockSpec(memory_space=pltpu.SMEM)] + [vmem] * (len(hs) + 3),
-        out_specs=(vmem,) * 8,
+        functools.partial(down_kernel, len(own)),
+        out_shape=tuple(jax.ShapeDtypeStruct((LINE, HALF), jnp.bfloat16) for _ in range(2 * chunks)),
+        in_specs=[pl.BlockSpec(memory_space=pltpu.SMEM)] + [vmem] * (len(own) + 4),
+        out_specs=(vmem,) * (2 * chunks),
         compiler_params=pltpu.CompilerParams(vmem_limit_bytes=20 * MIB),
         cost_estimate=pl.CostEstimate(flops=2 * total * 2 * FF * D, bytes_accessed=4 * FF * D + 2 * total * D, transcendentals=0),
         name="down",
-    )(info, *hs, own_w, wa, wb)
-    return outs[:4], outs[4:]
+    )(info, *own, other, own_w, wa, wb)
+    return outs[:chunks], outs[chunks:]
 
 
 def hold(value, flops):
@@ -398,20 +399,21 @@
 
     own_gu = (gate_weight, up_weight)
     g_rest = hold(g_rest, 3 * HINT // 2)
-    h_line = hidden(info, [after(line, g_rest)], ("own",), own_gu)
+    (h_line,) = hidden(info, [after(line, g_rest)], ("own",), own_gu)
     g_first, g_rest, u_half = after((g_first, g_rest, u_half), h_line)
     other_gu = (g_first, g_rest, send(g_first, beside), send(g_rest, beside), u_half, send(u_half, beside))
-    h_near = hidden(info, [c1, c3], ("own",), own_gu, HINT)
+    (h_near,) = hidden(info, [c1, c3], ("own",), own_gu, HINT)
     wa = send(after(lax.dynamic_slice_in_dim(down_weight, dp * (FF // 2), FF // 2, 0), line), across)
-    h_other = hidden(info, [after(line, h_near), c1, c3], ("other",), other_gu)
+    (h_other,) = hidden(info, [after(line, h_near), c1, c3], ("other",), other_gu)
     wa = hold(after(wa, (h_other, c2)), 3*HINT//2)
-    h_last = hidden(info, [after(c2, wa)], ("own", "other"), own_gu + other_gu)
-    hs = (h_line, h_near, h_other, h_last)
-
-    outs0, outs1 = down(info, hs, down_weight, wa, send(wa, beside))
-
-    relay0 = send(outs0[3], plane_shift(2, 1))
-    relay1 = send(outs1[3], plane_shift(2, 3))
+    own_last, other_last = hidden(info, [after(c2, wa)], ("own", "other"), own_gu + other_gu)
+
+    wb = send(wa, beside)
+    (far0,), (far1,) = down(info, [own_last], other_last, down_weight, wa, wb)
+    outs0, outs1 = down(info, [h_line, h_near], h_other, down_weight, wa, after(wb, far0))
+
+    relay0 = send(far0, plane_shift(2, 1))
+    relay1 = send(far1, plane_shift(2, 3))
     plain0 = send(outs0[1], plane_shift(2, 3))
     plain1 = send(outs1[2], plane_shift(2, 1))
     both0 = send(add_up([outs0[2], relay0]), plane_shift(2, 1))

time: 174 us -> 171 us (0.983)
  waiting for transfers between devices: 77.3 us -> 74.1 us
    ppermute x33, waiting for transfers between devices: 77.3 us -> 74.1 us  [send(): return lax.ppermute(value, ALL, pairs)]
    pallas_call x1 -> x2, Pallas kernels: 4.11 us -> 4.82 us  [down(): pl.pallas_call(functools.partial(down_kernel, len(own)), out_shape=tuple(...]
  transfers between devices with their start and end apart: 33 -> 33, of which waited for: 16 -> 16; matrix products, arithmetic and copies ran while one was open for 4% -> 4% of each run, Pallas kernels for 12% -> 14%
where the time goes in v3:
time: 171 us
  waiting for transfers between devices  74.1 us (43%)
  starting transfers between devices  55.4 us (32%)
  Pallas kernels  29.4 us (17%)
  local copies, waits for them, and re-layouts  8.71 us (5%)
  other arithmetic  2.3 us (1%)
    ppermute x33, waiting for transfers between devices, send(): return lax.ppermute(value, ALL, pairs)  74.1 us
    ppermute x33, starting transfers between devices, send(): return lax.ppermute(value, ALL, pairs)  55.4 us
    pallas_call x4, Pallas kernels, hidden(): pl.pallas_call(functools.partial(hidden_kernel, count, parts), out_shape=...  11.9 us
    pallas_call x1, Pallas kernels, attention(): pl.pallas_call(attention_kernel, out_shape=(jax.ShapeDtypeStruct((TOK, D)...  5.88 us
    pallas_call x2, Pallas kernels, down(): pl.pallas_call(functools.partial(down_kernel, len(own)), out_shape=tuple(...  4.82 us
    unnamed x24, local copies, waits for them, and re-layouts  4.45 us
  transfers between devices with their start and end apart: 33, of which 16 were waited for; matrix products, arithmetic and copies ran while one was open for 4% of the time, Pallas kernels for 14%

profile of v3, /device:TPU:6, one launch (start us, length us, event | category | flops | bytes accessed | tf_op | source)
XLA Modules:
  0.0 170.8 jit_solution(18425169772153758416)
XLA Ops:
  1.7 2.4 %constant_dynamic-slice_fusion.2 = (bf16[1280,256]{1,0:T(8,128)(2,1)}, bf16[1280,256]{1,0:T(8,128)(2,1)}) fusion(bf16[5120,256]{1,0:T(8,128)(2,1)} %refs_1_.3, s32[]{:T(128)S(6)} %select_n.43, s32[]{:T(128)S(6)} %select_n.42), kind=kLoop, calls=%fused_computation.7 | loop fusion | bytes 2621448 | tf_op jit(solution)/shard_map/dynamic_slice | solution.py:393
  10.4 5.9 %attention.1 = (bf16[128,5120]{1,0:T(8,128)(2,1)}, s32[1,128]{1,0:T(1,128)}, bf16[40,1280]{1,0:T(8,128)(2,1)}, bf16[40,1280]{1,0:T(8,128)(2,1)}, bf16[40,1280]{1,0:T(8,128)(2,1)}, /*index=5*/bf16[40,1280]{1,0:T(8,128)(2,1)}) custom-call(s32[4]{0:T(128)} %pad_add_fusion.info, bf16[128,5120]{1,0:T(8,128)(2,1)} %q0.1, bf16[128,5120]{1,0:T(8,128)(2,1)} %copy-done.7, ...), custom_call_target="tpu_custom_call" | custom-call | flops 400000000 | bytes 6000000 | tf_op jit(solution)/shard_map/attention/pallas_call | solution.py:123
  16.3 3.4 %collective-permute-start.4 = (bf16[40,1280]{1,0:T(8,128)(2,1)}, bf16[40,1280]{1,0:T(8,128)(2,1)S(1)}, u32[]{:S(2)}, u32[]{:S(2)}) collective-permute-start(bf16[40,1280]{1,0:T(8,128)(2,1)} %get-tuple-element.46), channel_id=1, source_target_pairs={{0,32},{1,33},{2,34},{3,35},{4,36},{5,37},{6,38},{7,39},{8,40},{9,... | collective-permute-start | bytes 307208 | tf_op jit(solution)/shard_map/ppermute | solution.py:57
  19.6 2.7 %collective-permute-start.5 = (bf16[40,1280]{1,0:T(8,128)(2,1)}, bf16[40,1280]{1,0:T(8,128)(2,1)S(1)}, u32[]{:S(2)}, u32[]{:S(2)}) collective-permute-start(bf16[40,1280]{1,0:T(8,128)(2,1)} %get-tuple-element.47), channel_id=1, source_target_pairs={{0,80},{1,81},{2,82},{3,83},{4,84},{5,85},{6,86},{7,87},{8,88},{9,... | collective-permute-start | bytes 307208 | tf_op jit(solution)/shard_map/ppermute | solution.py:57
  22.3 3.6 %collective-permute-start.6 = (bf16[40,1280]{1,0:T(8,128)(2,1)}, bf16[40,1280]{1,0:T(8,128)(2,1)S(1)}, u32[]{:S(2)}, u32[]{:S(2)}) collective-permute-start(bf16[40,1280]{1,0:T(8,128)(2,1)} %get-tuple-element.48), channel_id=1, source_target_pairs={{0,112},{1,113},{2,114},{3,115},{4,116},{5,117},{6,118},{7,119},{8... | collective-permute-start | bytes 307208 | tf_op jit(solution)/shard_map/ppermute | solution.py:57
  25.9 5.7 %collective-permute-done.4.p1 = bf16[40,1280]{1,0:T(8,128)(2,1)S(1)} collective-permute-done((bf16[40,1280]{1,0:T(8,128)(2,1)}, bf16[40,1280]{1,0:T(8,128)(2,1)S(1)}, u32[]{:S(2)}, u32[]{:S(2)}) %collective-permute-start.4) | collective-permute-done | bytes 102432 | tf_op jit(solution)/shard_map/ppermute | solution.py:57
  40.8 3.7 %collective-permute-done.8.refs_1_ = bf16[40,5120]{1,0:T(8,128)(2,1)} collective-permute-done((bf16[40,5120]{1,0:T(8,128)(2,1)}, bf16[40,5120]{1,0:T(8,128)(2,1)}, u32[]{:S(2)}, u32[]{:S(2)}) %collective-permute-start.8) | collective-permute-done | bytes 409632 | tf_op jit(solution)/shard_map/ppermute | solution.py:57
  44.5 6.1 %collective-permute-done.9.refs_2_ = bf16[40,5120]{1,0:T(8,128)(2,1)} collective-permute-done((bf16[40,5120]{1,0:T(8,128)(2,1)}, bf16[40,5120]{1,0:T(8,128)(2,1)}, u32[]{:S(2)}, u32[]{:S(2)}) %collective-permute-start.9) | collective-permute-done | bytes 409632 | tf_op jit(solution)/shard_map/ppermute | solution.py:57
  60.7 11.3 %collective-permute-done.14.refs_7_ = bf16[2560,256]{1,0:T(8,128)(2,1)} collective-permute-done((bf16[2560,256]{1,0:T(8,128)(2,1)}, bf16[2560,256]{1,0:T(8,128)(2,1)}, u32[]{:S(2)}, u32[]{:S(2)}) %collective-permute-start.14) | collective-permute-done | bytes 1310752 | tf_op jit(solution)/shard_map/ppermute | solution.py:57
  74.8 15.8 %collective-permute-start.16 = (bf16[1280,256]{1,0:T(8,128)(2,1)}, bf16[1280,256]{1,0:T(8,128)(2,1)S(1)}, u32[]{:S(2)}, u32[]{:S(2)}) collective-permute-start(bf16[1280,256]{1,0:T(8,128)(2,1)} %hold.2.refs_4_), channel_id=1, source_target_pairs={{0,128},{1,129},{2,130},{3,131},{4,132},{5,133},{6,134},{7,135},{8... | collective-permute-start | bytes 1966088 | tf_op jit(solution)/shard_map/ppermute | solution.py:57
  90.6 2.5 %hidden.5.refs_1_ = bf16[320,256]{1,0:T(8,128)(2,1)S(1)} custom-call(s32[4]{0:T(128)S(1)} %copy-done.5, bf16[160,5120]{1,0:T(8,128)(2,1)S(1)} %collective-permute-done.12.refs_0_.refs_1_, bf16[160,5120]{1,0:T(8,128)(2,1)S(1)} %collective-permute-done.13.refs_1_.refs_2_, bf16[5120,256]{1,0:T(8,128)(2,1)S(1)} %copy-done, bf16[5120,256]{1,0:T(8,128)(2,1)S(1)} %copy-done.1), custom_call_target="tpu_custom_call" | custom-call | flops 6000000000 | bytes 8519680 | tf_op jit(solution)/shard_map/hidden/pallas_call | solution.py:180
  93.1 4.3 %hidden.6.refs_2_ = bf16[480,256]{1,0:T(8,128)(2,1)S(1)} custom-call(s32[4]{0:T(128)S(1)} %copy-done.5, bf16[160,5120]{1,0:T(8,128)(2,1)S(1)} %stack.17.refs_0_, bf16[160,5120]{1,0:T(8,128)(2,1)S(1)} %collective-permute-done.12.refs_0_.refs_1_, bf16[160,5120]{1,0:T(8,128)(2,1)S(1)} %collective-permute-done.13.refs_1_.refs_2_, ...), custom_call_target="tpu_custom_call" | custom-call | flops 2516582400 | bytes 10158080 | tf_op jit(solution)/shard_map/hidden/pallas_call | solution.py:180
  97.4 6.0 %collective-permute-done.18.value_ref = bf16[128,5120]{1,0:T(8,128)(2,1)S(1)} collective-permute-done((bf16[128,5120]{1,0:T(8,128)(2,1)S(1)}, bf16[128,5120]{1,0:T(8,128)(2,1)S(1)}, u32[]{:S(2)}, u32[]{:S(2)}) %collective-permute-start.18) | collective-permute-done | bytes 1310752 | tf_op jit(solution)/shard_map/ppermute | solution.py:57
  103.4 3.5 %hidden.7 = (bf16[160,256]{1,0:T(8,128)(2,1)S(1)}, bf16[160,256]{1,0:T(8,128)(2,1)S(1)}) custom-call(s32[4]{0:T(128)S(1)} %copy-done.5, bf16[160,5120]{1,0:T(8,128)(2,1)S(1)} %collective-permute-done.19.refs_0_, bf16[5120,256]{1,0:T(8,128)(2,1)S(1)} %copy-done, bf16[5120,256]{1,0:T(8,128)(2,1)S(1)} %copy-done.1, ...), custom_call_target="tpu_custom_call" | custom-call | flops 1677721600 | bytes 12124160 | tf_op jit(solution)/shard_map/hidden/pallas_call | solution.py:180
  109.2 2.6 %collective-permute-start.25 = (bf16[160,2560]{1,0:T(8,128)(2,1)S(1)}, bf16[160,2560]{1,0:T(8,128)(2,1)S(1)}, u32[]{:S(2)}, u32[]{:S(2)}) collective-permute-start(bf16[160,2560]{1,0:T(8,128)(2,1)S(1)} %get-tuple-element.72), channel_id=1, source_target_pairs={{0,12},{1,13},{2,14},{3,15},{4,0},{5,1},{6,2},{7,3},{8,4},{9,5},{1... | collective-permute-start | bytes 2457608 | tf_op jit(solution)/shard_map/ppermute | solution.py:57
  111.8 3.3 %down.3 = (bf16[160,2560]{1,0:T(8,128)(2,1)S(1)}, bf16[160,2560]{1,0:T(8,128)(2,1)S(1)}, bf16[160,2560]{1,0:T(8,128)(2,1)S(1)}, bf16[160,2560]{1,0:T(8,128)(2,1)...) custom-call(s32[4]{0:T(128)S(1)} %copy-done.5, bf16[160,256]{1,0:T(8,128)(2,1)S(1)} %hidden.4.refs_0_, ...), custom_call_target="tpu_custom_call" | custom-call | flops 2516582400 | bytes 10158080 | tf_op jit(solution)/shard_map/down/pallas_call | solution.py:212
  117.1 4.9 %collective-permute-done.22 = bf16[160,2560]{1,0:T(8,128)(2,1)S(1)} collective-permute-done((bf16[160,2560]{1,0:T(8,128)(2,1)S(1)}, bf16[160,2560]{1,0:T(8,128)(2,1)S(1)}, u32[]{:S(2)}, u32[]{:S(2)}) %collective-permute-start.22) | collective-permute-done | bytes 819232 | tf_op jit(solution)/shard_map/ppermute | solution.py:57
  122.6 3.3 %collective-permute-start.26 = (bf16[160,2560]{1,0:T(8,128)(2,1)S(1)}, bf16[160,2560]{1,0:T(8,128)(2,1)S(1)}, u32[]{:S(2)}, u32[]{:S(2)}) collective-permute-start(bf16[160,2560]{1,0:T(8,128)(2,1)S(1)} %add_convert_fusion), channel_id=1, source_target_pairs={{0,12},{1,13},{2,14},{3,15},{4,0},{5,1},{6,2},{7,3},{8,4},{9,5},{1... | collective-permute-start | bytes 2457608 | tf_op jit(solution)/shard_map/ppermute | solution.py:57
  125.9 4.5 %collective-permute-done.21.refs_1_ = bf16[160,2560]{1,0:T(8,128)(2,1)S(1)} collective-permute-done((bf16[160,2560]{1,0:T(8,128)(2,1)S(1)}, bf16[160,2560]{1,0:T(8,128)(2,1)S(1)}, u32[]{:S(2)}, u32[]{:S(2)}) %collective-permute-start.21) | collective-permute-done | bytes 819232 | tf_op jit(solution)/shard_map/ppermute | solution.py:57
  130.9 8.8 %collective-permute-done.23.refs_2_ = bf16[160,2560]{1,0:T(8,128)(2,1)S(1)} collective-permute-done((bf16[160,2560]{1,0:T(8,128)(2,1)S(1)}, bf16[160,2560]{1,0:T(8,128)(2,1)S(1)}, u32[]{:S(2)}, u32[]{:S(2)}) %collective-permute-start.23) | collective-permute-done | bytes 819232 | tf_op jit(solution)/shard_map/ppermute | solution.py:57
  143.8 10.1 %collective-permute-done.27.b = bf16[40,5120]{1,0:T(8,128)(2,1)S(1)} collective-permute-done((bf16[40,5120]{1,0:T(8,128)(2,1)S(1)}, bf16[40,5120]{1,0:T(8,128)(2,1)S(1)}, u32[]{:S(2)}, u32[]{:S(2)}) %collective-permute-start.27) | collective-permute-done | bytes 409632 | tf_op jit(solution)/shard_map/ppermute | solution.py:57
  154.6 2.4 %collective-permute-start.30 = (bf16[40,1280]{1,0:T(8,128)(2,1)S(1)}, bf16[40,1280]{1,0:T(8,128)(2,1)S(1)}, u32[]{:S(2)}, u32[]{:S(2)}) collective-permute-start(bf16[40,1280]{1,0:T(8,128)(2,1)S(1)} %get-tuple-element.78), channel_id=1, source_target_pairs={{32,0},{33,1},{34,2},{35,3},{36,4},{37,5},{38,6},{39,7},{40,8},{41... | collective-permute-start | bytes 307208 | tf_op jit(solution)/shard_map/ppermute | solution.py:57
  160.5 5.7 %collective-permute-done.31.r2 = bf16[40,1280]{1,0:T(8,128)(2,1)S(1)} collective-permute-done((bf16[40,1280]{1,0:T(8,128)(2,1)S(1)}, bf16[40,1280]{1,0:T(8,128)(2,1)S(1)}, u32[]{:S(2)}, u32[]{:S(2)}) %collective-permute-start.31) | collective-permute-done | bytes 102432 | tf_op jit(solution)/shard_map/ppermute | solution.py:57
  168.2 2.6 %combine.1 = bf16[128,5120]{1,0:T(8,128)(2,1)} custom-call(s32[1,128]{1,0:T(1,128)S(1)} %copy-done.6, bf16[128,5120]{1,0:T(8,128)(2,1)S(1)} %copy-done.3, bf16[40,1280]{1,0:T(8,128)(2,1)S(1)} %get-tuple-element.77.r0, bf16[40,1280]{1,0:T(8,128)(2,1)S(1)} %collective-permute-done.30.r1, bf16[40,1280]{1,0:T(8,128)(2,1)S(1)} %collective-permute-done.31.r2, ...), custom_call_target="tpu_custom_call" | custom-call | flops 60000000 | bytes 3000000 | tf_op jit(solution)/shard_map/combine/pallas_call | solution.py:297
  (90 shorter events, 45.0 us)
Async XLA Ops:
  4.1 21.8 %collective-permute-start.7 = (bf16[1280,256]{1,0:T(8,128)(2,1)}, bf16[1280,256]{1,0:T(8,128)(2,1)S(1)}, u32[]{:S(2)}, u32[]{:S(2)}) collective-permute-start(bf16[1280,256]{1,0:T(8,128)(2,1)} %get-tuple-element.82), channel_id=1, source_target_pairs={{0,16},{1,17},{2,18},{3,19},{4,20},{5,21},{6,22},{7,23},{8,24},{9,... | collective-permute-start | bytes 1966088 | tf_op jit(solution)/shard_map/ppermute | solution.py:57
  16.3 15.3 %collective-permute-start.4 = (bf16[40,1280]{1,0:T(8,128)(2,1)}, bf16[40,1280]{1,0:T(8,128)(2,1)S(1)}, u32[]{:S(2)}, u32[]{:S(2)}) collective-permute-start(bf16[40,1280]{1,0:T(8,128)(2,1)} %get-tuple-element.46), channel_id=1, source_target_pairs={{0,32},{1,33},{2,34},{3,35},{4,36},{5,37},{6,38},{7,39},{8,40},{9,... | collective-permute-start | bytes 307208 | tf_op jit(solution)/shard_map/ppermute | solution.py:57
  19.6 12.0 %collective-permute-start.5 = (bf16[40,1280]{1,0:T(8,128)(2,1)}, bf16[40,1280]{1,0:T(8,128)(2,1)S(1)}, u32[]{:S(2)}, u32[]{:S(2)}) collective-permute-start(bf16[40,1280]{1,0:T(8,128)(2,1)} %get-tuple-element.47), channel_id=1, source_target_pairs={{0,80},{1,81},{2,82},{3,83},{4,84},{5,85},{6,86},{7,87},{8,88},{9,... | collective-permute-start | bytes 307208 | tf_op jit(solution)/shard_map/ppermute | solution.py:57
  22.3 11.6 %collective-permute-start.6 = (bf16[40,1280]{1,0:T(8,128)(2,1)}, bf16[40,1280]{1,0:T(8,128)(2,1)S(1)}, u32[]{:S(2)}, u32[]{:S(2)}) collective-permute-start(bf16[40,1280]{1,0:T(8,128)(2,1)} %get-tuple-element.48), channel_id=1, source_target_pairs={{0,112},{1,113},{2,114},{3,115},{4,116},{5,117},{6,118},{7,119},{8... | collective-permute-start | bytes 307208 | tf_op jit(solution)/shard_map/ppermute | solution.py:57
  25.9 31.5 %collective-permute-start.11 = (bf16[1280,256]{1,0:T(8,128)(2,1)}, bf16[1280,256]{1,0:T(8,128)(2,1)}, u32[]{:S(2)}, u32[]{:S(2)}) collective-permute-start(bf16[1280,256]{1,0:T(8,128)(2,1)} %get-tuple-element.52), channel_id=1, source_target_pairs={{0,16},{1,17},{2,18},{3,19},{4,20},{5,21},{6,22},{7,23},{8,24},{9,... | collective-permute-start | bytes 1966088 | tf_op jit(solution)/shard_map/ppermute | solution.py:57
  36.7 13.9 %collective-permute-start.9 = (bf16[40,5120]{1,0:T(8,128)(2,1)}, bf16[40,5120]{1,0:T(8,128)(2,1)}, u32[]{:S(2)}, u32[]{:S(2)}) collective-permute-start(bf16[40,5120]{1,0:T(8,128)(2,1)} %unpack.1.refs_0_), channel_id=1, source_target_pairs={{0,3},{1,0},{2,1},{3,2},{4,7},{5,4},{6,5},{7,6},{8,11},{9,8},{10,9... | collective-permute-start | bytes 1228808 | tf_op jit(solution)/shard_map/ppermute | solution.py:57
  38.2 12.3 %collective-permute-start.10 = (bf16[40,5120]{1,0:T(8,128)(2,1)}, bf16[40,5120]{1,0:T(8,128)(2,1)}, u32[]{:S(2)}, u32[]{:S(2)}) collective-permute-start(bf16[40,5120]{1,0:T(8,128)(2,1)} %unpack.1.refs_0_), channel_id=1, source_target_pairs={{0,2},{1,3},{2,0},{3,1},{4,6},{5,7},{6,4},{7,5},{8,10},{9,11},{10,... | collective-permute-start | bytes 1228808 | tf_op jit(solution)/shard_map/ppermute | solution.py:57
  40.8 31.2 %collective-permute-start.14 = (bf16[2560,256]{1,0:T(8,128)(2,1)}, bf16[2560,256]{1,0:T(8,128)(2,1)}, u32[]{:S(2)}, u32[]{:S(2)}) collective-permute-start(bf16[2560,256]{1,0:T(8,128)(2,1)} %constant_dynamic-slice_fusion.1), channel_id=1, source_target_pairs={{0,16},{1,17},{2,18},{3,19},{4,20},{5,21},{6,22},{7,23},{8,24},{9,... | collective-permute-start | bytes 3932168 | tf_op jit(solution)/shard_map/ppermute | solution.py:57
  52.1 22.4 %collective-permute-start.12 = (bf16[160,5120]{1,0:T(8,128)(2,1)S(1)}, bf16[160,5120]{1,0:T(8,128)(2,1)S(1)}, u32[]{:S(2)}, u32[]{:S(2)}) collective-permute-start(bf16[160,5120]{1,0:T(8,128)(2,1)S(1)} %stack.17.refs_0_), channel_id=1, source_target_pairs={{0,4},{1,5},{2,6},{3,7},{4,8},{5,9},{6,10},{7,11},{8,12},{9,13},{1... | collective-permute-start | bytes 4915208 | tf_op jit(solution)/shard_map/ppermute | solution.py:57
  53.7 21.1 %collective-permute-start.13 = (bf16[160,5120]{1,0:T(8,128)(2,1)S(1)}, bf16[160,5120]{1,0:T(8,128)(2,1)S(1)}, u32[]{:S(2)}, u32[]{:S(2)}) collective-permute-start(bf16[160,5120]{1,0:T(8,128)(2,1)S(1)} %stack.17.refs_0_), channel_id=1, source_target_pairs={{0,12},{1,13},{2,14},{3,15},{4,0},{5,1},{6,2},{7,3},{8,4},{9,5},{1... | collective-permute-start | bytes 4915208 | tf_op jit(solution)/shard_map/ppermute | solution.py:57
  55.4 47.9 %collective-permute-start.19 = (bf16[160,5120]{1,0:T(8,128)(2,1)S(1)}, bf16[160,5120]{1,0:T(8,128)(2,1)S(1)}, u32[]{:S(2)}, u32[]{:S(2)}) collective-permute-start(bf16[160,5120]{1,0:T(8,128)(2,1)S(1)} %stack.17.refs_0_), channel_id=1, source_target_pairs={{0,8},{1,9},{2,10},{3,11},{4,12},{5,13},{6,14},{7,15},{8,0},{9,1},... | collective-permute-start | bytes 4915208 | tf_op jit(solution)/shard_map/ppermute | solution.py:57
  72.0 21.1 %collective-permute-start.17 = (bf16[2560,256]{1,0:T(8,128)(2,1)}, bf16[2560,256]{1,0:T(8,128)(2,1)S(1)}, u32[]{:S(2)}, u32[]{:S(2)}) collective-permute-start(bf16[2560,256]{1,0:T(8,128)(2,1)} %collective-permute-done.14.refs_7_), channel_id=1, source_target_pairs={{0,128},{1,129},{2,130},{3,131},{4,132},{5,133},{6,134},{7,135},{8... | collective-permute-start | bytes 3932168 | tf_op jit(solution)/shard_map/ppermute | solution.py:57
  72.1 31.3 %collective-permute-start.18 = (bf16[128,5120]{1,0:T(8,128)(2,1)S(1)}, bf16[128,5120]{1,0:T(8,128)(2,1)S(1)}, u32[]{:S(2)}, u32[]{:S(2)}) collective-permute-start(bf16[128,5120]{1,0:T(8,128)(2,1)S(1)} %constant_dynamic-slice_fusion), channel_id=1, source_target_pairs={{0,16},{1,17},{2,18},{3,19},{4,20},{5,21},{6,22},{7,23},{8,24},{9,... | collective-permute-start | bytes 3932168 | tf_op jit(solution)/shard_map/ppermute | solution.py:57
  74.5 18.6 %collective-permute-start.15 = (bf16[1280,256]{1,0:T(8,128)(2,1)S(1)}, bf16[1280,256]{1,0:T(8,128)(2,1)S(1)}, u32[]{:S(2)}, u32[]{:S(2)}) collective-permute-start(bf16[1280,256]{1,0:T(8,128)(2,1)S(1)} %collective-permute-done.7.refs_3_), channel_id=1, source_target_pairs={{0,128},{1,129},{2,130},{3,131},{4,132},{5,133},{6,134},{7,135},{8... | collective-permute-start | bytes 1966088 | tf_op jit(solution)/shard_map/ppermute | solution.py:57
  74.8 18.3 %collective-permute-start.16 = (bf16[1280,256]{1,0:T(8,128)(2,1)}, bf16[1280,256]{1,0:T(8,128)(2,1)S(1)}, u32[]{:S(2)}, u32[]{:S(2)}) collective-permute-start(bf16[1280,256]{1,0:T(8,128)(2,1)} %hold.2.refs_4_), channel_id=1, source_target_pairs={{0,128},{1,129},{2,130},{3,131},{4,132},{5,133},{6,134},{7,135},{8... | collective-permute-start | bytes 1966088 | tf_op jit(solution)/shard_map/ppermute | solution.py:57
  108.4 13.6 %collective-permute-start.22 = (bf16[160,2560]{1,0:T(8,128)(2,1)S(1)}, bf16[160,2560]{1,0:T(8,128)(2,1)S(1)}, u32[]{:S(2)}, u32[]{:S(2)}) collective-permute-start(bf16[160,2560]{1,0:T(8,128)(2,1)S(1)} %get-tuple-element.64), channel_id=1, source_target_pairs={{0,4},{1,5},{2,6},{3,7},{4,8},{5,9},{6,10},{7,11},{8,12},{9,13},{1... | collective-permute-start | bytes 2457608 | tf_op jit(solution)/shard_map/ppermute | solution.py:57
  109.2 13.2 %collective-permute-start.25 = (bf16[160,2560]{1,0:T(8,128)(2,1)S(1)}, bf16[160,2560]{1,0:T(8,128)(2,1)S(1)}, u32[]{:S(2)}, u32[]{:S(2)}) collective-permute-start(bf16[160,2560]{1,0:T(8,128)(2,1)S(1)} %get-tuple-element.72), channel_id=1, source_target_pairs={{0,12},{1,13},{2,14},{3,15},{4,0},{5,1},{6,2},{7,3},{8,4},{9,5},{1... | collective-permute-start | bytes 2457608 | tf_op jit(solution)/shard_map/ppermute | solution.py:57
  115.0 15.4 %collective-permute-start.21 = (bf16[160,2560]{1,0:T(8,128)(2,1)S(1)}, bf16[160,2560]{1,0:T(8,128)(2,1)S(1)}, u32[]{:S(2)}, u32[]{:S(2)}) collective-permute-start(bf16[160,2560]{1,0:T(8,128)(2,1)S(1)} %get-tuple-element.67), channel_id=1, source_target_pairs={{0,12},{1,13},{2,14},{3,15},{4,0},{5,1},{6,2},{7,3},{8,4},{9,5},{1... | collective-permute-start | bytes 2457608 | tf_op jit(solution)/shard_map/ppermute | solution.py:57
  115.6 15.3 %collective-permute-start.24 = (bf16[160,2560]{1,0:T(8,128)(2,1)S(1)}, bf16[160,2560]{1,0:T(8,128)(2,1)S(1)}, u32[]{:S(2)}, u32[]{:S(2)}) collective-permute-start(bf16[160,2560]{1,0:T(8,128)(2,1)S(1)} %get-tuple-element.70), channel_id=1, source_target_pairs={{0,4},{1,5},{2,6},{3,7},{4,8},{5,9},{6,10},{7,11},{8,12},{9,13},{1... | collective-permute-start | bytes 2457608 | tf_op jit(solution)/shard_map/ppermute | solution.py:57
  122.3 17.4 %collective-permute-start.23 = (bf16[160,2560]{1,0:T(8,128)(2,1)S(1)}, bf16[160,2560]{1,0:T(8,128)(2,1)S(1)}, u32[]{:S(2)}, u32[]{:S(2)}) collective-permute-start(bf16[160,2560]{1,0:T(8,128)(2,1)S(1)} %add_convert_fusion.1), channel_id=1, source_target_pairs={{0,4},{1,5},{2,6},{3,7},{4,8},{5,9},{6,10},{7,11},{8,12},{9,13},{1... | collective-permute-start | bytes 2457608 | tf_op jit(solution)/shard_map/ppermute | solution.py:57
  122.6 17.1 %collective-permute-start.26 = (bf16[160,2560]{1,0:T(8,128)(2,1)S(1)}, bf16[160,2560]{1,0:T(8,128)(2,1)S(1)}, u32[]{:S(2)}, u32[]{:S(2)}) collective-permute-start(bf16[160,2560]{1,0:T(8,128)(2,1)S(1)} %add_convert_fusion), channel_id=1, source_target_pairs={{0,12},{1,13},{2,14},{3,15},{4,0},{5,1},{6,2},{7,3},{8,4},{9,5},{1... | collective-permute-start | bytes 2457608 | tf_op jit(solution)/shard_map/ppermute | solution.py:57
  140.2 13.6 %collective-permute-start.27 = (bf16[40,5120]{1,0:T(8,128)(2,1)S(1)}, bf16[40,5120]{1,0:T(8,128)(2,1)S(1)}, u32[]{:S(2)}, u32[]{:S(2)}) collective-permute-start(bf16[40,5120]{1,0:T(8,128)(2,1)S(1)} %get-tuple-element.74), channel_id=1, source_target_pairs={{0,3},{1,0},{2,1},{3,2},{4,7},{5,4},{6,5},{7,6},{8,11},{9,8},{10,9... | collective-permute-start | bytes 1228808 | tf_op jit(solution)/shard_map/ppermute | solution.py:57
  141.2 12.7 %collective-permute-start.28 = (bf16[40,5120]{1,0:T(8,128)(2,1)S(1)}, bf16[40,5120]{1,0:T(8,128)(2,1)S(1)}, u32[]{:S(2)}, u32[]{:S(2)}) collective-permute-start(bf16[40,5120]{1,0:T(8,128)(2,1)S(1)} %get-tuple-element.75), channel_id=1, source_target_pairs={{0,1},{1,2},{2,3},{3,0},{4,5},{5,6},{6,7},{7,4},{8,9},{9,10},{10,1... | collective-permute-start | bytes 1228808 | tf_op jit(solution)/shard_map/ppermute | solution.py:57
  143.6 10.3 %collective-permute-start.29 = (bf16[40,5120]{1,0:T(8,128)(2,1)S(1)}, bf16[40,5120]{1,0:T(8,128)(2,1)S(1)}, u32[]{:S(2)}, u32[]{:S(2)}) collective-permute-start(bf16[40,5120]{1,0:T(8,128)(2,1)S(1)} %get-tuple-element.76), channel_id=1, source_target_pairs={{0,2},{1,3},{2,0},{3,1},{4,6},{5,7},{6,4},{7,5},{8,10},{9,11},{10,... | collective-permute-start | bytes 1228808 | tf_op jit(solution)/shard_map/ppermute | solution.py:57
  (21 other events, 192.6 us)

commit v4 on v3

--- a/solution.py
+++ b/solution.py
@@ -390,7 +390,7 @@
 
     moved = [send(rows[k], to_expert(k)) for k in (1, 2, 3)]
     mine = unpack([rows[0]] + after(moved, g_first))
-    g_rest = lax.dynamic_slice_in_dim(gate_weight, dp * HALF + CUT, HALF - CUT, 0)
+    g_rest = lax.dynamic_slice_in_dim(gate_weight, after(dp, k1) * HALF + CUT, HALF - CUT, 0)
     g_rest = send(after(g_rest, code), across)
     line = stack([mine] + [send(mine, plane_shift(1, s)) for s in (1, 3, 2)])
     c1, c3, c2 = (send(line, plane_shift(2, s)) for s in (1, 3, 2))

time: 171 us -> 173 us (1.012)
  no operation moved by 1% of the time
where the time goes in v4:
time: 173 us; the launch traced here: 172 us
  waiting for transfers between devices  74.9 us (43%)
  starting transfers between devices  56.1 us (32%)
  Pallas kernels  29.4 us (17%)
  local copies, waits for them, and re-layouts  8.55 us (5%)
  other arithmetic  2.3 us (1%)
    ppermute x33, waiting for transfers between devices, send(): return lax.ppermute(value, ALL, pairs)  74.9 us
    ppermute x33, starting transfers between devices, send(): return lax.ppermute(value, ALL, pairs)  56.1 us
    pallas_call x4, Pallas kernels, hidden(): pl.pallas_call(functools.partial(hidden_kernel, count, parts), out_shape=...  11.9 us
    pallas_call x1, Pallas kernels, attention(): pl.pallas_call(attention_kernel, out_shape=(jax.ShapeDtypeStruct((TOK, D)...  5.87 us
    pallas_call x2, Pallas kernels, down(): pl.pallas_call(functools.partial(down_kernel, len(own)), out_shape=tuple(...  4.82 us
    unnamed x24, local copies, waits for them, and re-layouts  4.41 us
  transfers between devices with their start and end apart: 33, of which 16 were waited for; matrix products, arithmetic and copies ran while one was open for 4% of the time, Pallas kernels for 14%

profile of v4, /device:TPU:6, one launch (start us, length us, event | category | flops | bytes accessed | tf_op | source)
XLA Modules:
  0.0 172.1 jit_solution(1762690214599261792)
XLA Ops:
  3.6 2.3 %constant_dynamic-slice_fusion.2 = (bf16[1280,256]{1,0:T(8,128)(2,1)}, bf16[1280,256]{1,0:T(8,128)(2,1)S(1)}) fusion(bf16[5120,256]{1,0:T(8,128)(2,1)} %refs_1_.3, s32[]{:T(128)S(6)} %select_n.43, s32[]{:T(128)S(6)} %select_n.42), kind=kLoop, calls=%fused_computation.7 | loop fusion | bytes 2621448 | tf_op jit(solution)/shard_map/dynamic_slice | solution.py:393
  11.5 5.9 %attention.1 = (bf16[128,5120]{1,0:T(8,128)(2,1)}, s32[1,128]{1,0:T(1,128)}, bf16[40,1280]{1,0:T(8,128)(2,1)}, bf16[40,1280]{1,0:T(8,128)(2,1)}, bf16[40,1280]{1,0:T(8,128)(2,1)}, /*index=5*/bf16[40,1280]{1,0:T(8,128)(2,1)}) custom-call(s32[4]{0:T(128)} %pad_add_fusion.info, bf16[128,5120]{1,0:T(8,128)(2,1)} %q0.1, bf16[128,5120]{1,0:T(8,128)(2,1)} %copy-done.7, ...), custom_call_target="tpu_custom_call" | custom-call | flops 400000000 | bytes 6000000 | tf_op jit(solution)/shard_map/attention/pallas_call | solution.py:123
  17.4 3.4 %collective-permute-start.4 = (bf16[40,1280]{1,0:T(8,128)(2,1)}, bf16[40,1280]{1,0:T(8,128)(2,1)S(1)}, u32[]{:S(2)}, u32[]{:S(2)}) collective-permute-start(bf16[40,1280]{1,0:T(8,128)(2,1)} %get-tuple-element.47), channel_id=1, source_target_pairs={{0,32},{1,33},{2,34},{3,35},{4,36},{5,37},{6,38},{7,39},{8,40},{9,... | collective-permute-start | bytes 307208 | tf_op jit(solution)/shard_map/ppermute | solution.py:57
  20.7 2.7 %collective-permute-start.5 = (bf16[40,1280]{1,0:T(8,128)(2,1)}, bf16[40,1280]{1,0:T(8,128)(2,1)S(1)}, u32[]{:S(2)}, u32[]{:S(2)}) collective-permute-start(bf16[40,1280]{1,0:T(8,128)(2,1)} %get-tuple-element.48), channel_id=1, source_target_pairs={{0,80},{1,81},{2,82},{3,83},{4,84},{5,85},{6,86},{7,87},{8,88},{9,... | collective-permute-start | bytes 307208 | tf_op jit(solution)/shard_map/ppermute | solution.py:57
  23.4 3.6 %collective-permute-start.6 = (bf16[40,1280]{1,0:T(8,128)(2,1)}, bf16[40,1280]{1,0:T(8,128)(2,1)S(1)}, u32[]{:S(2)}, u32[]{:S(2)}) collective-permute-start(bf16[40,1280]{1,0:T(8,128)(2,1)} %get-tuple-element.49), channel_id=1, source_target_pairs={{0,112},{1,113},{2,114},{3,115},{4,116},{5,117},{6,118},{7,119},{8... | collective-permute-start | bytes 307208 | tf_op jit(solution)/shard_map/ppermute | solution.py:57
  27.0 6.2 %collective-permute-done.4.p1 = bf16[40,1280]{1,0:T(8,128)(2,1)S(1)} collective-permute-done((bf16[40,1280]{1,0:T(8,128)(2,1)}, bf16[40,1280]{1,0:T(8,128)(2,1)S(1)}, u32[]{:S(2)}, u32[]{:S(2)}) %collective-permute-start.4) | collective-permute-done | bytes 102432 | tf_op jit(solution)/shard_map/ppermute | solution.py:57
  41.9 3.7 %collective-permute-done.8.refs_1_ = bf16[40,5120]{1,0:T(8,128)(2,1)} collective-permute-done((bf16[40,5120]{1,0:T(8,128)(2,1)}, bf16[40,5120]{1,0:T(8,128)(2,1)}, u32[]{:S(2)}, u32[]{:S(2)}) %collective-permute-start.8) | collective-permute-done | bytes 409632 | tf_op jit(solution)/shard_map/ppermute | solution.py:57
  45.6 6.1 %collective-permute-done.9.refs_2_ = bf16[40,5120]{1,0:T(8,128)(2,1)} collective-permute-done((bf16[40,5120]{1,0:T(8,128)(2,1)}, bf16[40,5120]{1,0:T(8,128)(2,1)}, u32[]{:S(2)}, u32[]{:S(2)}) %collective-permute-start.9) | collective-permute-done | bytes 409632 | tf_op jit(solution)/shard_map/ppermute | solution.py:57
  61.9 10.7 %collective-permute-done.14.refs_7_ = bf16[2560,256]{1,0:T(8,128)(2,1)} collective-permute-done((bf16[2560,256]{1,0:T(8,128)(2,1)}, bf16[2560,256]{1,0:T(8,128)(2,1)}, u32[]{:S(2)}, u32[]{:S(2)}) %collective-permute-start.14) | collective-permute-done | bytes 1310752 | tf_op jit(solution)/shard_map/ppermute | solution.py:57
  76.0 15.5 %collective-permute-start.16 = (bf16[1280,256]{1,0:T(8,128)(2,1)}, bf16[1280,256]{1,0:T(8,128)(2,1)S(1)}, u32[]{:S(2)}, u32[]{:S(2)}) collective-permute-start(bf16[1280,256]{1,0:T(8,128)(2,1)} %hold.2.refs_4_), channel_id=1, source_target_pairs={{0,128},{1,129},{2,130},{3,131},{4,132},{5,133},{6,134},{7,135},{8... | collective-permute-start | bytes 1966088 | tf_op jit(solution)/shard_map/ppermute | solution.py:57
  91.5 2.5 %hidden.5.refs_1_ = bf16[320,256]{1,0:T(8,128)(2,1)S(1)} custom-call(s32[4]{0:T(128)S(1)} %copy-done.5, bf16[160,5120]{1,0:T(8,128)(2,1)S(1)} %collective-permute-done.12.refs_0_.refs_1_, bf16[160,5120]{1,0:T(8,128)(2,1)S(1)} %collective-permute-done.13.refs_1_.refs_2_, bf16[5120,256]{1,0:T(8,128)(2,1)S(1)} %copy-done, bf16[5120,256]{1,0:T(8,128)(2,1)S(1)} %copy-done.1), custom_call_target="tpu_custom_call" | custom-call | flops 6000000000 | bytes 8519680 | tf_op jit(solution)/shard_map/hidden/pallas_call | solution.py:180
  94.0 4.3 %hidden.6.refs_2_ = bf16[480,256]{1,0:T(8,128)(2,1)S(1)} custom-call(s32[4]{0:T(128)S(1)} %copy-done.5, bf16[160,5120]{1,0:T(8,128)(2,1)S(1)} %stack.17.refs_0_, bf16[160,5120]{1,0:T(8,128)(2,1)S(1)} %collective-permute-done.12.refs_0_.refs_1_, bf16[160,5120]{1,0:T(8,128)(2,1)S(1)} %collective-permute-done.13.refs_1_.refs_2_, ...), custom_call_target="tpu_custom_call" | custom-call | flops 2516582400 | bytes 10158080 | tf_op jit(solution)/shard_map/hidden/pallas_call | solution.py:180
  98.3 5.7 %collective-permute-done.18.value_ref = bf16[128,5120]{1,0:T(8,128)(2,1)S(1)} collective-permute-done((bf16[128,5120]{1,0:T(8,128)(2,1)S(1)}, bf16[128,5120]{1,0:T(8,128)(2,1)S(1)}, u32[]{:S(2)}, u32[]{:S(2)}) %collective-permute-start.18) | collective-permute-done | bytes 1310752 | tf_op jit(solution)/shard_map/ppermute | solution.py:57
  104.0 3.5 %hidden.7 = (bf16[160,256]{1,0:T(8,128)(2,1)S(1)}, bf16[160,256]{1,0:T(8,128)(2,1)S(1)}) custom-call(s32[4]{0:T(128)S(1)} %copy-done.5, bf16[160,5120]{1,0:T(8,128)(2,1)S(1)} %collective-permute-done.19.refs_0_, bf16[5120,256]{1,0:T(8,128)(2,1)S(1)} %copy-done, bf16[5120,256]{1,0:T(8,128)(2,1)S(1)} %copy-done.1, ...), custom_call_target="tpu_custom_call" | custom-call | flops 1677721600 | bytes 12124160 | tf_op jit(solution)/shard_map/hidden/pallas_call | solution.py:180
  112.4 3.3 %down.3 = (bf16[160,2560]{1,0:T(8,128)(2,1)S(1)}, bf16[160,2560]{1,0:T(8,128)(2,1)S(1)}, bf16[160,2560]{1,0:T(8,128)(2,1)S(1)}, bf16[160,2560]{1,0:T(8,128)(2,1)...) custom-call(s32[4]{0:T(128)S(1)} %copy-done.5, bf16[160,256]{1,0:T(8,128)(2,1)S(1)} %hidden.4.refs_0_, ...), custom_call_target="tpu_custom_call" | custom-call | flops 2516582400 | bytes 10158080 | tf_op jit(solution)/shard_map/down/pallas_call | solution.py:212
  117.7 4.9 %collective-permute-done.22 = bf16[160,2560]{1,0:T(8,128)(2,1)S(1)} collective-permute-done((bf16[160,2560]{1,0:T(8,128)(2,1)S(1)}, bf16[160,2560]{1,0:T(8,128)(2,1)S(1)}, u32[]{:S(2)}, u32[]{:S(2)}) %collective-permute-start.22) | collective-permute-done | bytes 819232 | tf_op jit(solution)/shard_map/ppermute | solution.py:57
  123.2 3.3 %collective-permute-start.26 = (bf16[160,2560]{1,0:T(8,128)(2,1)S(1)}, bf16[160,2560]{1,0:T(8,128)(2,1)S(1)}, u32[]{:S(2)}, u32[]{:S(2)}) collective-permute-start(bf16[160,2560]{1,0:T(8,128)(2,1)S(1)} %add_convert_fusion), channel_id=1, source_target_pairs={{0,12},{1,13},{2,14},{3,15},{4,0},{5,1},{6,2},{7,3},{8,4},{9,5},{1... | collective-permute-start | bytes 2457608 | tf_op jit(solution)/shard_map/ppermute | solution.py:57
  126.5 5.0 %collective-permute-done.21.refs_1_ = bf16[160,2560]{1,0:T(8,128)(2,1)S(1)} collective-permute-done((bf16[160,2560]{1,0:T(8,128)(2,1)S(1)}, bf16[160,2560]{1,0:T(8,128)(2,1)S(1)}, u32[]{:S(2)}, u32[]{:S(2)}) %collective-permute-start.21) | collective-permute-done | bytes 819232 | tf_op jit(solution)/shard_map/ppermute | solution.py:57
  131.5 8.7 %collective-permute-done.23.refs_2_ = bf16[160,2560]{1,0:T(8,128)(2,1)S(1)} collective-permute-done((bf16[160,2560]{1,0:T(8,128)(2,1)S(1)}, bf16[160,2560]{1,0:T(8,128)(2,1)S(1)}, u32[]{:S(2)}, u32[]{:S(2)}) %collective-permute-start.23) | collective-permute-done | bytes 819232 | tf_op jit(solution)/shard_map/ppermute | solution.py:57
  141.8 2.4 %collective-permute-start.28 = (bf16[40,5120]{1,0:T(8,128)(2,1)S(1)}, bf16[40,5120]{1,0:T(8,128)(2,1)S(1)}, u32[]{:S(2)}, u32[]{:S(2)}) collective-permute-start(bf16[40,5120]{1,0:T(8,128)(2,1)S(1)} %get-tuple-element.77), channel_id=1, source_target_pairs={{0,1},{1,2},{2,3},{3,0},{4,5},{5,6},{6,7},{7,4},{8,9},{9,10},{10,1... | collective-permute-start | bytes 1228808 | tf_op jit(solution)/shard_map/ppermute | solution.py:57
  144.4 10.1 %collective-permute-done.27.b = bf16[40,5120]{1,0:T(8,128)(2,1)S(1)} collective-permute-done((bf16[40,5120]{1,0:T(8,128)(2,1)S(1)}, bf16[40,5120]{1,0:T(8,128)(2,1)S(1)}, u32[]{:S(2)}, u32[]{:S(2)}) %collective-permute-start.27) | collective-permute-done | bytes 409632 | tf_op jit(solution)/shard_map/ppermute | solution.py:57
  155.2 3.5 %collective-permute-start.30 = (bf16[40,1280]{1,0:T(8,128)(2,1)S(1)}, bf16[40,1280]{1,0:T(8,128)(2,1)S(1)}, u32[]{:S(2)}, u32[]{:S(2)}) collective-permute-start(bf16[40,1280]{1,0:T(8,128)(2,1)S(1)} %get-tuple-element.80), channel_id=1, source_target_pairs={{32,0},{33,1},{34,2},{35,3},{36,4},{37,5},{38,6},{39,7},{40,8},{41... | collective-permute-start | bytes 307208 | tf_op jit(solution)/shard_map/ppermute | solution.py:57
  161.8 5.7 %collective-permute-done.31.r2 = bf16[40,1280]{1,0:T(8,128)(2,1)S(1)} collective-permute-done((bf16[40,1280]{1,0:T(8,128)(2,1)S(1)}, bf16[40,1280]{1,0:T(8,128)(2,1)S(1)}, u32[]{:S(2)}, u32[]{:S(2)}) %collective-permute-start.31) | collective-permute-done | bytes 102432 | tf_op jit(solution)/shard_map/ppermute | solution.py:57
  169.5 2.6 %combine.1 = bf16[128,5120]{1,0:T(8,128)(2,1)} custom-call(s32[1,128]{1,0:T(1,128)S(1)} %copy-done.6, bf16[128,5120]{1,0:T(8,128)(2,1)S(1)} %copy-done.3, bf16[40,1280]{1,0:T(8,128)(2,1)S(1)} %get-tuple-element.79.r0, bf16[40,1280]{1,0:T(8,128)(2,1)S(1)} %collective-permute-done.30.r1, bf16[40,1280]{1,0:T(8,128)(2,1)S(1)} %collective-permute-done.31.r2, ...), custom_call_target="tpu_custom_call" | custom-call | flops 60000000 | bytes 3000000 | tf_op jit(solution)/shard_map/combine/pallas_call | solution.py:297
  (90 shorter events, 45.8 us)
Async XLA Ops:
  5.9 21.1 %collective-permute-start.7 = (bf16[1280,256]{1,0:T(8,128)(2,1)S(1)}, bf16[1280,256]{1,0:T(8,128)(2,1)S(1)}, u32[]{:S(2)}, u32[]{:S(2)}) collective-permute-start(bf16[1280,256]{1,0:T(8,128)(2,1)S(1)} %get-tuple-element.84), channel_id=1, source_target_pairs={{0,16},{1,17},{2,18},{3,19},{4,20},{5,21},{6,22},{7,23},{8,24},{9,... | collective-permute-start | bytes 1966088 | tf_op jit(solution)/shard_map/ppermute | solution.py:57
  17.4 15.8 %collective-permute-start.4 = (bf16[40,1280]{1,0:T(8,128)(2,1)}, bf16[40,1280]{1,0:T(8,128)(2,1)S(1)}, u32[]{:S(2)}, u32[]{:S(2)}) collective-permute-start(bf16[40,1280]{1,0:T(8,128)(2,1)} %get-tuple-element.47), channel_id=1, source_target_pairs={{0,32},{1,33},{2,34},{3,35},{4,36},{5,37},{6,38},{7,39},{8,40},{9,... | collective-permute-start | bytes 307208 | tf_op jit(solution)/shard_map/ppermute | solution.py:57
  20.7 12.5 %collective-permute-start.5 = (bf16[40,1280]{1,0:T(8,128)(2,1)}, bf16[40,1280]{1,0:T(8,128)(2,1)S(1)}, u32[]{:S(2)}, u32[]{:S(2)}) collective-permute-start(bf16[40,1280]{1,0:T(8,128)(2,1)} %get-tuple-element.48), channel_id=1, source_target_pairs={{0,80},{1,81},{2,82},{3,83},{4,84},{5,85},{6,86},{7,87},{8,88},{9,... | collective-permute-start | bytes 307208 | tf_op jit(solution)/shard_map/ppermute | solution.py:57
  23.4 11.6 %collective-permute-start.6 = (bf16[40,1280]{1,0:T(8,128)(2,1)}, bf16[40,1280]{1,0:T(8,128)(2,1)S(1)}, u32[]{:S(2)}, u32[]{:S(2)}) collective-permute-start(bf16[40,1280]{1,0:T(8,128)(2,1)} %get-tuple-element.49), channel_id=1, source_target_pairs={{0,112},{1,113},{2,114},{3,115},{4,116},{5,117},{6,118},{7,119},{8... | collective-permute-start | bytes 307208 | tf_op jit(solution)/shard_map/ppermute | solution.py:57
  27.0 31.5 %collective-permute-start.11 = (bf16[1280,256]{1,0:T(8,128)(2,1)}, bf16[1280,256]{1,0:T(8,128)(2,1)}, u32[]{:S(2)}, u32[]{:S(2)}) collective-permute-start(bf16[1280,256]{1,0:T(8,128)(2,1)} %get-tuple-element.54), channel_id=1, source_target_pairs={{0,16},{1,17},{2,18},{3,19},{4,20},{5,21},{6,22},{7,23},{8,24},{9,... | collective-permute-start | bytes 1966088 | tf_op jit(solution)/shard_map/ppermute | solution.py:57
  37.8 13.9 %collective-permute-start.9 = (bf16[40,5120]{1,0:T(8,128)(2,1)}, bf16[40,5120]{1,0:T(8,128)(2,1)}, u32[]{:S(2)}, u32[]{:S(2)}) collective-permute-start(bf16[40,5120]{1,0:T(8,128)(2,1)} %unpack.1.refs_0_), channel_id=1, source_target_pairs={{0,3},{1,0},{2,1},{3,2},{4,7},{5,4},{6,5},{7,6},{8,11},{9,8},{10,9... | collective-permute-start | bytes 1228808 | tf_op jit(solution)/shard_map/ppermute | solution.py:57
  39.4 12.3 %collective-permute-start.10 = (bf16[40,5120]{1,0:T(8,128)(2,1)}, bf16[40,5120]{1,0:T(8,128)(2,1)}, u32[]{:S(2)}, u32[]{:S(2)}) collective-permute-start(bf16[40,5120]{1,0:T(8,128)(2,1)} %unpack.1.refs_0_), channel_id=1, source_target_pairs={{0,2},{1,3},{2,0},{3,1},{4,6},{5,7},{6,4},{7,5},{8,10},{9,11},{10,... | collective-permute-start | bytes 1228808 | tf_op jit(solution)/shard_map/ppermute | solution.py:57
  41.9 30.7 %collective-permute-start.14 = (bf16[2560,256]{1,0:T(8,128)(2,1)}, bf16[2560,256]{1,0:T(8,128)(2,1)}, u32[]{:S(2)}, u32[]{:S(2)}) collective-permute-start(bf16[2560,256]{1,0:T(8,128)(2,1)} %constant_dynamic-slice_fusion.1), channel_id=1, source_target_pairs={{0,16},{1,17},{2,18},{3,19},{4,20},{5,21},{6,22},{7,23},{8,24},{9,... | collective-permute-start | bytes 3932168 | tf_op jit(solution)/shard_map/ppermute | solution.py:57
  53.2 22.4 %collective-permute-start.12 = (bf16[160,5120]{1,0:T(8,128)(2,1)S(1)}, bf16[160,5120]{1,0:T(8,128)(2,1)S(1)}, u32[]{:S(2)}, u32[]{:S(2)}) collective-permute-start(bf16[160,5120]{1,0:T(8,128)(2,1)S(1)} %stack.17.refs_0_), channel_id=1, source_target_pairs={{0,4},{1,5},{2,6},{3,7},{4,8},{5,9},{6,10},{7,11},{8,12},{9,13},{1... | collective-permute-start | bytes 4915208 | tf_op jit(solution)/shard_map/ppermute | solution.py:57
  54.9 21.1 %collective-permute-start.13 = (bf16[160,5120]{1,0:T(8,128)(2,1)S(1)}, bf16[160,5120]{1,0:T(8,128)(2,1)S(1)}, u32[]{:S(2)}, u32[]{:S(2)}) collective-permute-start(bf16[160,5120]{1,0:T(8,128)(2,1)S(1)} %stack.17.refs_0_), channel_id=1, source_target_pairs={{0,12},{1,13},{2,14},{3,15},{4,0},{5,1},{6,2},{7,3},{8,4},{9,5},{1... | collective-permute-start | bytes 4915208 | tf_op jit(solution)/shard_map/ppermute | solution.py:57
  56.6 47.4 %collective-permute-start.19 = (bf16[160,5120]{1,0:T(8,128)(2,1)S(1)}, bf16[160,5120]{1,0:T(8,128)(2,1)S(1)}, u32[]{:S(2)}, u32[]{:S(2)}) collective-permute-start(bf16[160,5120]{1,0:T(8,128)(2,1)S(1)} %stack.17.refs_0_), channel_id=1, source_target_pairs={{0,8},{1,9},{2,10},{3,11},{4,12},{5,13},{6,14},{7,15},{8,0},{9,1},... | collective-permute-start | bytes 4915208 | tf_op jit(solution)/shard_map/ppermute | solution.py:57
  72.6 21.4 %collective-permute-start.17 = (bf16[2560,256]{1,0:T(8,128)(2,1)}, bf16[2560,256]{1,0:T(8,128)(2,1)S(1)}, u32[]{:S(2)}, u32[]{:S(2)}) collective-permute-start(bf16[2560,256]{1,0:T(8,128)(2,1)} %collective-permute-done.14.refs_7_), channel_id=1, source_target_pairs={{0,128},{1,129},{2,130},{3,131},{4,132},{5,133},{6,134},{7,135},{8... | collective-permute-start | bytes 3932168 | tf_op jit(solution)/shard_map/ppermute | solution.py:57
  72.7 31.3 %collective-permute-start.18 = (bf16[128,5120]{1,0:T(8,128)(2,1)S(1)}, bf16[128,5120]{1,0:T(8,128)(2,1)S(1)}, u32[]{:S(2)}, u32[]{:S(2)}) collective-permute-start(bf16[128,5120]{1,0:T(8,128)(2,1)S(1)} %constant_dynamic-slice_fusion), channel_id=1, source_target_pairs={{0,16},{1,17},{2,18},{3,19},{4,20},{5,21},{6,22},{7,23},{8,24},{9,... | collective-permute-start | bytes 3932168 | tf_op jit(solution)/shard_map/ppermute | solution.py:57
  75.6 18.4 %collective-permute-start.15 = (bf16[1280,256]{1,0:T(8,128)(2,1)S(1)}, bf16[1280,256]{1,0:T(8,128)(2,1)S(1)}, u32[]{:S(2)}, u32[]{:S(2)}) collective-permute-start(bf16[1280,256]{1,0:T(8,128)(2,1)S(1)} %collective-permute-done.7.refs_3_), channel_id=1, source_target_pairs={{0,128},{1,129},{2,130},{3,131},{4,132},{5,133},{6,134},{7,135},{8... | collective-permute-start | bytes 1966088 | tf_op jit(solution)/shard_map/ppermute | solution.py:57
  76.0 18.0 %collective-permute-start.16 = (bf16[1280,256]{1,0:T(8,128)(2,1)}, bf16[1280,256]{1,0:T(8,128)(2,1)S(1)}, u32[]{:S(2)}, u32[]{:S(2)}) collective-permute-start(bf16[1280,256]{1,0:T(8,128)(2,1)} %hold.2.refs_4_), channel_id=1, source_target_pairs={{0,128},{1,129},{2,130},{3,131},{4,132},{5,133},{6,134},{7,135},{8... | collective-permute-start | bytes 1966088 | tf_op jit(solution)/shard_map/ppermute | solution.py:57
  109.1 13.6 %collective-permute-start.22 = (bf16[160,2560]{1,0:T(8,128)(2,1)S(1)}, bf16[160,2560]{1,0:T(8,128)(2,1)S(1)}, u32[]{:S(2)}, u32[]{:S(2)}) collective-permute-start(bf16[160,2560]{1,0:T(8,128)(2,1)S(1)} %get-tuple-element.66), channel_id=1, source_target_pairs={{0,4},{1,5},{2,6},{3,7},{4,8},{5,9},{6,10},{7,11},{8,12},{9,13},{1... | collective-permute-start | bytes 2457608 | tf_op jit(solution)/shard_map/ppermute | solution.py:57
  110.4 12.6 %collective-permute-start.25 = (bf16[160,2560]{1,0:T(8,128)(2,1)S(1)}, bf16[160,2560]{1,0:T(8,128)(2,1)S(1)}, u32[]{:S(2)}, u32[]{:S(2)}) collective-permute-start(bf16[160,2560]{1,0:T(8,128)(2,1)S(1)} %get-tuple-element.74), channel_id=1, source_target_pairs={{0,12},{1,13},{2,14},{3,15},{4,0},{5,1},{6,2},{7,3},{8,4},{9,5},{1... | collective-permute-start | bytes 2457608 | tf_op jit(solution)/shard_map/ppermute | solution.py:57
  115.6 15.9 %collective-permute-start.21 = (bf16[160,2560]{1,0:T(8,128)(2,1)S(1)}, bf16[160,2560]{1,0:T(8,128)(2,1)S(1)}, u32[]{:S(2)}, u32[]{:S(2)}) collective-permute-start(bf16[160,2560]{1,0:T(8,128)(2,1)S(1)} %get-tuple-element.69), channel_id=1, source_target_pairs={{0,12},{1,13},{2,14},{3,15},{4,0},{5,1},{6,2},{7,3},{8,4},{9,5},{1... | collective-permute-start | bytes 2457608 | tf_op jit(solution)/shard_map/ppermute | solution.py:57
  117.2 14.3 %collective-permute-start.24 = (bf16[160,2560]{1,0:T(8,128)(2,1)S(1)}, bf16[160,2560]{1,0:T(8,128)(2,1)S(1)}, u32[]{:S(2)}, u32[]{:S(2)}) collective-permute-start(bf16[160,2560]{1,0:T(8,128)(2,1)S(1)} %get-tuple-element.72), channel_id=1, source_target_pairs={{0,4},{1,5},{2,6},{3,7},{4,8},{5,9},{6,10},{7,11},{8,12},{9,13},{1... | collective-permute-start | bytes 2457608 | tf_op jit(solution)/shard_map/ppermute | solution.py:57
  122.9 17.4 %collective-permute-start.23 = (bf16[160,2560]{1,0:T(8,128)(2,1)S(1)}, bf16[160,2560]{1,0:T(8,128)(2,1)S(1)}, u32[]{:S(2)}, u32[]{:S(2)}) collective-permute-start(bf16[160,2560]{1,0:T(8,128)(2,1)S(1)} %add_convert_fusion.1), channel_id=1, source_target_pairs={{0,4},{1,5},{2,6},{3,7},{4,8},{5,9},{6,10},{7,11},{8,12},{9,13},{1... | collective-permute-start | bytes 2457608 | tf_op jit(solution)/shard_map/ppermute | solution.py:57
  123.2 17.1 %collective-permute-start.26 = (bf16[160,2560]{1,0:T(8,128)(2,1)S(1)}, bf16[160,2560]{1,0:T(8,128)(2,1)S(1)}, u32[]{:S(2)}, u32[]{:S(2)}) collective-permute-start(bf16[160,2560]{1,0:T(8,128)(2,1)S(1)} %add_convert_fusion), channel_id=1, source_target_pairs={{0,12},{1,13},{2,14},{3,15},{4,0},{5,1},{6,2},{7,3},{8,4},{9,5},{1... | collective-permute-start | bytes 2457608 | tf_op jit(solution)/shard_map/ppermute | solution.py:57
  140.9 13.6 %collective-permute-start.27 = (bf16[40,5120]{1,0:T(8,128)(2,1)S(1)}, bf16[40,5120]{1,0:T(8,128)(2,1)S(1)}, u32[]{:S(2)}, u32[]{:S(2)}) collective-permute-start(bf16[40,5120]{1,0:T(8,128)(2,1)S(1)} %get-tuple-element.76), channel_id=1, source_target_pairs={{0,3},{1,0},{2,1},{3,2},{4,7},{5,4},{6,5},{7,6},{8,11},{9,8},{10,9... | collective-permute-start | bytes 1228808 | tf_op jit(solution)/shard_map/ppermute | solution.py:57
  141.8 12.7 %collective-permute-start.28 = (bf16[40,5120]{1,0:T(8,128)(2,1)S(1)}, bf16[40,5120]{1,0:T(8,128)(2,1)S(1)}, u32[]{:S(2)}, u32[]{:S(2)}) collective-permute-start(bf16[40,5120]{1,0:T(8,128)(2,1)S(1)} %get-tuple-element.77), channel_id=1, source_target_pairs={{0,1},{1,2},{2,3},{3,0},{4,5},{5,6},{6,7},{7,4},{8,9},{9,10},{10,1... | collective-permute-start | bytes 1228808 | tf_op jit(solution)/shard_map/ppermute | solution.py:57
  144.2 10.3 %collective-permute-start.29 = (bf16[40,5120]{1,0:T(8,128)(2,1)S(1)}, bf16[40,5120]{1,0:T(8,128)(2,1)S(1)}, u32[]{:S(2)}, u32[]{:S(2)}) collective-permute-start(bf16[40,5120]{1,0:T(8,128)(2,1)S(1)} %get-tuple-element.78), channel_id=1, source_target_pairs={{0,2},{1,3},{2,0},{3,1},{4,6},{5,7},{6,4},{7,5},{8,10},{9,11},{10,... | collective-permute-start | bytes 1228808 | tf_op jit(solution)/shard_map/ppermute | solution.py:57
  (21 other events, 200.3 us)
